TPU v7x, 32 devices: a whole 2x2x4 slice. The times are simulated.
32 devices in a mesh: band: 4 (over y, x), slab: 8 (over z, core).
Axes of the slice: x: 2, y: 2, z: 4, core: 2. Of those that a mesh axis runs over, the one named last changes fastest.
Arguments:
- band_fields: float32 [16, 6, 6, 128, 1024], P(None, None, None, ('band', 'slab')), may hold values from -12 to 12
Outputs:
- pair_transfer: float32 [16, 16, 1024], P('band', None, 'slab')
All inputs are finite; a program needn't handle non-finite values.
Results may differ from a plain program's by a relative error of at most 0.0042.
Values may be sent and summed in bfloat16 or wider, within the bound.
No kernel may reach another device: no remote copies, remote signals or barrier semaphores. Data moves between devices by JAX's collectives and lax.ppermute only.
A program may use at most 256 MiB of HBM per device.

v0:
```python
import jax
import jax.numpy as jnp
from jax import lax
from jax.sharding import PartitionSpec as P

XW = 4
NY = 128


hall_length = 0.5


def padded(array, sides, width):
    for axis, dim in sides:
        peers, length = (lax.axis_size(axis), array.shape[dim])
        up = [(i, (i + 1) % peers) for i in range(peers)]
        down = [(j, i) for i, j in up]
        last = lax.slice_in_dim(array, length - width, length, axis=dim)
        first = lax.slice_in_dim(array, 0, width, axis=dim)
        before = lax.ppermute(last, axis, up)
        after = lax.ppermute(first, axis, down)
        array = jnp.concatenate([before, array, after], axis=dim)
    return array


def advect(vector, ddx, ddy, ddz, first):
    return (
        vector[0] * ddx[:, first : first + 3]
        + vector[1] * ddy[:, first : first + 3]
        + vector[2] * ddz[:, first : first + 3]
    )


def stack_fields(inner, ddx, ddy, ddz):
    currents = jnp.stack([ddy[:, 5] - ddz[:, 4], ddz[:, 3] - ddx[:, 5], ddx[:, 4] - ddy[:, 3]], 1)
    return jnp.concatenate([inner, currents], 1)


def make_drive(inner, ddx, ddy, ddz, full):
    velocity, magnetic, current = (full[0:3], full[3:6], full[6:9])
    part_a = -advect(velocity, ddx, ddy, ddz, 0) + advect(magnetic, ddx, ddy, ddz, 3)
    part_c = -advect(velocity, ddx, ddy, ddz, 3) + advect(magnetic, ddx, ddy, ddz, 0)
    bfield = inner[:, 3:6]
    cross = jnp.stack(
        [
            current[1] * bfield[:, 2] - current[2] * bfield[:, 1],
            current[2] * bfield[:, 0] - current[0] * bfield[:, 2],
            current[0] * bfield[:, 1] - current[1] * bfield[:, 0],
        ],
        1,
    )
    return jnp.concatenate([part_a, part_c, -hall_length * cross], 1).astype(jnp.bfloat16)


def body(band_fields):
    inner = band_fields[:, :, 1:-1]
    ddx = (band_fields[:, :, 2:] - band_fields[:, :, :-2]) * 0.5
    widened = padded(inner, ((("band", "slab"), 3),), 1)
    ddy = (widened[:, :, :, 2:] - widened[:, :, :, :-2]) * 0.5
    ddz = (jnp.roll(inner, -1, 4) - jnp.roll(inner, 1, 4)) * 0.5
    stacked = stack_fields(inner, ddx, ddy, ddz)
    full = jnp.sum(stacked, 0)
    drive = make_drive(inner, ddx, ddy, ddz, full)
    resp = stacked.astype(jnp.bfloat16)
    partial_value = jnp.einsum("qcxyz,kcxyz->qkz", resp, drive, preferred_element_type=jnp.float32)
    zpart = lax.psum_scatter(partial_value, "slab", scatter_dimension=2, tiled=True)
    sums = lax.psum_scatter(zpart, "band", scatter_dimension=0, tiled=True)
    return sums * (1.0 / (XW * NY))


def solution(mesh):
    return jax.shard_map(
        body,
        mesh=mesh,
        in_specs=(P(None, None, None, ("band", "slab"), None),),
        out_specs=P("band", None, "slab"),
        check_vma=False,
    )
```

profile of v0, /device:TPU:0, one launch (start us, length us, event | category | flops | bytes accessed | tf_op | source)
XLA Modules:
  0.0 495.9 jit_solution(9880047658088729911)
XLA Ops:
  6.5 8.3 %fusion.11 = (f32[16,6,4,1,1024]{4,3,2,1,0:T(1,128)S(1)}, f32[16,6,4,1,1024]{4,3,2,1,0:T(1,128)S(1)}) fusion(f32[16,6,6,4,1024]{4,3,2,1,0:T(4,128)} %param.1), kind=kLoop, calls=%fused_computation.37 | loop fusion | bytes 6291456 | tf_op jit(solution)/shard_map/slice | solution.py:19
  14.8 2.1 copy.75
  17.4 2.1 copy.74
  19.5 5.9 %collective-permute-start = (f32[16,6,4,1,1024]{4,0,3,2,1:T(8,128)}, f32[16,6,4,1,1024]{4,0,3,2,1:T(8,128)}, u32[]{:S(2)}, u32[]{:S(2)}) collective-permute-start(f32[16,6,4,1,1024]{4,0,3,2,1:T(8,128)} %copy.74), channel_id=1, source_target_pairs={{1,0},{2,1},{3,2},{4,3},{5,4},{6,5},{7,6},{8,7},{9,8},{10,9},{11,1... | collective-permute-start | bytes 4718600 | tf_op jit(solution)/shard_map/ppermute | solution.py:21
  26.0 11.4 %fusion.10 = (f32[16,6,4,4,1024]{4,3,2,1,0:T(4,128)}, f32[16,6,4,4,1024]{4,3,2,1,0:T(4,128)}, f32[16,6,4,4,1024]{4,3,2,1,0:T(4,128)}) fusion(f32[16,6,6,4,1024]{4,3,2,1,0:T(4,128)S(1)} %copy-done), kind=kLoop, calls=%fused_computation.36 | loop fusion | bytes 37748736 | tf_op jit(solution)/shard_map/slice | solution.py:57
  38.8 1.4 copy.77
  40.1 13.4 %fusion.9 = (f32[16,6,4,4,1023]{4,3,2,1,0:T(4,128)}, f32[16,6,4,4,1023]{4,3,2,1,0:T(4,128)}) fusion(f32[16,6,6,4,1024]{4,3,2,1,0:T(4,128)} %param.1), kind=kLoop, calls=%fused_computation.35 | loop fusion | bytes 25141248 | tf_op jit(solution)/shard_map/jit(_roll_static)/slice | solution.py:60
  53.5 11.0 %copy.79 = f32[16,6,4,4,1023]{4,0,3,2,1:T(8,128)} copy(f32[16,6,4,4,1023]{4,3,2,1,0:T(4,128)} %get-tuple-element.12) | data formatting | bytes 12570624
  64.6 8.3 %copy.76 = f32[16,6,4,4,1023]{4,0,3,2,1:T(8,128)} copy(f32[16,6,4,4,1023]{4,3,2,1,0:T(4,128)S(1)} %copy-done.2) | data formatting | bytes 12570624
  72.9 5.4 %copy.73 = f32[16,6,4,4,1024]{4,0,3,2,1:T(8,128)S(1)} copy(f32[16,6,4,4,1024]{4,3,2,1,0:T(4,128)S(1)} %bitcast.27) | data formatting | bytes 12582912
  78.3 2.6 fusion.7
  80.9 22.0 %fusion.2 = (f32[16,6,4,4,1024]{4,0,3,2,1:T(8,128)S(1)}, f32[16,6,4,4,1024]{4,0,3,2,1:T(8,128)}) fusion(f32[16,6,4,4,1]{4,0,3,2,1:T(8,128)} %copy.77, f32[16,6,4,4,1023]{4,0,3,2,1:T(8,128)} %copy.76, f32[16,6,4,4,1023]{4,0,3,2,1:T(8,128)} %copy.79, f32[16,6,4,4,1]{4,0,3,2,1:T(8,128)} %copy.78, f32[16,6,4,4,1024]{4,3,2,1,0:T(4,128)} %get-tuple-element.15, ...), kind=kLoop, calls=%fused_computation.6 | loop fusion | flops 9437184 | bytes 37748736 | tf_op jit(solution)/shard_map/mul | solution.py:60
  102.9 3.4 fusion.1
  107.4 2.2 fusion.5
  109.6 2.9 fusion.4
  112.6 2.7 multiply_subtract_fusion.2
  115.7 2.9 add_convert_fusion.1
  118.5 2.4 pad_maximum_fusion.3
  120.9 102.8 %copy.68 = bf16[16,9,4,4,1024]{1,0,3,2,4:T(8,128)(2,1)} copy(bf16[16,9,4,4,1024]{4,0,3,2,1:T(8,128)(2,1)} %pad_maximum_fusion.3) | data formatting | bytes 9437184 | tf_op jit(solution)/shard_map/concatenate | solution.py:52
  223.7 102.8 %copy.69 = bf16[16,9,4,4,1024]{1,0,3,2,4:T(8,128)(2,1)} copy(bf16[16,9,4,4,1024]{4,0,3,2,1:T(8,128)(2,1)} %fusion.4) | data formatting | bytes 9437184 | tf_op jit(solution)/shard_map/convert_element_type | solution.py:64
  326.5 47.8 %convolution_bitcast_fusion = f32[16,16,1024]{0,1,2:T(8,128)} fusion(bf16[16,9,4,4,1024]{1,0,3,2,4:T(8,128)(2,1)} %copy.68, bf16[16,9,4,4,1024]{1,0,3,2,4:T(8,128)(2,1)} %copy.69), kind=kOutput, calls=%fused_computation.12 | convolution fusion | flops 75497472 | bytes 10485760 | tf_op jit(solution)/shard_map/qcxyz,kcxyz->qkz/dot_general | solution.py:65
  374.5 87.9 %reduce-scatter.3.cloned.1.call-done = f32[16,16,128]{0,1,2:T(8,128)} async-done(((f32[16,16,1024]{0,1,2:T(8,128)}), f32[16,16,128]{0,1,2:T(8,128)}) %reduce-scatter.3.cloned.1.call-update) | async-done | bytes 131088 | tf_op jit(solution)/shard_map/reduce_scatter | solution.py:66
  462.4 2.3 copy.70
  464.7 22.6 %reduce-scatter.5.cloned.1.call-done = f32[4,16,128]{2,1,0:T(8,128)} async-done(((f32[16,16,128]{2,1,0:T(8,128)}), f32[4,16,128]{2,1,0:T(8,128)}) %reduce-scatter.5.cloned.1.call-update) | async-done | bytes 32784 | tf_op jit(solution)/shard_map/reduce_scatter | solution.py:67
  (24 shorter events, 5.4 us)
Async XLA Ops:
  6.5 455.8 %reduce-scatter.3.cloned.1.call-start = ((), (), s32[]{:S(2)}) async-start(), calls=%async_computation.2 | async-start | bytes 9437184 | tf_op jit(solution)/shard_map/reduce_scatter | solution.py:66
  6.5 18.9 %copy-start = (f32[16,6,6,4,1024]{4,3,2,1,0:T(4,128)S(1)}, f32[16,6,6,4,1024]{4,3,2,1,0:T(4,128)}, u32[]{:S(2)}) copy-start(f32[16,6,6,4,1024]{4,3,2,1,0:T(4,128)} %param.1) | copy-start | bytes 28311556
  16.9 86.0 %collective-permute-start.1 = (f32[16,6,4,1,1024]{4,0,3,2,1:T(8,128)}, f32[16,6,4,1,1024]{4,0,3,2,1:T(8,128)}, u32[]{:S(2)}, u32[]{:S(2)}) collective-permute-start(f32[16,6,4,1,1024]{4,0,3,2,1:T(8,128)} %copy.75), channel_id=1, source_target_pairs={{0,1},{1,2},{2,3},{3,4},{4,5},{5,6},{6,7},{7,8},{8,9},{9,10},{10,1... | collective-permute-start | bytes 4718600 | tf_op jit(solution)/shard_map/ppermute | solution.py:20
  19.5 83.4 %collective-permute-start = (f32[16,6,4,1,1024]{4,0,3,2,1:T(8,128)}, f32[16,6,4,1,1024]{4,0,3,2,1:T(8,128)}, u32[]{:S(2)}, u32[]{:S(2)}) collective-permute-start(f32[16,6,4,1,1024]{4,0,3,2,1:T(8,128)} %copy.74), channel_id=1, source_target_pairs={{1,0},{2,1},{3,2},{4,3},{5,4},{6,5},{7,6},{8,7},{9,8},{10,9},{11,1... | collective-permute-start | bytes 4718600 | tf_op jit(solution)/shard_map/ppermute | solution.py:21
  53.5 11.1 %copy-start.2 = (f32[16,6,4,4,1023]{4,3,2,1,0:T(4,128)S(1)}, f32[16,6,4,4,1023]{4,3,2,1,0:T(4,128)}, u32[]{:S(2)}) copy-start(f32[16,6,4,4,1023]{4,3,2,1,0:T(4,128)} %get-tuple-element.13) | copy-start | bytes 18855940
  53.5 19.4 %slice-start = ((s8[6291456]{0:T(1024)(128)(4,1)}), s8[4194304]{0:T(1024)(128)(4,1)S(1)}, s32[]{:S(2)}) async-start(s8[6291456]{0:T(1024)(128)(4,1)} %bitcast.26), calls=%async_computation.4 | async-start | bytes 8388608
  64.6 8.3 %slice-start.1 = ((s8[6291456]{0:T(1024)(128)(4,1)}), s8[2097152]{0:T(1024)(128)(4,1)S(1)}, s32[]{:S(2)}) async-start(s8[6291456]{0:T(1024)(128)(4,1)} %bitcast.26), calls=%async_computation.5 | async-start | bytes 4194304
  102.9 3.7 copy-start.1
  374.4 112.9 %reduce-scatter.5.cloned.1.call-start = ((), (), s32[]{:S(2)}) async-start(), calls=%async_computation.3 | async-start | bytes 163840 | tf_op jit(solution)/shard_map/reduce_scatter | solution.py:67
Sparse Core Ops, SparseCore 0:
  374.5 87.7 reduce-scatter.2
  465.1 22.1 reduce-scatter.4
where the time goes:
time: 502 us; the launch traced here: 496 us
  local copies, waits for them, and re-layouts  276 us (55%)
  waiting for transfers between devices  111 us (22%)
  matrix products  47.8 us (10%)
  other arithmetic  41 us (8%)
  between operations  14 us (3%)
  starting transfers between devices  6.42 us (1%)
    convert_element_type x1, local copies, waits for them, and re-layouts, body(): resp = stacked.astype(jnp.bfloat16)  103 us
    concatenate x1, local copies, waits for them, and re-layouts, make_drive(): jnp.concatenate([part_a, part_c, -hall_length * cross], 1)  103 us
    reduce_scatter x1, waiting for transfers between devices, body(): lax.psum_scatter(partial_value, 'slab', scatter_dimension=2, tiled=True)  87.9 us
    dot_general x1, matrix products, body(): jnp.einsum('qcxyz,kcxyz->qkz', resp, drive, preferred_element_type=jnp.fl...  47.8 us
    unnamed x17, local copies, waits for them, and re-layouts  31.9 us
    reduce_scatter x1, waiting for transfers between devices, body(): sums = lax.psum_scatter(zpart, 'band', scatter_dimension=0, tiled=True)  22.6 us
    mul x1, other arithmetic, body(): ddz = (jnp.roll(inner, -1, 4) - jnp.roll(inner, 1, 4)) * 0.5  22 us
    slice x2, local copies, waits for them, and re-layouts, body(): ddz = (jnp.roll(inner, -1, 4) - jnp.roll(inner, 1, 4)) * 0.5  14 us
  transfers between devices with their start and end apart: 4, of which 2 were waited for; matrix products, arithmetic and copies ran while one was open for 16% of the time, Pallas kernels for 0%

commit v1 on v0

v1 whole, which is shorter than its diff:
```python
import jax
import jax.numpy as jnp
from jax import lax
from jax.experimental import pallas as pl
from jax.experimental.pallas import tpu as pltpu
from jax.sharding import PartitionSpec as P

AXES = ("band", "slab")
LANES = 128
GROUP = 16
F32 = jnp.float32
BF16 = jnp.bfloat16
VMEM = pl.BlockSpec(memory_space=pltpu.VMEM)
SMEM = pl.BlockSpec(memory_space=pltpu.SMEM)
ANY = pl.BlockSpec(memory_space=pl.ANY)
PARAMS = pltpu.CompilerParams(vmem_limit_bytes=56 * 2**20)


class Sizes:
    def __init__(self, shape):
        self.bands, self.comps, self.planes, self.rows, cells = shape
        self.inner = self.planes - 2
        self.tiles = cells // LANES
        self.chunks = 4 if self.bands % 4 == 0 else 1
        self.per_chunk = self.bands // self.chunks


def row(ref, s, q, c, x, y):
    if s.rows == 1:
        return ref[q, c, x]
    return ref[q, c, x, pl.ds(y, s.tiles, stride=s.rows), :]


def z_difference(value):
    tiles = value.shape[0]
    lane = lax.broadcasted_iota(jnp.int32, value.shape, 1)
    left = pltpu.roll(value, LANES - 1, 1)
    right = pltpu.roll(value, 1, 1)
    after = jnp.where(lane == LANES - 1, pltpu.roll(left, tiles - 1, 0), left)
    before = jnp.where(lane == 0, pltpu.roll(right, 1, 0), right)
    return after - before


def start_copies(s, x_hbm, buf, sems):
    copies = []
    for i in range(s.chunks):
        part = pl.ds(i * s.per_chunk, s.per_chunk)
        copy = pltpu.make_async_copy(x_hbm.at[part], buf.at[part], sems.at[i])
        copy.start()
        copies.append(copy)
    return copies


def edge_kernel(s, x_hbm, up_ref, down_ref, buf, sems):
    copies = start_copies(s, x_hbm, buf, sems)
    last = s.rows - 1
    n = s.inner
    zero = jnp.zeros((s.tiles, LANES), F32)

    def band(q, sums):
        at_last, below, first = sums
        for c in range(s.comps):
            for p in range(n // 2):
                pair = [row(buf, s, q, c, 1 + 2 * p + k, last) for k in range(2)]
                up_ref[(q * s.comps + c) * (n // 2) + p] = jnp.concatenate(pair, 0).astype(BF16)
        at_last = [a + row(buf, s, q, 3 + i // s.planes, i % s.planes, last) for i, a in enumerate(at_last)]
        first = [a + row(buf, s, q, 3 + 2 * (i // n), 1 + i % n, 0) for i, a in enumerate(first)]
        if s.rows > 1:
            below = [a + row(buf, s, q, 3 + 2 * (i // n), 1 + i % n, last - 1) for i, a in enumerate(below)]
        return at_last, below, first

    sums = ([zero] * (3 * s.planes), [zero] * (2 * n), [zero] * (2 * n))
    for i, copy in enumerate(copies):
        copy.wait()
        sums = lax.fori_loop(i * s.per_chunk, (i + 1) * s.per_chunk, band, sums)
    at_last, below, first = sums
    for i, value in enumerate(first):
        down_ref[i] = value
    current = [[], [], []]
    for x in range(n):
        bx, by, bz = ([at_last[c * s.planes + x + k] for k in range(3)] for c in range(3))
        current[0].append((-below[n + x] - z_difference(by[1])) * 0.5)
        current[1].append((z_difference(bx[1]) - (bz[2] - bz[0])) * 0.5)
        current[2].append(((by[2] - by[0]) + below[x]) * 0.5)
    base = s.bands * s.comps * (n // 2)
    for c in range(3):
        for p in range(n // 2):
            up_ref[base + c * (n // 2) + p] = jnp.concatenate(current[c][2 * p : 2 * p + 2], 0).astype(BF16)


def transposed_store(s, source, target, slot, zt):
    depth = source.shape[0] // s.tiles
    block = source[pl.ds(zt, depth, stride=s.tiles), :].astype(BF16).T
    target[zt, :, slot] = block.reshape(LANES // GROUP, GROUP, depth)


def diagonal_products(s, rt, dt, zt, g):
    wide = s.bands * GROUP
    left = rt[zt, g].reshape(wide, rt.shape[-1])
    right = dt[zt, g].reshape(wide, dt.shape[-1])
    full = lax.dot_general(left, right, (((1,), (1,)), ((), ())), preferred_element_type=F32)
    full = full.reshape(s.bands, GROUP, wide)
    cell = lax.broadcasted_iota(jnp.int32, full.shape, 1)
    lane = lax.broadcasted_iota(jnp.int32, full.shape, 2)
    return jnp.sum(jnp.where(cell == lane % GROUP, full, 0.0), 1)


def zero_tail(s, ref, used):
    tail = ref.shape[0] - used * s.tiles
    if tail:
        ref[pl.ds(used * s.tiles, tail), :] = jnp.zeros((tail, LANES), F32)


def slot_of(s, place, q, n_band):
    share = s.bands // n_band
    return (q // share ^ place[0]) * share + q % share


def cross(a, b):
    return [a[1] * b[2] - a[2] * b[1], a[2] * b[0] - a[0] * b[2], a[0] * b[1] - a[1] * b[0]]


def local_depth(s):
    return (s.rows - 1) * s.inner * 6 + max(s.rows - 2, 0) * s.inner * 3


def local_kernel(s, n_band, place, x_hbm, g_ref, drive_ref, field_ref, last_ref, coef_ref, buf, sums, coefs, sr, sd, rt, dt, sems):
    copies = start_copies(s, x_hbm, buf, sems)
    n = s.inner
    for i, copy in enumerate(copies):
        copy.wait()

        def add(j, carry):
            c, x = (j // s.planes, j % s.planes)
            for y in range(s.rows):
                total = row(buf, s, i * s.per_chunk, c, x, y)
                for q in range(1, s.per_chunk):
                    total = total + row(buf, s, i * s.per_chunk + q, c, x, y)
                if i:
                    total = total + sums[c, x, y]
                sums[c, x, y] = total
            return carry

        lax.fori_loop(0, s.comps * s.planes, add, 0)
    for x in range(n):
        for y in range(s.rows):
            v = [sums[c, x + 1, y] for c in range(3)]
            b = [sums[c, x + 1, y] for c in range(3, 6)]

            def dy(c):
                high = sums[c, x + 1, y + 1] if y + 1 < s.rows else 0.0
                low = sums[c, x + 1, y - 1] if y else 0.0
                return high - low

            def dx(c):
                return sums[c, x + 2, y] - sums[c, x, y]

            j = [dy(5) - z_difference(b[1]), z_difference(b[0]) - dx(5), dx(4) - dy(3)]
            j = [value * 0.5 for value in j]
            for d in range(3):
                coefs[x, y, d] = (v[d] - b[d]) * -0.25
                coefs[x, y, 3 + d] = (v[d] + b[d]) * -0.25
                coefs[x, y, 6 + d] = j[d]
            if y == 0:
                coef_ref[x, 0] = coefs[x, 0, 1]
                coef_ref[x, 1] = coefs[x, 0, 4]
                for d in range(3):
                    coef_ref[x, 2 + d] = j[d]
                coef_ref[x, 5] = b[0]
                coef_ref[x, 6] = b[2]
            if y == s.rows - 1:
                for d in range(3):
                    coef_ref[x, 7 + d] = j[d]
    used = local_depth(s)
    zero_tail(s, sr, used)
    zero_tail(s, sd, used)

    def band(q, carry):
        entry = 0
        for x in range(n):
            for y in range(s.rows):
                f = [row(buf, s, q, c, x + 1, y) for c in range(6)]
                deltas = [[], [], []]
                for c in range(6):
                    deltas[0].append(row(buf, s, q, c, x + 2, y) - row(buf, s, q, c, x, y))
                    high = row(buf, s, q, c, x + 1, y + 1) if y + 1 < s.rows else None
                    low = row(buf, s, q, c, x + 1, y - 1) if y else None
                    if high is None:
                        delta = jnp.zeros_like(f[0]) if low is None else -low
                    else:
                        delta = high if low is None else high - low
                    deltas[1].append(delta)
                    deltas[2].append(z_difference(f[c]))
                da, dc = ([], [])
                for c in range(3):
                    plus = minus = None
                    for d in range(3):
                        p = coefs[x, y, d] * (deltas[d][c] + deltas[d][c + 3])
                        m = coefs[x, y, 3 + d] * (deltas[d][c] - deltas[d][c + 3])
                        plus = p if plus is None else plus + p
                        minus = m if minus is None else minus + m
                    da.append(plus + minus)
                    dc.append(plus - minus)
                dx, dy, dz = deltas
                j = [(dy[5] - dz[4]) * 0.5, (dz[3] - dx[5]) * 0.5, (dx[4] - dy[3]) * 0.5]
                drives = da + dc
                if y == 0:
                    for c in range(6):
                        drive_ref[q, x, c] = drives[c]
                        field_ref[q, x, c] = f[c]
                    for c in range(3):
                        drive_ref[q, x, 6 + c] = j[c]
                if y == s.rows - 1 and s.rows > 1:
                    for c in range(3):
                        last_ref[q, x, c] = j[c]
                        last_ref[q, x, 3 + c] = f[3 + c]
                left, right = ([], [])
                if y:
                    left, right = (list(f), list(drives))
                if 0 < y < s.rows - 1:
                    turn = cross([coefs[x, y, 6 + d] * -0.5 for d in range(3)], f[3:6])
                    left, right = (left + j, right + turn)
                for a, b in zip(left, right):
                    sr[pl.ds(entry * s.tiles, s.tiles), :] = a
                    sd[pl.ds(entry * s.tiles, s.tiles), :] = b
                    entry += 1
        if used:
            slot = slot_of(s, place, q, n_band)
            for zt in range(s.tiles):
                transposed_store(s, sr, rt, slot, zt)
                transposed_store(s, sd, dt, q, zt)
        return carry

    lax.fori_loop(0, s.bands, band, 0)

    def tile(zt, carry):
        for g in range(LANES // GROUP):
            g_ref[zt, g] = diagonal_products(s, rt, dt, zt, g)
        return carry

    if used:
        lax.fori_loop(0, s.tiles, tile, 0)
    else:
        g_ref[...] = jnp.zeros_like(g_ref)


def halo_row(s, up_ref, index, x):
    pair = up_ref[index * (s.inner // 2) + x // 2].astype(F32)
    return pair[(x % 2) * s.tiles : (x % 2 + 1) * s.tiles]


def boundary_kernel(s, n_band, scale, place, g_ref, drive_ref, field_ref, last_ref, coef_ref, up_ref, down_ref, keep_ref, send_ref, tots, consts, sr, sd, rt, dt):
    n = s.inner
    zero = jnp.zeros((s.tiles, LANES), F32)
    kinds = (1, 4, 3, 5)

    def add(q, totals):
        return [t + halo_row(s, up_ref, q * s.comps + kinds[i // n], i % n) for i, t in enumerate(totals)]

    totals = lax.fori_loop(0, s.bands, add, [zero] * (4 * n))
    for x in range(n):
        vy, my, bx, bz = (totals[k * n + x] for k in range(4))
        ahead_x, ahead_z = (down_ref[x], down_ref[n + x])
        tots[x, 0] = coef_ref[x, 0]
        tots[x, 1] = coef_ref[x, 1]
        tots[x, 2] = (vy - my) * -0.25
        tots[x, 3] = (vy + my) * -0.25
        j = [coef_ref[x, 2] - bz * 0.5, coef_ref[x, 3], coef_ref[x, 4] + bx * 0.5]
        if s.rows == 1:
            j = [j[0] + ahead_z * 0.5, j[1], j[2] - ahead_x * 0.5]
        behind = [halo_row(s, up_ref, s.bands * s.comps + c, x) for c in range(3)]
        behind = [behind[0] + coef_ref[x, 6] * 0.5, behind[1], behind[2] - coef_ref[x, 5] * 0.5]
        at_last = [coef_ref[x, 7] + ahead_z * 0.5, coef_ref[x, 8], coef_ref[x, 9] - ahead_x * 0.5]
        for c in range(3):
            tots[x, 4 + c] = j[c] * -0.5
            tots[x, 7 + c] = behind[c] * -0.5
            tots[x, 10 + c] = at_last[c] * -0.5
    used = n * (15 + (3 if s.rows > 1 else 0))
    zero_tail(s, sr, used)
    zero_tail(s, sd, used)

    def band(q, carry):
        entry = 0
        for x in range(n):
            f = [field_ref[q, x, c] for c in range(6)]
            h = [halo_row(s, up_ref, q * s.comps + c, x) for c in range(6)]
            left, right = ([], [])
            local, other = ([], [])
            for c in range(3):
                p = tots[x, 0] * (h[c] + h[c + 3])
                m = tots[x, 1] * (h[c] - h[c + 3])
                local.append((p, m))
                p = tots[x, 2] * (f[c] + f[c + 3])
                m = tots[x, 3] * (f[c] - f[c + 3])
                other.append((p, m))
            da = [drive_ref[q, x, c] - (p + m) for c, (p, m) in enumerate(local)]
            dc = [drive_ref[q, x, 3 + c] - (p - m) for c, (p, m) in enumerate(local)]
            behind = cross([tots[x, 7 + c] for c in range(3)], h[3:6])
            dc[0] = dc[0] - behind[2] * 0.5
            dc[2] = dc[2] + behind[0] * 0.5
            j = [drive_ref[q, x, 6] - h[5] * 0.5, drive_ref[q, x, 7], drive_ref[q, x, 8] + h[3] * 0.5]
            left += f + j
            right += da + dc + cross([tots[x, 4 + c] for c in range(3)], f[3:6])
            left += h
            right += [p + m for p, m in other] + [p - m for p, m in other]
            if s.rows > 1:
                left += [last_ref[q, x, c] for c in range(3)]
                right += cross([tots[x, 10 + c] for c in range(3)], [last_ref[q, x, 3 + c] for c in range(3)])
            for a, b in zip(left, right):
                sr[pl.ds(entry * s.tiles, s.tiles), :] = a
                sd[pl.ds(entry * s.tiles, s.tiles), :] = b
                entry += 1
        slot = slot_of(s, place, q, n_band)
        for zt in range(s.tiles):
            transposed_store(s, sr, rt, slot, zt)
            transposed_store(s, sd, dt, q, zt)
        return carry

    lax.fori_loop(0, s.bands, band, 0)
    share = s.bands // n_band

    def tile(r, carry):
        for core in range(2):
            zt = (r * 2 + core) ^ place[1]
            parts = [(diagonal_products(s, rt, dt, zt, g) + g_ref[zt, g]) * scale for g in range(LANES // GROUP)]
            for b in range(n_band):
                block = jnp.concatenate([p[b * share : (b + 1) * share] for p in parts], 0)
                if core == 0:
                    keep_ref[r, b] = block
                else:
                    send_ref[r, b] = block.astype(BF16)
        return carry

    lax.fori_loop(0, s.tiles // 2, tile, 0)


def exchange(value, distance, size):
    return lax.ppermute(value, AXES, [(i, i ^ distance) for i in range(size)])


def body(band_fields):
    s = Sizes(band_fields.shape)
    n_band, n_slab = (lax.axis_size("band"), lax.axis_size("slab"))
    devices = n_band * n_slab
    n, tiles, rows = (s.inner, s.tiles, s.rows)
    x = band_fields.reshape(s.bands, s.comps, s.planes, rows, tiles, LANES)
    x = x.transpose(0, 1, 2, 4, 3, 5).reshape(s.bands, s.comps, s.planes, tiles * rows, LANES)
    place = jnp.stack([lax.axis_index("band"), lax.axis_index("slab")]).astype(jnp.int32)

    def vector(*lead):
        return jax.ShapeDtypeStruct(lead + (tiles, LANES), F32)

    buffer = pltpu.VMEM(x.shape, F32)
    sems = pltpu.SemaphoreType.DMA((s.chunks,))
    depth = -(-(max(local_depth(s), 1)) // LANES) * LANES
    groups = LANES // GROUP
    wide = s.bands * GROUP
    rows_up = (s.bands * s.comps + 3) * (n // 2)

    up, down = pl.pallas_call(
        lambda *refs: edge_kernel(s, *refs),
        out_shape=(jax.ShapeDtypeStruct((rows_up, 2 * tiles, LANES), BF16), vector(2 * n)),
        in_specs=[ANY],
        out_specs=(VMEM, VMEM),
        scratch_shapes=[buffer, sems],
        compiler_params=PARAMS,
    )(x)
    step = [(i, (i + 1) % devices) for i in range(devices)]
    from_below = lax.ppermute(up, AXES, step)
    from_above = lax.ppermute(down, AXES, [(j, i) for i, j in step])

    def operands(used):
        return [
            pltpu.VMEM((used * tiles, LANES), F32),
            pltpu.VMEM((used * tiles, LANES), F32),
            pltpu.VMEM((tiles, groups, s.bands, GROUP, used), BF16),
            pltpu.VMEM((tiles, groups, s.bands, GROUP, used), BF16),
        ]

    local = pl.pallas_call(
        lambda *refs: local_kernel(s, n_band, *refs),
        out_shape=(
            jax.ShapeDtypeStruct((tiles, groups, s.bands, wide), F32),
            vector(s.bands, n, 9),
            vector(s.bands, n, 6),
            vector(s.bands, n, 6),
            vector(n, 10),
        ),
        in_specs=[SMEM, ANY],
        out_specs=(VMEM,) * 5,
        scratch_shapes=[buffer, pltpu.VMEM((s.comps, s.planes, rows, tiles, LANES), F32), pltpu.VMEM((n, rows, 9, tiles, LANES), F32)]
        + operands(depth)
        + [sems],
        compiler_params=PARAMS,
        cost_estimate=pl.CostEstimate(flops=2 * 10**9, bytes_accessed=2 * 10**7, transcendentals=0),
    )(place, x)
    if rows == 1:
        two = lax.ppermute(down, AXES, [(i, (i + 2) % devices) for i in range(devices)])
        two = two.reshape(2, n // 2, 2 * tiles, LANES) * 0.5
        base = s.bands * s.comps * (n // 2)
        behind = from_below[base:].astype(F32).reshape(3, n // 2, 2 * tiles, LANES)
        behind = jnp.stack([behind[0] - two[1], behind[1], behind[2] + two[0]])
        behind = behind.reshape(3 * (n // 2), 2 * tiles, LANES).astype(BF16)
        from_below = jnp.concatenate([from_below[:base], behind], 0)

    share = s.bands // n_band
    shape = (tiles // 2, n_band, groups * share, wide)
    scale = 1.0 / (n * rows * devices)
    keep, send = pl.pallas_call(
        lambda *refs: boundary_kernel(s, n_band, scale, *refs),
        out_shape=(jax.ShapeDtypeStruct(shape, F32), jax.ShapeDtypeStruct(shape, BF16)),
        in_specs=[SMEM] + [VMEM] * 7,
        out_specs=(VMEM, VMEM),
        scratch_shapes=[pltpu.VMEM((n, 13, tiles, LANES), F32), pltpu.SMEM((1,), jnp.int32)] + operands(LANES),
        compiler_params=PARAMS,
    )(place, *local, from_below, from_above)

    value = keep + exchange(send, 1, devices).astype(F32)
    parts = [exchange(value[:, d].astype(BF16), d * n_slab, devices) for d in range(1, n_band)]
    value = sum([p.astype(F32) for p in parts], value[:, 0])
    parts = [exchange(value[e].astype(BF16), 2 * e, devices) for e in range(1, tiles // 2)]
    value = sum([p.astype(F32) for p in parts], value[0])
    value = value.reshape(groups, share, s.bands, GROUP).transpose(1, 2, 0, 3)
    return value.reshape(share, s.bands, groups * GROUP)


def solution(mesh):
    return jax.shard_map(
        body,
        mesh=mesh,
        in_specs=(P(None, None, None, AXES, None),),
        out_specs=P("band", None, "slab"),
        check_vma=False,
    )
```

time: 502 us -> 62.9 us (0.13); the launches traced: 496 us -> 62.7 us
  local copies, waits for them, and re-layouts: 276 us -> 1.93 us
  waiting for transfers between devices: 111 us -> 8.27 us
  matrix products: 47.8 us -> 0 us
  other arithmetic: 41 us -> 1.82 us
  Pallas kernels: 0 us -> 37 us
  between operations: 14 us -> 0.11 us
  starting transfers between devices: 6.42 us -> 13.6 us
    reduce_scatter x2 -> x0, waiting for transfers between devices: 111 us -> none  [the longest x1 87.9 us: body(): lax.psum_scatter(partial_value, 'slab', scatter_dimension=2, tiled=True)]
    concatenate x1 -> x0, local copies, waits for them, and re-layouts: 103 us -> none  [make_drive(): jnp.concatenate([part_a, part_c, -hall_length * cross], 1)]
    convert_element_type x1 -> x2, local copies, waits for them, and re-layouts: 103 us -> 0.02 us  [the longest x1 0.02 us: body(): value[:, d].astype(BF16)]
    dot_general x1 -> x0, matrix products: 47.8 us -> none  [body(): jnp.einsum('qcxyz,kcxyz->qkz', resp, drive, preferred_element_type=jnp.fl...]
    pallas_call x0 -> x3, Pallas kernels: none -> 37 us  [the longest x1 19.8 us: body(): pl.pallas_call(lambda *refs: local_kernel(s, n_band, *refs), out_shape=(j...]
    slice x5 -> x0, local copies, waits for them, and re-layouts: 36.2 us -> none  [the longest x2 14 us: body(): ddz = (jnp.roll(inner, -1, 4) - jnp.roll(inner, 1, 4)) * 0.5]
    unnamed x17 -> x4, local copies, waits for them, and re-layouts: 31.9 us -> 0.89 us
    mul x3 -> x0, other arithmetic: 26.8 us -> none  [the longest x1 22 us: body(): ddz = (jnp.roll(inner, -1, 4) - jnp.roll(inner, 1, 4)) * 0.5]
  transfers between devices with their start and end apart: 4 -> 9, of which waited for: 2 -> 6; matrix products, arithmetic and copies ran while one was open for 16% -> 1% of each run, Pallas kernels for 0% -> 32%
where the time goes in v1:
time: 62.9 us; the launch traced here: 62.7 us
  Pallas kernels  37 us (59%)
  starting transfers between devices  13.6 us (22%)
  waiting for transfers between devices  8.27 us (13%)
  local copies, waits for them, and re-layouts  1.93 us (3%)
  other arithmetic  1.82 us (3%)
    pallas_call x1, Pallas kernels, body(): pl.pallas_call(lambda *refs: local_kernel(s, n_band, *refs), out_shape=(j...  19.8 us
    pallas_call x1, Pallas kernels, body(): pl.pallas_call(lambda *refs: boundary_kernel(s, n_band, scale, *refs), ou...  12.3 us
    ppermute x7, waiting for transfers between devices, exchange(): return lax.ppermute(value, AXES, [(i, i ^ distance) for i in range(size)])  8.26 us
    ppermute x7, starting transfers between devices, exchange(): return lax.ppermute(value, AXES, [(i, i ^ distance) for i in range(size)])  7.1 us
    ppermute x1, starting transfers between devices, body(): from_above = lax.ppermute(down, AXES, [(j, i) for i, j in step])  5.98 us
    pallas_call x1, Pallas kernels, body(): pl.pallas_call(lambda *refs: edge_kernel(s, *refs), out_shape=(jax.ShapeD...  4.86 us
  transfers between devices with their start and end apart: 9, of which 6 were waited for; matrix products, arithmetic and copies ran while one was open for 1% of the time, Pallas kernels for 32%

profile of v1, /device:TPU:0, one launch (start us, length us, event | category | flops | bytes accessed | tf_op | source)
XLA Modules:
  0.0 62.7 jit_solution(4850375871412256422)
XLA Ops:
  0.0 4.9 %shard_map.18 = (bf16[198,16,128]{2,1,0:T(8,128)(2,1)}, f32[8,8,128]{2,1,0:T(8,128)}) custom-call(f32[16,6,6,32,128]{4,3,2,1,0:T(8,128)} %bitcast.45), custom_call_target="tpu_custom_call" | custom-call | tf_op jit(solution)/shard_map/pallas_call | solution.py:360
  4.9 0.5 collective-permute-start
  5.4 6.0 %collective-permute-start.1 = (f32[8,8,128]{2,1,0:T(8,128)}, f32[8,8,128]{2,1,0:T(8,128)S(1)}, u32[]{:S(2)}, u32[]{:S(2)}) collective-permute-start(f32[8,8,128]{2,1,0:T(8,128)} %get-tuple-element.20), channel_id=1, source_target_pairs={{1,0},{2,1},{3,2},{4,3},{5,4},{6,5},{7,6},{8,7},{9,8},{10,9},{11,1... | collective-permute-start | bytes 98312 | tf_op jit(solution)/shard_map/ppermute | solution.py:370
  11.4 0.6 %pad_add_fusion.refs_0_ = s32[2]{0:T(128)} fusion(s32[1]{0:T(128)} %bitcast.1, s32[1]{0:T(128)} %bitcast), kind=kLoop, calls=%fused_computation.15 | loop fusion | flops 2 | bytes 16 | tf_op jit(solution)/shard_map/stack | solution.py:348
  12.0 19.8 %shard_map.17 = (f32[8,8,16,256]{3,2,1,0:T(8,128)}, f32[16,4,9,8,128]{4,3,2,1,0:T(8,128)}, f32[16,4,6,8,128]{4,3,2,1,0:T(8,128)}, f32[16,4,6,8,128]{4,3,2,1,0:T(8,128)}, f32[4,10,8,128]{3,2,1,0:T(8,128)}) custom-call(s32[2]{0:T(128)} %pad_add_fusion.refs_0_, f32[16,6,6,32,128]{4,3,2,1,0:T(8,128)} %bitcast.46), custom_call_target="tpu_custom_call" | custom-call | flops 2000000000 | bytes 20000000 | tf_op jit(solution)/shard_map/pallas_call | solution.py:380
  31.9 0.6 copy-done.1
  32.5 0.3 copy-done
  32.8 12.3 %shard_map.19 = (f32[4,4,32,256]{3,2,1,0:T(8,128)}, bf16[4,4,32,256]{3,2,1,0:T(8,128)(2,1)}) custom-call(s32[2]{0:T(128)} %pad_add_fusion.refs_0_, f32[8,8,16,256]{3,2,1,0:T(8,128)} %get-tuple-element.14.refs_1_, f32[16,4,9,8,128]{4,3,2,1,0:T(8,128)} %get-tuple-element.15.refs_2_, f32[16,4,6,8,128]{4,3,2,1,0:T(8,128)} %get-tuple-element.16.refs_3_, ...), custom_call_target="tpu_custom_call" | custom-call | tf_op jit(solution)/shard_map/pallas_call | solution.py:409
  45.1 1.7 %collective-permute-done.2 = bf16[4,4,32,256]{3,2,1,0:T(8,128)(2,1)S(1)} collective-permute-done((bf16[4,4,32,256]{3,2,1,0:T(8,128)(2,1)}, bf16[4,4,32,256]{3,2,1,0:T(8,128)(2,1)S(1)}, u32[]{:S(2)}, u32[]{:S(2)}) %collective-permute-start.2) | collective-permute-done | bytes 262176 | tf_op jit(solution)/shard_map/ppermute | solution.py:338
  46.8 1.1 %fusion.8 = (bf16[4,4,32,256]{3,2,1,0:T(8,128)(2,1)S(1)}, f32[4,4,32,256]{3,2,1,0:T(8,128)S(1)}) fusion(f32[4,4,32,256]{3,2,1,0:T(8,128)} %get-tuple-element.21, bf16[4,4,32,256]{3,2,1,0:T(8,128)(2,1)S(1)} %collective-permute-done.2), kind=kLoop, calls=%fused_computation.17 | loop fusion | flops 393216 | bytes 1572864 | tf_op jit(solution)/shard_map/convert.5
  48.0 1.0 %collective-permute-start.3 = (bf16[4,32,256]{2,1,0:T(8,128)(2,1)S(1)}, bf16[4,32,256]{2,1,0:T(8,128)(2,1)S(1)}, u32[]{:S(2)}, u32[]{:S(2)}) collective-permute-start(bf16[4,32,256]{2,1,0:T(8,128)(2,1)S(1)} %get-tuple-element.27), channel_id=1, source_target_pairs={{0,8},{1,9},{2,10},{3,11},{4,12},{5,13},{6,14},{7,15},{8,0},{9,1},... | collective-permute-start | bytes 196616 | tf_op jit(solution)/shard_map/ppermute | solution.py:338
  49.0 2.4 %collective-permute-start.5 = (bf16[4,32,256]{2,1,0:T(8,128)(2,1)S(1)}, bf16[4,32,256]{2,1,0:T(8,128)(2,1)S(1)}, u32[]{:S(2)}, u32[]{:S(2)}) collective-permute-start(bf16[4,32,256]{2,1,0:T(8,128)(2,1)S(1)} %get-tuple-element.28), channel_id=1, source_target_pairs={{0,24},{1,25},{2,26},{3,27},{4,28},{5,29},{6,30},{7,31},{8,16},{9,... | collective-permute-start | bytes 196616 | tf_op jit(solution)/shard_map/ppermute | solution.py:338
  51.4 0.2 collective-permute-start.4
  51.6 0.8 %collective-permute-done.3 = bf16[4,32,256]{2,1,0:T(8,128)(2,1)S(1)} collective-permute-done((bf16[4,32,256]{2,1,0:T(8,128)(2,1)S(1)}, bf16[4,32,256]{2,1,0:T(8,128)(2,1)S(1)}, u32[]{:S(2)}, u32[]{:S(2)}) %collective-permute-start.3) | collective-permute-done | bytes 65568 | tf_op jit(solution)/shard_map/ppermute | solution.py:338
  52.3 2.7 %collective-permute-done.5 = bf16[4,32,256]{2,1,0:T(8,128)(2,1)S(1)} collective-permute-done((bf16[4,32,256]{2,1,0:T(8,128)(2,1)S(1)}, bf16[4,32,256]{2,1,0:T(8,128)(2,1)S(1)}, u32[]{:S(2)}, u32[]{:S(2)}) %collective-permute-start.5) | collective-permute-done | bytes 65568 | tf_op jit(solution)/shard_map/ppermute | solution.py:338
  55.0 0.9 %collective-permute-done.4 = bf16[4,32,256]{2,1,0:T(8,128)(2,1)S(1)} collective-permute-done((bf16[4,32,256]{2,1,0:T(8,128)(2,1)S(1)}, bf16[4,32,256]{2,1,0:T(8,128)(2,1)S(1)}, u32[]{:S(2)}, u32[]{:S(2)}) %collective-permute-start.4) | collective-permute-done | bytes 65568 | tf_op jit(solution)/shard_map/ppermute | solution.py:338
  56.0 0.1 collective-permute-start.6
  56.1 0.7 %collective-permute-start.8 = (bf16[32,256]{1,0:T(8,128)(2,1)S(1)}, bf16[32,256]{1,0:T(8,128)(2,1)S(1)}, u32[]{:S(2)}, u32[]{:S(2)}) collective-permute-start(bf16[32,256]{1,0:T(8,128)(2,1)S(1)} %get-tuple-element.31), channel_id=1, source_target_pairs={{0,6},{1,7},{2,4},{3,5},{4,2},{5,3},{6,0},{7,1},{8,14},{9,15},{10,... | collective-permute-start | bytes 49160 | tf_op jit(solution)/shard_map/ppermute | solution.py:338
  56.8 2.8 %collective-permute-start.7 = (bf16[32,256]{1,0:T(8,128)(2,1)S(1)}, bf16[32,256]{1,0:T(8,128)(2,1)S(1)}, u32[]{:S(2)}, u32[]{:S(2)}) collective-permute-start(bf16[32,256]{1,0:T(8,128)(2,1)S(1)} %get-tuple-element.32), channel_id=1, source_target_pairs={{0,4},{1,5},{2,6},{3,7},{4,0},{5,1},{6,2},{7,3},{8,12},{9,13},{10,... | collective-permute-start | bytes 49160 | tf_op jit(solution)/shard_map/ppermute | solution.py:338
  59.6 0.4 collective-permute-done.6
  60.0 1.7 %collective-permute-done.8 = bf16[32,256]{1,0:T(8,128)(2,1)S(1)} collective-permute-done((bf16[32,256]{1,0:T(8,128)(2,1)S(1)}, bf16[32,256]{1,0:T(8,128)(2,1)S(1)}, u32[]{:S(2)}, u32[]{:S(2)}) %collective-permute-start.8) | collective-permute-done | bytes 16416 | tf_op jit(solution)/shard_map/ppermute | solution.py:338
  61.7 0.1 reshape.20
  61.8 0.2 copy.6
  62.0 0.7 %reshape.21 = f32[4,16,128]{2,1,0:T(8,128)} reshape(f32[4,16,8,16]{3,2,1,0:T(8,128)S(1)} %copy.6) | data formatting | bytes 65536 | tf_op jit(solution)/shard_map/reshape | solution.py:424
  (10 shorter events, 0.1 us)
Async XLA Ops:
  4.9 27.0 %collective-permute-start = (bf16[198,16,128]{2,1,0:T(8,128)(2,1)}, bf16[198,16,128]{2,1,0:T(8,128)(2,1)S(1)}, u32[]{:S(2)}, u32[]{:S(2)}) collective-permute-start(bf16[198,16,128]{2,1,0:T(8,128)(2,1)} %get-tuple-element.19), channel_id=1, source_target_pairs={{0,1},{1,2},{2,3},{3,4},{4,5},{5,6},{6,7},{7,8},{8,9},{9,10},{10,1... | collective-permute-start | bytes 2433032 | tf_op jit(solution)/shard_map/ppermute | solution.py:369
  5.4 26.5 %collective-permute-start.1 = (f32[8,8,128]{2,1,0:T(8,128)}, f32[8,8,128]{2,1,0:T(8,128)S(1)}, u32[]{:S(2)}, u32[]{:S(2)}) collective-permute-start(f32[8,8,128]{2,1,0:T(8,128)} %get-tuple-element.20), channel_id=1, source_target_pairs={{1,0},{2,1},{3,2},{4,3},{5,4},{6,5},{7,6},{8,7},{9,8},{10,9},{11,1... | collective-permute-start | bytes 98312 | tf_op jit(solution)/shard_map/ppermute | solution.py:370
  31.9 0.6 copy-start.1
  31.9 0.9 %copy-start = (bf16[198,16,128]{2,1,0:T(8,128)(2,1)}, bf16[198,16,128]{2,1,0:T(8,128)(2,1)S(1)}, u32[]{:S(2)}) copy-start(bf16[198,16,128]{2,1,0:T(8,128)(2,1)S(1)} %collective-permute-done.refs_6_) | copy-start | bytes 2433028
  45.1 1.7 %collective-permute-start.2 = (bf16[4,4,32,256]{3,2,1,0:T(8,128)(2,1)}, bf16[4,4,32,256]{3,2,1,0:T(8,128)(2,1)S(1)}, u32[]{:S(2)}, u32[]{:S(2)}) collective-permute-start(bf16[4,4,32,256]{3,2,1,0:T(8,128)(2,1)} %get-tuple-element.22), channel_id=1, source_target_pairs={{0,1},{1,0},{2,3},{3,2},{4,5},{5,4},{6,7},{7,6},{8,9},{9,8},{10,11... | collective-permute-start | bytes 786440 | tf_op jit(solution)/shard_map/ppermute | solution.py:338
  48.0 4.3 %collective-permute-start.3 = (bf16[4,32,256]{2,1,0:T(8,128)(2,1)S(1)}, bf16[4,32,256]{2,1,0:T(8,128)(2,1)S(1)}, u32[]{:S(2)}, u32[]{:S(2)}) collective-permute-start(bf16[4,32,256]{2,1,0:T(8,128)(2,1)S(1)} %get-tuple-element.27), channel_id=1, source_target_pairs={{0,8},{1,9},{2,10},{3,11},{4,12},{5,13},{6,14},{7,15},{8,0},{9,1},... | collective-permute-start | bytes 196616 | tf_op jit(solution)/shard_map/ppermute | solution.py:338
  49.0 6.0 %collective-permute-start.5 = (bf16[4,32,256]{2,1,0:T(8,128)(2,1)S(1)}, bf16[4,32,256]{2,1,0:T(8,128)(2,1)S(1)}, u32[]{:S(2)}, u32[]{:S(2)}) collective-permute-start(bf16[4,32,256]{2,1,0:T(8,128)(2,1)S(1)} %get-tuple-element.28), channel_id=1, source_target_pairs={{0,24},{1,25},{2,26},{3,27},{4,28},{5,29},{6,30},{7,31},{8,16},{9,... | collective-permute-start | bytes 196616 | tf_op jit(solution)/shard_map/ppermute | solution.py:338
  51.4 4.5 %collective-permute-start.4 = (bf16[4,32,256]{2,1,0:T(8,128)(2,1)S(1)}, bf16[4,32,256]{2,1,0:T(8,128)(2,1)S(1)}, u32[]{:S(2)}, u32[]{:S(2)}) collective-permute-start(bf16[4,32,256]{2,1,0:T(8,128)(2,1)S(1)} %get-tuple-element.29), channel_id=1, source_target_pairs={{0,16},{1,17},{2,18},{3,19},{4,20},{5,21},{6,22},{7,23},{8,24},{9,... | collective-permute-start | bytes 196616 | tf_op jit(solution)/shard_map/ppermute | solution.py:338
  56.0 4.0 %collective-permute-start.6 = (bf16[32,256]{1,0:T(8,128)(2,1)S(1)}, bf16[32,256]{1,0:T(8,128)(2,1)S(1)}, u32[]{:S(2)}, u32[]{:S(2)}) collective-permute-start(bf16[32,256]{1,0:T(8,128)(2,1)S(1)} %get-tuple-element.30), channel_id=1, source_target_pairs={{0,2},{1,3},{2,0},{3,1},{4,6},{5,7},{6,4},{7,5},{8,10},{9,11},{10,... | collective-permute-start | bytes 49160 | tf_op jit(solution)/shard_map/ppermute | solution.py:338
  56.1 5.6 %collective-permute-start.8 = (bf16[32,256]{1,0:T(8,128)(2,1)S(1)}, bf16[32,256]{1,0:T(8,128)(2,1)S(1)}, u32[]{:S(2)}, u32[]{:S(2)}) collective-permute-start(bf16[32,256]{1,0:T(8,128)(2,1)S(1)} %get-tuple-element.31), channel_id=1, source_target_pairs={{0,6},{1,7},{2,4},{3,5},{4,2},{5,3},{6,0},{7,1},{8,14},{9,15},{10,... | collective-permute-start | bytes 49160 | tf_op jit(solution)/shard_map/ppermute | solution.py:338
  56.8 4.9 %collective-permute-start.7 = (bf16[32,256]{1,0:T(8,128)(2,1)S(1)}, bf16[32,256]{1,0:T(8,128)(2,1)S(1)}, u32[]{:S(2)}, u32[]{:S(2)}) collective-permute-start(bf16[32,256]{1,0:T(8,128)(2,1)S(1)} %get-tuple-element.32), channel_id=1, source_target_pairs={{0,4},{1,5},{2,6},{3,7},{4,0},{5,1},{6,2},{7,3},{8,12},{9,13},{10,... | collective-permute-start | bytes 49160 | tf_op jit(solution)/shard_map/ppermute | solution.py:338

commit v2 on v0

v2 whole, which is shorter than its diff:
```python
import jax
import jax.numpy as jnp
from jax import lax
from jax.experimental import pallas as pl
from jax.experimental.pallas import tpu as pltpu
from jax.sharding import PartitionSpec as P

AXES = ("band", "slab")
LANES = 128
GROUP = 16
F32 = jnp.float32
BF16 = jnp.bfloat16
VMEM = pl.BlockSpec(memory_space=pltpu.VMEM)
SMEM = pl.BlockSpec(memory_space=pltpu.SMEM)
ANY = pl.BlockSpec(memory_space=pl.ANY)
PARAMS = pltpu.CompilerParams(vmem_limit_bytes=32 * 2**20)


class Sizes:
    def __init__(self, shape):
        self.bands, self.comps, self.planes, self.rows, cells = shape
        self.inner = self.planes - 2
        self.tiles = cells // LANES


def row(ref, s, q, c, x, y):
    if s.rows == 1:
        return ref[q, c, x]
    return ref[q, c, x, pl.ds(y, s.tiles, stride=s.rows), :]


def z_difference(value):
    tiles = value.shape[0]
    lane = lax.broadcasted_iota(jnp.int32, value.shape, 1)
    left = pltpu.roll(value, LANES - 1, 1)
    right = pltpu.roll(value, 1, 1)
    after = jnp.where(lane == LANES - 1, pltpu.roll(left, tiles - 1, 0), left)
    before = jnp.where(lane == 0, pltpu.roll(right, 1, 0), right)
    return after - before


def edge_kernel(s, x_ref, up_ref, down_ref, coefs, sums):
    last = s.rows - 1
    n = s.inner

    def band(q, carry):
        for c in range(s.comps):
            for p in range(n // 2):
                pair = [row(x_ref, s, q, c, 1 + 2 * p + k, last) for k in range(2)]
                up_ref[(q * s.comps + c) * (n // 2) + p] = jnp.concatenate(pair, 0).astype(BF16)
        return carry

    lax.fori_loop(0, s.bands, band, 0)

    def add(j, carry):
        c, x = (j // s.planes, j % s.planes)
        for y in range(s.rows):
            total = row(x_ref, s, 0, c, x, y)
            for q in range(1, s.bands):
                total = total + row(x_ref, s, q, c, x, y)
            sums[c, x, y] = total
        return carry

    lax.fori_loop(0, s.comps * s.planes, add, 0)
    currents = [[], [], []]
    for x in range(n):
        down_ref[x] = sums[3, x + 1, 0]
        down_ref[n + x] = sums[5, x + 1, 0]
        for y in range(s.rows):
            v = [sums[c, x + 1, y] for c in range(3)]
            b = [sums[c, x + 1, y] for c in range(3, 6)]

            def dy(c):
                high = sums[c, x + 1, y + 1] if y + 1 < s.rows else 0.0
                low = sums[c, x + 1, y - 1] if y else 0.0
                return high - low

            def dx(c):
                return sums[c, x + 2, y] - sums[c, x, y]

            j = [dy(5) - z_difference(b[1]), z_difference(b[0]) - dx(5), dx(4) - dy(3)]
            j = [value * 0.5 for value in j]
            for d in range(3):
                coefs[x, y, d] = (v[d] - b[d]) * -0.25
                coefs[x, y, 3 + d] = (v[d] + b[d]) * -0.25
                coefs[x, y, 6 + d] = j[d]
                if y == last:
                    currents[d].append(j[d])
    base = s.bands * s.comps * (n // 2)
    for c in range(3):
        for p in range(n // 2):
            up_ref[base + c * (n // 2) + p] = jnp.concatenate(currents[c][2 * p : 2 * p + 2], 0).astype(BF16)


def transposed(s, source, zt):
    depth = source.shape[0] // s.tiles
    return source[pl.ds(zt, depth, stride=s.tiles), :].T.astype(BF16)


def put(s, target, zt, slot, block):
    target[zt, :, slot] = block.reshape(LANES // GROUP, GROUP, block.shape[-1])


def diagonal_products(s, rt, dt, zt, g):
    wide = s.bands * GROUP
    left = rt[zt, g].reshape(wide, rt.shape[-1])
    right = dt[zt, g].reshape(wide, dt.shape[-1])
    full = lax.dot_general(left, right, (((1,), (1,)), ((), ())), preferred_element_type=F32)
    full = full.reshape(s.bands, GROUP, wide)
    cell = lax.broadcasted_iota(jnp.int32, full.shape, 1)
    lane = lax.broadcasted_iota(jnp.int32, full.shape, 2)
    return jnp.sum(jnp.where(cell == lane % GROUP, full, 0.0), 1)


def slot_of(s, place, q, n_band):
    share = s.bands // n_band
    return (q // share ^ place[0]) * share + q % share


def cross(a, b):
    return [a[1] * b[2] - a[2] * b[1], a[2] * b[0] - a[0] * b[2], a[0] * b[1] - a[1] * b[0]]


def local_depth(s):
    return (s.rows - 1) * s.inner * 9 if s.rows > 1 else 0


def set_row(s, ref, entry, value):
    ref[pl.ds(entry * s.tiles, s.tiles), :] = value


def local_band(s, q, x_ref, coefs, above_ref, drive_ref, field_ref, sr, sd, between):
    n, last = (s.inner, s.rows - 1)
    entry = 0
    for y in range(s.rows):
        behind, here = ([row(x_ref, s, q, c, x, y) for c in range(6)] for x in range(2))
        for x in range(n):
            ahead = [row(x_ref, s, q, c, x + 2, y) for c in range(6)]
            f = here
            dx = [p - m for p, m in zip(ahead, behind)]
            dy, dz = ([], [])
            for c in range(6):
                high = row(x_ref, s, q, c, x + 1, y + 1) if y < last else None
                low = row(x_ref, s, q, c, x + 1, y - 1) if y else None
                if high is None:
                    dy.append(jnp.zeros_like(f[0]) if low is None else -low)
                else:
                    dy.append(high if low is None else high - low)
                dz.append(z_difference(f[c]))
            deltas = (dx, dy, dz)
            da, dc = ([], [])
            for c in range(3):
                plus = minus = None
                for d in range(3):
                    p = coefs[x, y, d] * (deltas[d][c] + deltas[d][c + 3])
                    m = coefs[x, y, 3 + d] * (deltas[d][c] - deltas[d][c + 3])
                    plus = p if plus is None else plus + p
                    minus = m if minus is None else minus + m
                da.append(plus + minus)
                dc.append(plus - minus)
            j = [(dy[5] - dz[4]) * 0.5, (dz[3] - dx[5]) * 0.5, (dx[4] - dy[3]) * 0.5]
            drives = da + dc
            if y == 0:
                for c in range(6):
                    drive_ref[q, x, c] = drives[c]
                    field_ref[q, x, c] = f[c]
                for c in range(3):
                    drive_ref[q, x, 6 + c] = j[c]
            else:
                turn = [coefs[x, y, 6 + d] * -0.5 for d in range(3)]
                if y == last:
                    turn = [turn[0] - above_ref[n + x] * 0.25, turn[1], turn[2] + above_ref[x] * 0.25]
                for a, b in zip(f + j, drives + cross(turn, f[3:6])):
                    set_row(s, sr, entry, a)
                    set_row(s, sd, entry, b)
                    entry += 1
            behind, here = (here, ahead)
        between(y)


def local_kernel(s, n_band, place, x_hbm, coefs, above_ref, g_ref, drive_ref, field_ref, x_ref, rt, dt, *rest):
    pads, sems = (rest[:-1], rest[-1])
    for q in range(s.bands):
        pltpu.make_async_copy(x_hbm.at[q], x_ref.at[q], sems.at[q]).start()
    used = local_depth(s)
    for ref in pads:
        tail = ref.shape[0] - used * s.tiles
        ref[pl.ds(used * s.tiles, tail), :] = jnp.zeros((tail, LANES), F32)

    def turn(sr, sd, q, tiles):
        for zt in tiles:
            put(s, rt, zt, slot_of(s, place, q, n_band), transposed(s, sr, zt))
            put(s, dt, zt, q, transposed(s, sd, zt))

    def pair(p, carry):
        for k in range(2):
            q = 2 * p + k
            pltpu.make_async_copy(x_hbm.at[q], x_ref.at[q], sems.at[q]).wait()
            other = pads[2 - 2 * k : 4 - 2 * k]
            before = lax.rem(q + s.bands - 1, s.bands)

            def between(y):
                if used:
                    turn(*other, before, range(y * s.tiles // s.rows, (y + 1) * s.tiles // s.rows))

            local_band(s, q, x_ref, coefs, above_ref, drive_ref, field_ref, *pads[2 * k : 2 * k + 2], between)
        return carry

    lax.fori_loop(0, s.bands // 2, pair, 0)

    def tile(zt, carry):
        for g in range(LANES // GROUP):
            g_ref[zt, g] = diagonal_products(s, rt, dt, zt, g)
        return carry

    if used:
        turn(*pads[2:4], s.bands - 1, range(s.tiles))
        lax.fori_loop(0, s.tiles, tile, 0)
    else:
        g_ref[...] = jnp.zeros_like(g_ref)


def halo_pair(s, up_ref, index):
    rows = []
    for p in range(s.inner // 2):
        both = up_ref[index * (s.inner // 2) + p].astype(F32)
        rows += [both[: s.tiles], both[s.tiles :]]
    return rows


def boundary_kernel(s, n_band, scale, place, g_ref, drive_ref, field_ref, coefs, down_ref, up_ref, above_ref, keep_ref, send_ref, tots, rt, dt, *pads):
    n = s.inner
    half = LANES // 2
    zero = jnp.zeros((s.tiles, LANES), F32)
    kinds = (1, 4, 3, 5)

    def add(q, totals):
        rows = sum([halo_pair(s, up_ref, q * s.comps + c) for c in kinds], [])
        return [t + r for t, r in zip(totals, rows)]

    totals = lax.fori_loop(0, s.bands, add, [zero] * (4 * n))
    behinds = [halo_pair(s, up_ref, s.bands * s.comps + c) for c in range(3)]
    for x in range(n):
        vy, my, bx, bz = (totals[k * n + x] for k in range(4))
        tots[x, 0] = coefs[x, 0, 1]
        tots[x, 1] = coefs[x, 0, 4]
        tots[x, 2] = (vy - my) * -0.25
        tots[x, 3] = (vy + my) * -0.25
        j = [coefs[x, 0, 6] - bz * 0.5, coefs[x, 0, 7], coefs[x, 0, 8] + bx * 0.5]
        if s.rows == 1:
            j = [j[0] + above_ref[n + x] * 0.5, j[1], j[2] - above_ref[x] * 0.5]
        behind = [behinds[0][x] + down_ref[n + x] * 0.5, behinds[1][x], behinds[2][x] - down_ref[x] * 0.5]
        for c in range(3):
            tots[x, 4 + c] = j[c] * -0.5
            tots[x, 7 + c] = behind[c] * -0.5
    used = n * 15
    for ref in pads:
        for start in (0, half):
            tail = (half - used) * s.tiles
            ref[pl.ds((start + used) * s.tiles, tail), :] = jnp.zeros((tail, LANES), F32)

    def turn(pad, q, tiles):
        lane = lax.broadcasted_iota(jnp.int32, (LANES, LANES), 1)
        for zt in tiles:
            block = transposed(s, pad, zt)
            put(s, rt, zt, slot_of(s, place, q, n_band), block)
            put(s, dt, zt, q, jnp.where(lane < half, pltpu.roll(block, half, 1), jnp.zeros_like(block)))

    def band(q, pad, between):
        entry = 0
        h_all = [halo_pair(s, up_ref, q * s.comps + c) for c in range(6)]
        for x in range(n):
            f = [field_ref[q, x, c] for c in range(6)]
            h = [h_all[c][x] for c in range(6)]
            da, dc, ea, ec = ([], [], [], [])
            for c in range(3):
                p = tots[x, 0] * (h[c] + h[c + 3])
                m = tots[x, 1] * (h[c] - h[c + 3])
                da.append(drive_ref[q, x, c] - (p + m))
                dc.append(drive_ref[q, x, 3 + c] - (p - m))
                p = tots[x, 2] * (f[c] + f[c + 3])
                m = tots[x, 3] * (f[c] - f[c + 3])
                ea.append(p + m)
                ec.append(p - m)
            behind = cross([tots[x, 7 + c] for c in range(3)], h[3:6])
            dc[0] = dc[0] - behind[2] * 0.5
            dc[2] = dc[2] + behind[0] * 0.5
            j = [drive_ref[q, x, 6] - h[5] * 0.5, drive_ref[q, x, 7], drive_ref[q, x, 8] + h[3] * 0.5]
            left = f + j + h
            right = da + dc + cross([tots[x, 4 + c] for c in range(3)], f[3:6]) + ea + ec
            for a, b in zip(left, right):
                set_row(s, pad, entry, a)
                set_row(s, pad, half + entry, b)
                entry += 1
            between(x)

    def pair(p, carry):
        for k in range(2):
            q = 2 * p + k
            before = lax.rem(q + s.bands - 1, s.bands)
            band(q, pads[k], lambda x: turn(pads[1 - k], before, range(x * s.tiles // n, (x + 1) * s.tiles // n)))
        return carry

    lax.fori_loop(0, s.bands // 2, pair, 0)
    turn(pads[1], s.bands - 1, range(s.tiles))
    share = s.bands // n_band

    def tile(r, carry):
        for core in range(2):
            zt = (r * 2 + core) ^ place[1]
            parts = [(diagonal_products(s, rt, dt, zt, g) + g_ref[zt, g]) * scale for g in range(LANES // GROUP)]
            for b in range(n_band):
                block = jnp.concatenate([p[b * share : (b + 1) * share] for p in parts], 0)
                if core == 0:
                    keep_ref[r, b] = block
                else:
                    send_ref[r, b] = block.astype(BF16)
        return carry

    lax.fori_loop(0, s.tiles // 2, tile, 0)


def exchange(value, distance, size):
    return lax.ppermute(value, AXES, [(i, i ^ distance) for i in range(size)])


def body(band_fields):
    s = Sizes(band_fields.shape)
    n_band, n_slab = (lax.axis_size("band"), lax.axis_size("slab"))
    devices = n_band * n_slab
    n, tiles, rows = (s.inner, s.tiles, s.rows)
    x = band_fields.reshape(s.bands, s.comps, s.planes, rows, tiles, LANES)
    x = x.transpose(0, 1, 2, 4, 3, 5).reshape(s.bands, s.comps, s.planes, tiles * rows, LANES)
    place = jnp.stack([lax.axis_index("band"), lax.axis_index("slab")]).astype(jnp.int32)

    def vector(*lead):
        return jax.ShapeDtypeStruct(lead + (tiles, LANES), F32)

    depth = -(-(max(local_depth(s), 1)) // LANES) * LANES
    groups = LANES // GROUP
    wide = s.bands * GROUP
    share = s.bands // n_band
    rows_up = (s.bands * s.comps + 3) * (n // 2)

    up, down, coefs = pl.pallas_call(
        lambda *refs: edge_kernel(s, *refs),
        out_shape=(jax.ShapeDtypeStruct((rows_up, 2 * tiles, LANES), BF16), vector(2 * n), vector(n, rows, 9)),
        in_specs=[VMEM],
        out_specs=(VMEM,) * 3,
        scratch_shapes=[pltpu.VMEM((s.comps, s.planes, rows, tiles, LANES), F32)],
        compiler_params=PARAMS,
    )(x)
    step = [(i, (i + 1) % devices) for i in range(devices)]
    from_below = lax.ppermute(up, AXES, step)
    from_above = lax.ppermute(down, AXES, [(j, i) for i, j in step])

    def operands(used, pads):
        return [pltpu.VMEM((tiles, groups, s.bands, GROUP, used), BF16)] * 2 + [pltpu.VMEM((used * tiles, LANES), F32)] * pads

    local, drive, field = pl.pallas_call(
        lambda *refs: local_kernel(s, n_band, *refs),
        out_shape=(jax.ShapeDtypeStruct((tiles, groups, s.bands, wide), F32), vector(s.bands, n, 9), vector(s.bands, n, 6)),
        in_specs=[SMEM, ANY, VMEM, VMEM],
        out_specs=(VMEM,) * 3,
        scratch_shapes=[pltpu.VMEM(x.shape, F32)] + operands(depth, 4) + [pltpu.SemaphoreType.DMA((s.bands,))],
        compiler_params=PARAMS,
        cost_estimate=pl.CostEstimate(flops=2 * 10**9, bytes_accessed=2 * 10**7, transcendentals=0),
    )(place, x, coefs, from_above)
    if rows == 1:
        two = lax.ppermute(down, AXES, [(i, (i + 2) % devices) for i in range(devices)])
        two = two.reshape(2, n // 2, 2 * tiles, LANES) * 0.5
        base = s.bands * s.comps * (n // 2)
        behind = from_below[base:].astype(F32).reshape(3, n // 2, 2 * tiles, LANES)
        behind = jnp.stack([behind[0] - two[1], behind[1], behind[2] + two[0]])
        behind = behind.reshape(3 * (n // 2), 2 * tiles, LANES).astype(BF16)
        from_below = jnp.concatenate([from_below[:base], behind], 0)

    shape = (tiles // 2, n_band, groups * share, wide)
    scale = 1.0 / (n * rows * devices)
    keep, send = pl.pallas_call(
        lambda *refs: boundary_kernel(s, n_band, scale, *refs),
        out_shape=(jax.ShapeDtypeStruct(shape, F32), jax.ShapeDtypeStruct(shape, BF16)),
        in_specs=[SMEM] + [VMEM] * 7,
        out_specs=(VMEM, VMEM),
        scratch_shapes=[pltpu.VMEM((n, 10, tiles, LANES), F32)] + operands(LANES, 2),
        compiler_params=PARAMS,
    )(place, local, drive, field, coefs, down, from_below, from_above)

    value = keep + exchange(send, 1, devices).astype(F32)
    parts = [exchange(value[:, d].astype(BF16), d * n_slab, devices) for d in range(1, n_band)]
    value = sum([p.astype(F32) for p in parts], value[:, 0])
    parts = [exchange(value[e].astype(BF16), 2 * e, devices) for e in range(1, tiles // 2)]
    value = sum([p.astype(F32) for p in parts], value[0])
    value = value.reshape(groups, share, s.bands, GROUP).transpose(1, 2, 0, 3)
    return value.reshape(share, s.bands, groups * GROUP)


def solution(mesh):
    return jax.shard_map(
        body,
        mesh=mesh,
        in_specs=(P(None, None, None, AXES, None),),
        out_specs=P("band", None, "slab"),
        check_vma=False,
    )
```

time: 502 us -> 61 us (0.12); the launches traced: 496 us -> 60.9 us
  local copies, waits for them, and re-layouts: 276 us -> 8.4 us
  waiting for transfers between devices: 111 us -> 12.1 us
  matrix products: 47.8 us -> 0 us
  other arithmetic: 41 us -> 0.2 us
  Pallas kernels: 0 us -> 25.2 us
  between operations: 14 us -> 0.09 us
  starting transfers between devices: 6.42 us -> 14.9 us
    reduce_scatter x2 -> x0, waiting for transfers between devices: 111 us -> none  [the longest x1 87.9 us: body(): lax.psum_scatter(partial_value, 'slab', scatter_dimension=2, tiled=True)]
    convert_element_type x1 -> x2, local copies, waits for them, and re-layouts: 103 us -> 0.02 us  [the longest x1 0.02 us: body(): value[:, d].astype(BF16)]
    concatenate x1 -> x0, local copies, waits for them, and re-layouts: 103 us -> none  [make_drive(): jnp.concatenate([part_a, part_c, -hall_length * cross], 1)]
    dot_general x1 -> x0, matrix products: 47.8 us -> none  [body(): jnp.einsum('qcxyz,kcxyz->qkz', resp, drive, preferred_element_type=jnp.fl...]
    slice x5 -> x0, local copies, waits for them, and re-layouts: 36.2 us -> none  [the longest x2 14 us: body(): ddz = (jnp.roll(inner, -1, 4) - jnp.roll(inner, 1, 4)) * 0.5]
    mul x3 -> x0, other arithmetic: 26.8 us -> none  [the longest x1 22 us: body(): ddz = (jnp.roll(inner, -1, 4) - jnp.roll(inner, 1, 4)) * 0.5]
    pallas_call x0 -> x3, Pallas kernels: none -> 25.2 us  [the longest x1 14.5 us: body(): pl.pallas_call(lambda *refs: local_kernel(s, n_band, *refs), out_shape=(j...]
    unnamed x17 -> x4, local copies, waits for them, and re-layouts: 31.9 us -> 7.36 us
  transfers between devices with their start and end apart: 4 -> 9, of which waited for: 2 -> 7; matrix products, arithmetic and copies ran while one was open for 16% -> 0% of each run, Pallas kernels for 0% -> 24%
where the time goes in v2:
time: 61 us; the launch traced here: 60.9 us
  Pallas kernels  25.2 us (41%)
  starting transfers between devices  14.9 us (24%)
  waiting for transfers between devices  12.1 us (20%)
  local copies, waits for them, and re-layouts  8.4 us (14%)
    pallas_call x1, Pallas kernels, body(): pl.pallas_call(lambda *refs: local_kernel(s, n_band, *refs), out_shape=(j...  14.5 us
    ppermute x7, waiting for transfers between devices, exchange(): return lax.ppermute(value, AXES, [(i, i ^ distance) for i in range(size)])  10.3 us
    pallas_call x1, Pallas kernels, body(): pl.pallas_call(lambda *refs: boundary_kernel(s, n_band, scale, *refs), ou...  9.17 us
    ppermute x7, starting transfers between devices, exchange(): return lax.ppermute(value, AXES, [(i, i ^ distance) for i in range(size)])  8.45 us
    unnamed x4, local copies, waits for them, and re-layouts  7.36 us
    ppermute x1, starting transfers between devices, body(): from_above = lax.ppermute(down, AXES, [(j, i) for i, j in step])  5.99 us
    ppermute x1, waiting for transfers between devices, body(): from_above = lax.ppermute(down, AXES, [(j, i) for i, j in step])  1.77 us
    pallas_call x1, Pallas kernels, body(): pl.pallas_call(lambda *refs: edge_kernel(s, *refs), out_shape=(jax.ShapeD...  1.47 us
  transfers between devices with their start and end apart: 9, of which 7 were waited for; matrix products, arithmetic and copies ran while one was open for 0% of the time, Pallas kernels for 24%

profile of v2, /device:TPU:0, one launch (start us, length us, event | category | flops | bytes accessed | tf_op | source)
XLA Modules:
  0.0 60.9 jit_solution(6502810045176456550)
XLA Ops:
  0.0 3.7 %copy-done = f32[16,6,6,4,1024]{4,3,2,1,0:T(4,128)S(1)} copy-done((f32[16,6,6,4,1024]{4,3,2,1,0:T(4,128)S(1)}, f32[16,6,6,4,1024]{4,3,2,1,0:T(4,128)}, u32[]{:S(2)}) %copy-start) | copy-done | bytes 9437208
  3.7 1.5 %shard_map.17 = (bf16[198,16,128]{2,1,0:T(8,128)(2,1)S(1)}, f32[8,8,128]{2,1,0:T(8,128)S(1)}, f32[4,4,9,8,128]{4,3,2,1,0:T(8,128)S(1)}) custom-call(f32[16,6,6,32,128]{4,3,2,1,0:T(8,128)S(1)} %bitcast.45), custom_call_target="tpu_custom_call" | custom-call | tf_op jit(solution)/shard_map/pallas_call | solution.py:345
  5.2 0.5 collective-permute-start.1
  5.7 6.0 %collective-permute-start = (f32[8,8,128]{2,1,0:T(8,128)S(1)}, f32[8,8,128]{2,1,0:T(8,128)S(1)}, u32[]{:S(2)}, u32[]{:S(2)}) collective-permute-start(f32[8,8,128]{2,1,0:T(8,128)S(1)} %get-tuple-element.14.refs_5_), channel_id=1, source_target_pairs={{1,0},{2,1},{3,2},{4,3},{5,4},{6,5},{7,6},{8,7},{9,8},{10,9},{11,1... | collective-permute-start | bytes 98312 | tf_op jit(solution)/shard_map/ppermute | solution.py:355
  11.7 1.8 %collective-permute-done.refs_3_.refs_7_ = f32[8,8,128]{2,1,0:T(8,128)S(1)} collective-permute-done((f32[8,8,128]{2,1,0:T(8,128)S(1)}, f32[8,8,128]{2,1,0:T(8,128)S(1)}, u32[]{:S(2)}, u32[]{:S(2)}) %collective-permute-start) | collective-permute-done | bytes 32800 | tf_op jit(solution)/shard_map/ppermute | solution.py:355
  13.5 3.7 %copy-done.1 = f32[16,6,6,4,1024]{4,3,2,1,0:T(4,128)S(1)} copy-done((f32[16,6,6,4,1024]{4,3,2,1,0:T(4,128)S(1)}, f32[16,6,6,4,1024]{4,3,2,1,0:T(4,128)}, u32[]{:S(2)}) %copy-start.1) | copy-done | bytes 9437208
  17.2 14.5 %shard_map.18 = (f32[8,8,16,256]{3,2,1,0:T(8,128)S(1)}, f32[16,4,9,8,128]{4,3,2,1,0:T(8,128)S(1)}, f32[16,4,6,8,128]{4,3,2,1,0:T(8,128)S(1)}) custom-call(s32[2]{0:T(128)S(1)} %pad_add_fusion.refs_0_, f32[16,6,6,32,128]{4,3,2,1,0:T(8,128)S(1)} %bitcast.46, f32[4,4,9,8,128]{4,3,2,1,0:T(8,128)S(1)} %get-tuple-element.13.refs_2_.refs_4_, ...), custom_call_target="tpu_custom_call" | custom-call | flops 2000000000 | bytes 20000000 | tf_op jit(solution)/shard_map/pallas_call | solution.py:360
  31.7 9.2 %shard_map.19 = (f32[4,4,32,256]{3,2,1,0:T(8,128)S(1)}, bf16[4,4,32,256]{3,2,1,0:T(8,128)(2,1)S(1)}) custom-call(s32[2]{0:T(128)S(1)} %pad_add_fusion.refs_0_, f32[8,8,16,256]{3,2,1,0:T(8,128)S(1)} %get-tuple-element.15.refs_1_, f32[16,4,9,8,128]{4,3,2,1,0:T(8,128)S(1)} %get-tuple-element.16.refs_2_, f32[16,4,6,8,128]{4,3,2,1,0:T(8,128)S(1)} %get-tuple-element.17.refs_3_, ...), custom_call_target="tpu_custom_call" | custom-call | tf_op jit(solution)/shard_map/pallas_call | solution.py:380
  41.0 1.5 %collective-permute-done.2 = bf16[4,4,32,256]{3,2,1,0:T(8,128)(2,1)S(1)} collective-permute-done((bf16[4,4,32,256]{3,2,1,0:T(8,128)(2,1)S(1)}, bf16[4,4,32,256]{3,2,1,0:T(8,128)(2,1)S(1)}, u32[]{:S(2)}, u32[]{:S(2)}) %collective-permute-start.2) | collective-permute-done | bytes 262176 | tf_op jit(solution)/shard_map/ppermute | solution.py:324
  42.5 0.1 fusion.8
  42.6 1.0 %collective-permute-start.3 = (bf16[4,32,256]{2,1,0:T(8,128)(2,1)S(1)}, bf16[4,32,256]{2,1,0:T(8,128)(2,1)S(1)}, u32[]{:S(2)}, u32[]{:S(2)}) collective-permute-start(bf16[4,32,256]{2,1,0:T(8,128)(2,1)S(1)} %get-tuple-element.25), channel_id=1, source_target_pairs={{0,8},{1,9},{2,10},{3,11},{4,12},{5,13},{6,14},{7,15},{8,0},{9,1},... | collective-permute-start | bytes 196616 | tf_op jit(solution)/shard_map/ppermute | solution.py:324
  43.6 2.4 %collective-permute-start.5 = (bf16[4,32,256]{2,1,0:T(8,128)(2,1)S(1)}, bf16[4,32,256]{2,1,0:T(8,128)(2,1)S(1)}, u32[]{:S(2)}, u32[]{:S(2)}) collective-permute-start(bf16[4,32,256]{2,1,0:T(8,128)(2,1)S(1)} %get-tuple-element.26), channel_id=1, source_target_pairs={{0,24},{1,25},{2,26},{3,27},{4,28},{5,29},{6,30},{7,31},{8,16},{9,... | collective-permute-start | bytes 196616 | tf_op jit(solution)/shard_map/ppermute | solution.py:324
  46.0 0.2 collective-permute-start.4
  46.2 0.7 %collective-permute-done.3 = bf16[4,32,256]{2,1,0:T(8,128)(2,1)S(1)} collective-permute-done((bf16[4,32,256]{2,1,0:T(8,128)(2,1)S(1)}, bf16[4,32,256]{2,1,0:T(8,128)(2,1)S(1)}, u32[]{:S(2)}, u32[]{:S(2)}) %collective-permute-start.3) | collective-permute-done | bytes 65568 | tf_op jit(solution)/shard_map/ppermute | solution.py:324
  46.9 2.9 %collective-permute-done.5 = bf16[4,32,256]{2,1,0:T(8,128)(2,1)S(1)} collective-permute-done((bf16[4,32,256]{2,1,0:T(8,128)(2,1)S(1)}, bf16[4,32,256]{2,1,0:T(8,128)(2,1)S(1)}, u32[]{:S(2)}, u32[]{:S(2)}) %collective-permute-start.5) | collective-permute-done | bytes 65568 | tf_op jit(solution)/shard_map/ppermute | solution.py:324
  49.8 1.1 %collective-permute-done.4 = bf16[4,32,256]{2,1,0:T(8,128)(2,1)S(1)} collective-permute-done((bf16[4,32,256]{2,1,0:T(8,128)(2,1)S(1)}, bf16[4,32,256]{2,1,0:T(8,128)(2,1)S(1)}, u32[]{:S(2)}, u32[]{:S(2)}) %collective-permute-start.4) | collective-permute-done | bytes 65568 | tf_op jit(solution)/shard_map/ppermute | solution.py:324
  50.9 0.9 %collective-permute-start.6 = (bf16[32,256]{1,0:T(8,128)(2,1)S(1)}, bf16[32,256]{1,0:T(8,128)(2,1)S(1)}, u32[]{:S(2)}, u32[]{:S(2)}) collective-permute-start(bf16[32,256]{1,0:T(8,128)(2,1)S(1)} %get-tuple-element.28), channel_id=1, source_target_pairs={{0,2},{1,3},{2,0},{3,1},{4,6},{5,7},{6,4},{7,5},{8,10},{9,11},{10,... | collective-permute-start | bytes 49160 | tf_op jit(solution)/shard_map/ppermute | solution.py:324
  51.9 3.3 %collective-permute-start.8 = (bf16[32,256]{1,0:T(8,128)(2,1)S(1)}, bf16[32,256]{1,0:T(8,128)(2,1)S(1)}, u32[]{:S(2)}, u32[]{:S(2)}) collective-permute-start(bf16[32,256]{1,0:T(8,128)(2,1)S(1)} %get-tuple-element.29), channel_id=1, source_target_pairs={{0,6},{1,7},{2,4},{3,5},{4,2},{5,3},{6,0},{7,1},{8,14},{9,15},{10,... | collective-permute-start | bytes 49160 | tf_op jit(solution)/shard_map/ppermute | solution.py:324
  55.2 0.5 collective-permute-start.7
  55.7 1.7 %collective-permute-done.8 = bf16[32,256]{1,0:T(8,128)(2,1)S(1)} collective-permute-done((bf16[32,256]{1,0:T(8,128)(2,1)S(1)}, bf16[32,256]{1,0:T(8,128)(2,1)S(1)}, u32[]{:S(2)}, u32[]{:S(2)}) %collective-permute-start.8) | collective-permute-done | bytes 16416 | tf_op jit(solution)/shard_map/ppermute | solution.py:324
  57.4 2.4 %collective-permute-done.7 = bf16[32,256]{1,0:T(8,128)(2,1)S(1)} collective-permute-done((bf16[32,256]{1,0:T(8,128)(2,1)S(1)}, bf16[32,256]{1,0:T(8,128)(2,1)S(1)}, u32[]{:S(2)}, u32[]{:S(2)}) %collective-permute-start.7) | collective-permute-done | bytes 16416 | tf_op jit(solution)/shard_map/ppermute | solution.py:324
  59.8 0.1 reshape.20
  60.0 0.2 copy.6
  60.1 0.7 %reshape.21 = f32[4,16,128]{2,1,0:T(8,128)} reshape(f32[4,16,8,16]{3,2,1,0:T(8,128)S(1)} %copy.6) | data formatting | bytes 65536 | tf_op jit(solution)/shard_map/reshape | solution.py:395
  (10 shorter events, 0.2 us)
Async XLA Ops:
  0.0 3.7 %copy-start = (f32[16,6,6,4,1024]{4,3,2,1,0:T(4,128)S(1)}, f32[16,6,6,4,1024]{4,3,2,1,0:T(4,128)}, u32[]{:S(2)}) copy-start(f32[16,6,6,4,1024]{4,3,2,1,0:T(4,128)} %param.1) | copy-start | bytes 28311556
  5.2 26.5 %collective-permute-start.1 = (bf16[198,16,128]{2,1,0:T(8,128)(2,1)S(1)}, bf16[198,16,128]{2,1,0:T(8,128)(2,1)S(1)}, u32[]{:S(2)}, u32[]{:S(2)}) collective-permute-start(bf16[198,16,128]{2,1,0:T(8,128)(2,1)S(1)} %get-tuple-element.18), channel_id=1, source_target_pairs={{0,1},{1,2},{2,3},{3,4},{4,5},{5,6},{6,7},{7,8},{8,9},{9,10},{10,1... | collective-permute-start | bytes 2433032 | tf_op jit(solution)/shard_map/ppermute | solution.py:354
  5.7 7.8 %collective-permute-start = (f32[8,8,128]{2,1,0:T(8,128)S(1)}, f32[8,8,128]{2,1,0:T(8,128)S(1)}, u32[]{:S(2)}, u32[]{:S(2)}) collective-permute-start(f32[8,8,128]{2,1,0:T(8,128)S(1)} %get-tuple-element.14.refs_5_), channel_id=1, source_target_pairs={{1,0},{2,1},{3,2},{4,3},{5,4},{6,5},{7,6},{8,7},{9,8},{10,9},{11,1... | collective-permute-start | bytes 98312 | tf_op jit(solution)/shard_map/ppermute | solution.py:355
  13.5 3.7 %copy-start.1 = (f32[16,6,6,4,1024]{4,3,2,1,0:T(4,128)S(1)}, f32[16,6,6,4,1024]{4,3,2,1,0:T(4,128)}, u32[]{:S(2)}) copy-start(f32[16,6,6,4,1024]{4,3,2,1,0:T(4,128)} %param.1) | copy-start | bytes 28311556
  40.9 1.6 %collective-permute-start.2 = (bf16[4,4,32,256]{3,2,1,0:T(8,128)(2,1)S(1)}, bf16[4,4,32,256]{3,2,1,0:T(8,128)(2,1)S(1)}, u32[]{:S(2)}, u32[]{:S(2)}) collective-permute-start(bf16[4,4,32,256]{3,2,1,0:T(8,128)(2,1)S(1)} %get-tuple-element.20), channel_id=1, source_target_pairs={{0,1},{1,0},{2,3},{3,2},{4,5},{5,4},{6,7},{7,6},{8,9},{9,8},{10,11... | collective-permute-start | bytes 786440 | tf_op jit(solution)/shard_map/ppermute | solution.py:324
  42.6 4.3 %collective-permute-start.3 = (bf16[4,32,256]{2,1,0:T(8,128)(2,1)S(1)}, bf16[4,32,256]{2,1,0:T(8,128)(2,1)S(1)}, u32[]{:S(2)}, u32[]{:S(2)}) collective-permute-start(bf16[4,32,256]{2,1,0:T(8,128)(2,1)S(1)} %get-tuple-element.25), channel_id=1, source_target_pairs={{0,8},{1,9},{2,10},{3,11},{4,12},{5,13},{6,14},{7,15},{8,0},{9,1},... | collective-permute-start | bytes 196616 | tf_op jit(solution)/shard_map/ppermute | solution.py:324
  43.6 6.2 %collective-permute-start.5 = (bf16[4,32,256]{2,1,0:T(8,128)(2,1)S(1)}, bf16[4,32,256]{2,1,0:T(8,128)(2,1)S(1)}, u32[]{:S(2)}, u32[]{:S(2)}) collective-permute-start(bf16[4,32,256]{2,1,0:T(8,128)(2,1)S(1)} %get-tuple-element.26), channel_id=1, source_target_pairs={{0,24},{1,25},{2,26},{3,27},{4,28},{5,29},{6,30},{7,31},{8,16},{9,... | collective-permute-start | bytes 196616 | tf_op jit(solution)/shard_map/ppermute | solution.py:324
  46.0 4.9 %collective-permute-start.4 = (bf16[4,32,256]{2,1,0:T(8,128)(2,1)S(1)}, bf16[4,32,256]{2,1,0:T(8,128)(2,1)S(1)}, u32[]{:S(2)}, u32[]{:S(2)}) collective-permute-start(bf16[4,32,256]{2,1,0:T(8,128)(2,1)S(1)} %get-tuple-element.27), channel_id=1, source_target_pairs={{0,16},{1,17},{2,18},{3,19},{4,20},{5,21},{6,22},{7,23},{8,24},{9,... | collective-permute-start | bytes 196616 | tf_op jit(solution)/shard_map/ppermute | solution.py:324
  50.9 4.7 %collective-permute-start.6 = (bf16[32,256]{1,0:T(8,128)(2,1)S(1)}, bf16[32,256]{1,0:T(8,128)(2,1)S(1)}, u32[]{:S(2)}, u32[]{:S(2)}) collective-permute-start(bf16[32,256]{1,0:T(8,128)(2,1)S(1)} %get-tuple-element.28), channel_id=1, source_target_pairs={{0,2},{1,3},{2,0},{3,1},{4,6},{5,7},{6,4},{7,5},{8,10},{9,11},{10,... | collective-permute-start | bytes 49160 | tf_op jit(solution)/shard_map/ppermute | solution.py:324
  51.9 5.6 %collective-permute-start.8 = (bf16[32,256]{1,0:T(8,128)(2,1)S(1)}, bf16[32,256]{1,0:T(8,128)(2,1)S(1)}, u32[]{:S(2)}, u32[]{:S(2)}) collective-permute-start(bf16[32,256]{1,0:T(8,128)(2,1)S(1)} %get-tuple-element.29), channel_id=1, source_target_pairs={{0,6},{1,7},{2,4},{3,5},{4,2},{5,3},{6,0},{7,1},{8,14},{9,15},{10,... | collective-permute-start | bytes 49160 | tf_op jit(solution)/shard_map/ppermute | solution.py:324
  55.2 4.6 %collective-permute-start.7 = (bf16[32,256]{1,0:T(8,128)(2,1)S(1)}, bf16[32,256]{1,0:T(8,128)(2,1)S(1)}, u32[]{:S(2)}, u32[]{:S(2)}) collective-permute-start(bf16[32,256]{1,0:T(8,128)(2,1)S(1)} %get-tuple-element.30), channel_id=1, source_target_pairs={{0,4},{1,5},{2,6},{3,7},{4,0},{5,1},{6,2},{7,3},{8,12},{9,13},{10,... | collective-permute-start | bytes 49160 | tf_op jit(solution)/shard_map/ppermute | solution.py:324

commit v3 on v2

--- a/solution.py
+++ b/solution.py
@@ -12,8 +12,10 @@
 BF16 = jnp.bfloat16
 VMEM = pl.BlockSpec(memory_space=pltpu.VMEM)
 SMEM = pl.BlockSpec(memory_space=pltpu.SMEM)
-ANY = pl.BlockSpec(memory_space=pl.ANY)
-PARAMS = pltpu.CompilerParams(vmem_limit_bytes=32 * 2**20)
+HBM = pl.BlockSpec(memory_space=pltpu.HBM)
+EDGE = pltpu.CompilerParams(vmem_limit_bytes=50 * 2**20)
+LOCAL = pltpu.CompilerParams(vmem_limit_bytes=38 * 2**20)
+BOUNDARY = pltpu.CompilerParams(vmem_limit_bytes=32 * 2**20)
 
 
 class Sizes:
@@ -39,9 +41,17 @@
     return after - before
 
 
-def edge_kernel(s, x_ref, up_ref, down_ref, coefs, sums):
+def edge_kernel(s, x_hbm, up_ref, down_ref, coefs, x_ref, sums, sems):
     last = s.rows - 1
     n = s.inner
+    whole, inside = (pl.ds(4, 2), pl.ds(0, 4))
+    copies = []
+    for q in range(s.bands):
+        copies.append(pltpu.make_async_copy(x_hbm.at[q, whole], x_ref.at[q, whole], sems.at[q, 0]))
+        part = (q, inside, pl.ds(1, n))
+        copies.append(pltpu.make_async_copy(x_hbm.at[part], x_ref.at[part], sems.at[q, 1]))
+    for copy in copies:
+        copy.start()
 
     def band(q, carry):
         for c in range(s.comps):
@@ -50,18 +60,32 @@
                 up_ref[(q * s.comps + c) * (n // 2) + p] = jnp.concatenate(pair, 0).astype(BF16)
         return carry
 
-    lax.fori_loop(0, s.bands, band, 0)
-
-    def add(j, carry):
-        c, x = (j // s.planes, j % s.planes)
+    def total_of(first, count, c, x):
         for y in range(s.rows):
-            total = row(x_ref, s, 0, c, x, y)
-            for q in range(1, s.bands):
+            total = row(x_ref, s, first, c, x, y)
+            for q in range(first + 1, first + count):
                 total = total + row(x_ref, s, q, c, x, y)
+            if first:
+                total = total + sums[c, x, y]
             sums[c, x, y] = total
-        return carry
-
-    lax.fori_loop(0, s.comps * s.planes, add, 0)
+
+    def add(first, count):
+        def one(j, carry):
+            c, x = (j // n, j % n + 1)
+            total_of(first, count, c, x)
+            return carry
+
+        lax.fori_loop(0, s.comps * n, one, 0)
+        for c in (4, 5):
+            for x in (0, s.planes - 1):
+                total_of(first, count, c, x)
+
+    share = s.bands // 4
+    for first in range(0, s.bands, share):
+        for copy in copies[2 * first : 2 * (first + share)]:
+            copy.wait()
+        lax.fori_loop(first, first + share, band, 0)
+        add(first, share)
     currents = [[], [], []]
     for x in range(n):
         down_ref[x] = sums[3, x + 1, 0]
@@ -101,10 +125,8 @@
     target[zt, :, slot] = block.reshape(LANES // GROUP, GROUP, block.shape[-1])
 
 
-def diagonal_products(s, rt, dt, zt, g):
+def diagonal_products(s, left, right):
     wide = s.bands * GROUP
-    left = rt[zt, g].reshape(wide, rt.shape[-1])
-    right = dt[zt, g].reshape(wide, dt.shape[-1])
     full = lax.dot_general(left, right, (((1,), (1,)), ((), ())), preferred_element_type=F32)
     full = full.reshape(s.bands, GROUP, wide)
     cell = lax.broadcasted_iota(jnp.int32, full.shape, 1)
@@ -121,24 +143,53 @@
     return [a[1] * b[2] - a[2] * b[1], a[2] * b[0] - a[0] * b[2], a[0] * b[1] - a[1] * b[0]]
 
 
+LAST_PAIRS = ((0, 1), (1, 0), (1, 2), (2, 1))
+
+
 def local_depth(s):
-    return (s.rows - 1) * s.inner * 9 if s.rows > 1 else 0
+    return (s.rows - 1) * s.inner * 9 + 4 * s.inner if s.rows > 1 else 0
 
 
 def set_row(s, ref, entry, value):
     ref[pl.ds(entry * s.tiles, s.tiles), :] = value
 
 
-def local_band(s, q, x_ref, coefs, above_ref, drive_ref, field_ref, sr, sd, between):
+def shift_matrix():
+    source = lax.broadcasted_iota(jnp.int32, (2 * LANES, 2 * LANES), 0) % LANES
+    target = lax.broadcasted_iota(jnp.int32, (2 * LANES, 2 * LANES), 1)
+    inside = jnp.where(source == target + 1, 1.0, jnp.where(source == target - 1, -1.0, 0.0))
+    carry_up = (target == 2 * LANES - 1) & (source == 0)
+    carry_down = (target == LANES) & (source == LANES - 1)
+    across = jnp.where(carry_up, 1.0, jnp.where(carry_down, -1.0, 0.0))
+    return jnp.where(target < LANES, inside, across).astype(BF16)
+
+
+def z_differences(s, values, matrix):
+    rows = jnp.concatenate(values, 0)
+    high = rows.astype(BF16)
+    low = (rows - high.astype(F32)).astype(BF16)
+    both = jnp.dot(jnp.concatenate([high, low], 1), matrix, preferred_element_type=F32)
+    lane = lax.broadcasted_iota(jnp.int32, (s.tiles, LANES), 1)
+    out = []
+    for i in range(len(values)):
+        part = both[i * s.tiles : (i + 1) * s.tiles]
+        across = part[:, LANES:]
+        across = jnp.where(lane < LANES // 2, pltpu.roll(across, 1, 0), pltpu.roll(across, s.tiles - 1, 0))
+        out.append(part[:, :LANES] + across)
+    return out
+
+
+def local_band(s, q, z_ref, x_ref, coefs, drive_ref, field_ref, sr, sd, before, between):
     n, last = (s.inner, s.rows - 1)
     entry = 0
     for y in range(s.rows):
+        before(y)
         behind, here = ([row(x_ref, s, q, c, x, y) for c in range(6)] for x in range(2))
         for x in range(n):
             ahead = [row(x_ref, s, q, c, x + 2, y) for c in range(6)]
             f = here
             dx = [p - m for p, m in zip(ahead, behind)]
-            dy, dz = ([], [])
+            dy, dz = ([], [z_ref[y, x, c] for c in range(6)])
             for c in range(6):
                 high = row(x_ref, s, q, c, x + 1, y + 1) if y < last else None
                 low = row(x_ref, s, q, c, x + 1, y - 1) if y else None
@@ -146,7 +197,6 @@
                     dy.append(jnp.zeros_like(f[0]) if low is None else -low)
                 else:
                     dy.append(high if low is None else high - low)
-                dz.append(z_difference(f[c]))
             deltas = (dx, dy, dz)
             da, dc = ([], [])
             for c in range(3):
@@ -168,9 +218,11 @@
                     drive_ref[q, x, 6 + c] = j[c]
             else:
                 turn = [coefs[x, y, 6 + d] * -0.5 for d in range(3)]
+                left, right = (f + j, drives + cross(turn, f[3:6]))
                 if y == last:
-                    turn = [turn[0] - above_ref[n + x] * 0.25, turn[1], turn[2] + above_ref[x] * 0.25]
-                for a, b in zip(f + j, drives + cross(turn, f[3:6])):
+                    left += [j[c] for c, _ in LAST_PAIRS]
+                    right += [f[3 + c] for _, c in LAST_PAIRS]
+                for a, b in zip(left, right):
                     set_row(s, sr, entry, a)
                     set_row(s, sd, entry, b)
                     entry += 1
@@ -178,15 +230,26 @@
         between(y)
 
 
-def local_kernel(s, n_band, place, x_hbm, coefs, above_ref, g_ref, drive_ref, field_ref, x_ref, rt, dt, *rest):
-    pads, sems = (rest[:-1], rest[-1])
+def local_kernel(s, n_band, place, x_hbm, coefs, rt, dt, drive_ref, field_ref, x_ref, sems, matrix, *rest):
+    n = s.inner
+    z_refs, pads = (rest[:2], rest[2:])
+
+    def fetch(q):
+        return pltpu.make_async_copy(x_hbm.at[q], x_ref.at[q], sems.at[q])
+
     for q in range(s.bands):
-        pltpu.make_async_copy(x_hbm.at[q], x_ref.at[q], sems.at[q]).start()
+        fetch(q).start()
+    matrix[...] = shift_matrix()
     used = local_depth(s)
     for ref in pads:
         tail = ref.shape[0] - used * s.tiles
         ref[pl.ds(used * s.tiles, tail), :] = jnp.zeros((tail, LANES), F32)
 
+    def shifted(z_ref, q, y):
+        values = [row(x_ref, s, q, c, x + 1, y) for x in range(n) for c in range(6)]
+        for i, value in enumerate(z_differences(s, values, matrix[...])):
+            z_ref[y, i // 6, i % 6] = value
+
     def turn(sr, sd, q, tiles):
         for zt in tiles:
             put(s, rt, zt, slot_of(s, place, q, n_band), transposed(s, sr, zt))
@@ -195,29 +258,33 @@
     def pair(p, carry):
         for k in range(2):
             q = 2 * p + k
-            pltpu.make_async_copy(x_hbm.at[q], x_ref.at[q], sems.at[q]).wait()
             other = pads[2 - 2 * k : 4 - 2 * k]
-            before = lax.rem(q + s.bands - 1, s.bands)
+            behind = lax.rem(q + s.bands - 1, s.bands)
+            ahead = lax.rem(q + 1, s.bands)
+
+            @pl.when(q + 1 < s.bands)
+            def _():
+                fetch(ahead).wait()
+
+            def before(y):
+                shifted(z_refs[1 - k], ahead, y)
 
             def between(y):
                 if used:
-                    turn(*other, before, range(y * s.tiles // s.rows, (y + 1) * s.tiles // s.rows))
-
-            local_band(s, q, x_ref, coefs, above_ref, drive_ref, field_ref, *pads[2 * k : 2 * k + 2], between)
+                    turn(*other, behind, range(y * s.tiles // s.rows, (y + 1) * s.tiles // s.rows))
+
+            local_band(s, q, z_refs[k], x_ref, coefs, drive_ref, field_ref, *pads[2 * k : 2 * k + 2], before, between)
         return carry
 
+    fetch(0).wait()
+    for y in range(s.rows):
+        shifted(z_refs[0], 0, y)
     lax.fori_loop(0, s.bands // 2, pair, 0)
-
-    def tile(zt, carry):
-        for g in range(LANES // GROUP):
-            g_ref[zt, g] = diagonal_products(s, rt, dt, zt, g)
-        return carry
-
     if used:
         turn(*pads[2:4], s.bands - 1, range(s.tiles))
-        lax.fori_loop(0, s.tiles, tile, 0)
     else:
-        g_ref[...] = jnp.zeros_like(g_ref)
+        rt[...] = jnp.zeros_like(rt)
+        dt[...] = jnp.zeros_like(dt)
 
 
 def halo_pair(s, up_ref, index):
@@ -228,7 +295,7 @@
     return rows
 
 
-def boundary_kernel(s, n_band, scale, place, g_ref, drive_ref, field_ref, coefs, down_ref, up_ref, above_ref, keep_ref, send_ref, tots, rt, dt, *pads):
+def boundary_kernel(s, n_band, scale, place, local_rt, local_dt, drive_ref, field_ref, coefs, down_ref, up_ref, above_ref, keep_ref, send_ref, tots, factors, rt, dt, *pads):
     n = s.inner
     half = LANES // 2
     zero = jnp.zeros((s.tiles, LANES), F32)
@@ -253,20 +320,30 @@
         for c in range(3):
             tots[x, 4 + c] = j[c] * -0.5
             tots[x, 7 + c] = behind[c] * -0.5
+    if s.rows > 1:
+        for k in range(2):
+            for entry in range(half):
+                e = k * half + entry - (s.rows - 2) * n * 9
+                x, i = divmod(e, 13)
+                value = jnp.ones((s.tiles, LANES), F32)
+                if 0 <= x < n and i >= 9:
+                    value = above_ref[(i - 9) // 2 * n + x] * (-0.25, 0.25, 0.25, -0.25)[i - 9]
+                set_row(s, pads[k], entry, value)
+        for zt in range(s.tiles):
+            both = [pads[k][pl.ds(zt, half, stride=s.tiles), :] for k in range(2)]
+            factors[zt] = jnp.concatenate(both, 0).T.astype(BF16).reshape(LANES // GROUP, GROUP, LANES)
     used = n * 15
     for ref in pads:
-        for start in (0, half):
-            tail = (half - used) * s.tiles
-            ref[pl.ds((start + used) * s.tiles, tail), :] = jnp.zeros((tail, LANES), F32)
-
-    def turn(pad, q, tiles):
-        lane = lax.broadcasted_iota(jnp.int32, (LANES, LANES), 1)
-        for zt in tiles:
-            block = transposed(s, pad, zt)
-            put(s, rt, zt, slot_of(s, place, q, n_band), block)
-            put(s, dt, zt, q, jnp.where(lane < half, pltpu.roll(block, half, 1), jnp.zeros_like(block)))
-
-    def band(q, pad, between):
+        tail = (half - used) * s.tiles
+        ref[pl.ds(used * s.tiles, tail), :] = jnp.zeros((tail, LANES), F32)
+
+    def turn(sr, sd, q, pairs):
+        for t in pairs:
+            for source, target, slot in ((sr, rt, slot_of(s, place, q, n_band)), (sd, dt, q)):
+                both = [source[pl.ds(2 * t + k, half, stride=s.tiles), :] for k in range(2)]
+                put(s, target, t, slot, jnp.concatenate(both, 0).T.astype(BF16))
+
+    def band(q, sr, sd, between):
         entry = 0
         h_all = [halo_pair(s, up_ref, q * s.comps + c) for c in range(6)]
         for x in range(n):
@@ -289,8 +366,8 @@
             left = f + j + h
             right = da + dc + cross([tots[x, 4 + c] for c in range(3)], f[3:6]) + ea + ec
             for a, b in zip(left, right):
-                set_row(s, pad, entry, a)
-                set_row(s, pad, half + entry, b)
+                set_row(s, sr, entry, a)
+                set_row(s, sd, entry, b)
                 entry += 1
             between(x)
 
@@ -298,17 +375,31 @@
         for k in range(2):
             q = 2 * p + k
             before = lax.rem(q + s.bands - 1, s.bands)
-            band(q, pads[k], lambda x: turn(pads[1 - k], before, range(x * s.tiles // n, (x + 1) * s.tiles // n)))
+            other = pads[2 - 2 * k : 4 - 2 * k]
+            band(q, *pads[2 * k : 2 * k + 2], lambda x: turn(*other, before, range(x * steps // n, (x + 1) * steps // n)))
         return carry
 
+    steps = s.tiles // 2
     lax.fori_loop(0, s.bands // 2, pair, 0)
-    turn(pads[1], s.bands - 1, range(s.tiles))
+    turn(*pads[2:4], s.bands - 1, range(steps))
+    wide = s.bands * GROUP
+    lane = lax.broadcasted_iota(jnp.int32, (wide, LANES), 1)
     share = s.bands // n_band
 
     def tile(r, carry):
         for core in range(2):
             zt = (r * 2 + core) ^ place[1]
-            parts = [(diagonal_products(s, rt, dt, zt, g) + g_ref[zt, g]) * scale for g in range(LANES // GROUP)]
+            wanted = (lane >= half) == ((core ^ place[1]) % 2 == 1)
+            parts = []
+            for g in range(LANES // GROUP):
+                left = rt[zt // 2, g].reshape(wide, LANES)
+                left = jnp.where(wanted, left, jnp.zeros_like(left))
+                right = dt[zt // 2, g].reshape(wide, LANES)
+                if s.rows > 1:
+                    scaled = local_rt[zt, g] * factors[zt, g][None]
+                    left = jnp.concatenate([scaled.reshape(wide, -1), left], 1)
+                    right = jnp.concatenate([local_dt[zt, g].reshape(wide, -1), right], 1)
+                parts.append(diagonal_products(s, left, right) * scale)
             for b in range(n_band):
                 block = jnp.concatenate([p[b * share : (b + 1) * share] for p in parts], 0)
                 if core == 0:
@@ -345,27 +436,27 @@
     up, down, coefs = pl.pallas_call(
         lambda *refs: edge_kernel(s, *refs),
         out_shape=(jax.ShapeDtypeStruct((rows_up, 2 * tiles, LANES), BF16), vector(2 * n), vector(n, rows, 9)),
-        in_specs=[VMEM],
+        in_specs=[HBM],
         out_specs=(VMEM,) * 3,
-        scratch_shapes=[pltpu.VMEM((s.comps, s.planes, rows, tiles, LANES), F32)],
-        compiler_params=PARAMS,
+        scratch_shapes=[pltpu.VMEM(x.shape, F32), pltpu.VMEM((s.comps, s.planes, rows, tiles, LANES), F32), pltpu.SemaphoreType.DMA((s.bands, 2))],
+        compiler_params=EDGE,
     )(x)
     step = [(i, (i + 1) % devices) for i in range(devices)]
     from_below = lax.ppermute(up, AXES, step)
     from_above = lax.ppermute(down, AXES, [(j, i) for i, j in step])
 
-    def operands(used, pads):
-        return [pltpu.VMEM((tiles, groups, s.bands, GROUP, used), BF16)] * 2 + [pltpu.VMEM((used * tiles, LANES), F32)] * pads
-
-    local, drive, field = pl.pallas_call(
+    turned = jax.ShapeDtypeStruct((tiles, groups, s.bands, GROUP, depth), BF16)
+    local_rt, local_dt, drive, field = pl.pallas_call(
         lambda *refs: local_kernel(s, n_band, *refs),
-        out_shape=(jax.ShapeDtypeStruct((tiles, groups, s.bands, wide), F32), vector(s.bands, n, 9), vector(s.bands, n, 6)),
-        in_specs=[SMEM, ANY, VMEM, VMEM],
-        out_specs=(VMEM,) * 3,
-        scratch_shapes=[pltpu.VMEM(x.shape, F32)] + operands(depth, 4) + [pltpu.SemaphoreType.DMA((s.bands,))],
-        compiler_params=PARAMS,
+        out_shape=(turned, turned, vector(s.bands, n, 9), vector(s.bands, n, 6)),
+        in_specs=[SMEM, HBM, VMEM],
+        out_specs=(VMEM,) * 4,
+        scratch_shapes=[pltpu.VMEM(x.shape, F32), pltpu.SemaphoreType.DMA((s.bands,)), pltpu.VMEM((2 * LANES, 2 * LANES), BF16)]
+        + [pltpu.VMEM((rows, n, 6, tiles, LANES), F32)] * 2
+        + [pltpu.VMEM((depth * tiles, LANES), F32)] * 4,
+        compiler_params=LOCAL,
         cost_estimate=pl.CostEstimate(flops=2 * 10**9, bytes_accessed=2 * 10**7, transcendentals=0),
-    )(place, x, coefs, from_above)
+    )(place, x, coefs)
     if rows == 1:
         two = lax.ppermute(down, AXES, [(i, (i + 2) % devices) for i in range(devices)])
         two = two.reshape(2, n // 2, 2 * tiles, LANES) * 0.5
@@ -380,11 +471,13 @@
     keep, send = pl.pallas_call(
         lambda *refs: boundary_kernel(s, n_band, scale, *refs),
         out_shape=(jax.ShapeDtypeStruct(shape, F32), jax.ShapeDtypeStruct(shape, BF16)),
-        in_specs=[SMEM] + [VMEM] * 7,
+        in_specs=[SMEM] + [VMEM] * 8,
         out_specs=(VMEM, VMEM),
-        scratch_shapes=[pltpu.VMEM((n, 10, tiles, LANES), F32)] + operands(LANES, 2),
-        compiler_params=PARAMS,
-    )(place, local, drive, field, coefs, down, from_below, from_above)
+        scratch_shapes=[pltpu.VMEM((n, 10, tiles, LANES), F32), pltpu.VMEM((tiles, groups, GROUP, LANES), BF16)]
+        + [pltpu.VMEM((tiles // 2, groups, s.bands, GROUP, LANES), BF16)] * 2
+        + [pltpu.VMEM((LANES // 2 * tiles, LANES), F32)] * 4,
+        compiler_params=BOUNDARY,
+    )(place, local_rt, local_dt, drive, field, coefs, down, from_below, from_above)
 
     value = keep + exchange(send, 1, devices).astype(F32)
     parts = [exchange(value[:, d].astype(BF16), d * n_slab, devices) for d in range(1, n_band)]

time: 61 us -> 46.2 us (0.76)
  local copies, waits for them, and re-layouts: 8.4 us -> 1.04 us
  waiting for transfers between devices: 12.1 us -> 8.05 us
  Pallas kernels: 25.2 us -> 23 us
  starting transfers between devices: 14.9 us -> 13.7 us
    unnamed x4 -> x0, local copies, waits for them, and re-layouts: 7.36 us -> none
    pallas_call x1, Pallas kernels: 14.5 us -> 10.6 us  [body(): pl.pallas_call(lambda *refs: local_kernel(s, n_band, *refs), out_shape=(t...]
    pallas_call x1, Pallas kernels: 1.47 us -> 4.02 us  [body(): pl.pallas_call(lambda *refs: edge_kernel(s, *refs), out_shape=(jax.ShapeD...]
    ppermute x7, waiting for transfers between devices: 10.3 us -> 8.05 us  [exchange(): return lax.ppermute(value, AXES, [(i, i ^ distance) for i in range(size)])]
    ppermute x1, waiting for transfers between devices: 1.77 us -> 0.01 us  [body(): from_above = lax.ppermute(down, AXES, [(j, i) for i, j in step])]
    ppermute x7, starting transfers between devices: 8.45 us -> 7.17 us  [exchange(): return lax.ppermute(value, AXES, [(i, i ^ distance) for i in range(size)])]
    pallas_call x1, Pallas kernels: 9.17 us -> 8.3 us  [body(): pl.pallas_call(lambda *refs: boundary_kernel(s, n_band, scale, *refs), ou...]
  transfers between devices with their start and end apart: 9 -> 9, of which waited for: 7 -> 6; matrix products, arithmetic and copies ran while one was open for 0% -> 0% of each run, Pallas kernels for 24% -> 23%
where the time goes in v3:
time: 46.2 us; the launch traced here: 46 us
  Pallas kernels  23 us (50%)
  starting transfers between devices  13.7 us (30%)
  waiting for transfers between devices  8.05 us (17%)
  local copies, waits for them, and re-layouts  1.04 us (2%)
    pallas_call x1, Pallas kernels, body(): pl.pallas_call(lambda *refs: local_kernel(s, n_band, *refs), out_shape=(t...  10.6 us
    pallas_call x1, Pallas kernels, body(): pl.pallas_call(lambda *refs: boundary_kernel(s, n_band, scale, *refs), ou...  8.3 us
    ppermute x7, waiting for transfers between devices, exchange(): return lax.ppermute(value, AXES, [(i, i ^ distance) for i in range(size)])  8.05 us
    ppermute x7, starting transfers between devices, exchange(): return lax.ppermute(value, AXES, [(i, i ^ distance) for i in range(size)])  7.17 us
    ppermute x1, starting transfers between devices, body(): from_above = lax.ppermute(down, AXES, [(j, i) for i, j in step])  5.99 us
    pallas_call x1, Pallas kernels, body(): pl.pallas_call(lambda *refs: edge_kernel(s, *refs), out_shape=(jax.ShapeD...  4.02 us
  transfers between devices with their start and end apart: 9, of which 6 were waited for; matrix products, arithmetic and copies ran while one was open for 0% of the time, Pallas kernels for 23%

profile of v3, /device:TPU:0, one launch (start us, length us, event | category | flops | bytes accessed | tf_op | source)
XLA Modules:
  0.0 46.0 jit_solution(11530479937992212092)
XLA Ops:
  0.0 4.0 %shard_map.17 = (bf16[198,16,128]{2,1,0:T(8,128)(2,1)S(1)}, f32[8,8,128]{2,1,0:T(8,128)S(1)}, f32[4,4,9,8,128]{4,3,2,1,0:T(8,128)S(1)}) custom-call(f32[16,6,6,32,128]{4,3,2,1,0:T(8,128)} %bitcast.45), custom_call_target="tpu_custom_call" | custom-call | tf_op jit(solution)/shard_map/pallas_call | solution.py:436
  4.0 0.5 %collective-permute-start = (bf16[198,16,128]{2,1,0:T(8,128)(2,1)S(1)}, bf16[198,16,128]{2,1,0:T(8,128)(2,1)S(1)}, u32[]{:S(2)}, u32[]{:S(2)}) collective-permute-start(bf16[198,16,128]{2,1,0:T(8,128)(2,1)S(1)} %get-tuple-element.20), channel_id=1, source_target_pairs={{0,1},{1,2},{2,3},{3,4},{4,5},{5,6},{6,7},{7,8},{8,9},{9,10},{10,1... | collective-permute-start | bytes 2433032 | tf_op jit(solution)/shard_map/ppermute | solution.py:445
  4.5 6.0 %collective-permute-start.1 = (f32[8,8,128]{2,1,0:T(8,128)S(1)}, f32[8,8,128]{2,1,0:T(8,128)S(1)}, u32[]{:S(2)}, u32[]{:S(2)}) collective-permute-start(f32[8,8,128]{2,1,0:T(8,128)S(1)} %get-tuple-element.19.refs_6_), channel_id=1, source_target_pairs={{1,0},{2,1},{3,2},{4,3},{5,4},{6,5},{7,6},{8,7},{9,8},{10,9},{11,1... | collective-permute-start | bytes 98312 | tf_op jit(solution)/shard_map/ppermute | solution.py:446
  10.5 0.1 pad_add_fusion.refs_0_
  10.6 10.6 %shard_map.18 = (bf16[8,8,16,16,128]{4,3,2,1,0:T(8,128)(2,1)S(1)}, bf16[8,8,16,16,128]{4,3,2,1,0:T(8,128)(2,1)S(1)}, f32[16,4,9,8,128]{4,3,2,1,0:T(8,128)S(1)}, f32[16,4,6,8,128]{4,3,2,1,0:T(8,128)S(1)}) custom-call(s32[2]{0:T(128)S(1)} %pad_add_fusion.refs_0_, f32[16,6,6,32,128]{4,3,2,1,0:T(8,128)} %bitcast.46, ...), custom_call_target="tpu_custom_call" | custom-call | flops 2000000000 | bytes 20000000 | tf_op jit(solution)/shard_map/pallas_call | solution.py:449
  21.3 0.0 collective-permute-done.1.refs_8_
  21.3 8.3 %shard_map.19 = (f32[4,4,32,256]{3,2,1,0:T(8,128)S(1)}, bf16[4,4,32,256]{3,2,1,0:T(8,128)(2,1)S(1)}) custom-call(s32[2]{0:T(128)S(1)} %pad_add_fusion.refs_0_, bf16[8,8,16,16,128]{4,3,2,1,0:T(8,128)(2,1)S(1)} %get-tuple-element.15.refs_1_, bf16[8,8,16,16,128]{4,3,2,1,0:T(8,128)(2,1)S(1)} %get-tuple-element.16.refs_2_, ...), custom_call_target="tpu_custom_call" | custom-call | tf_op jit(solution)/shard_map/pallas_call | solution.py:471
  29.6 0.1 collective-permute-start.2
  29.7 1.5 %collective-permute-done.2 = bf16[4,4,32,256]{3,2,1,0:T(8,128)(2,1)S(1)} collective-permute-done((bf16[4,4,32,256]{3,2,1,0:T(8,128)(2,1)S(1)}, bf16[4,4,32,256]{3,2,1,0:T(8,128)(2,1)S(1)}, u32[]{:S(2)}, u32[]{:S(2)}) %collective-permute-start.2) | collective-permute-done | bytes 262176 | tf_op jit(solution)/shard_map/ppermute | solution.py:415
  31.2 0.1 fusion.8
  31.3 1.0 %collective-permute-start.3 = (bf16[4,32,256]{2,1,0:T(8,128)(2,1)S(1)}, bf16[4,32,256]{2,1,0:T(8,128)(2,1)S(1)}, u32[]{:S(2)}, u32[]{:S(2)}) collective-permute-start(bf16[4,32,256]{2,1,0:T(8,128)(2,1)S(1)} %get-tuple-element.27), channel_id=1, source_target_pairs={{0,8},{1,9},{2,10},{3,11},{4,12},{5,13},{6,14},{7,15},{8,0},{9,1},... | collective-permute-start | bytes 196616 | tf_op jit(solution)/shard_map/ppermute | solution.py:415
  32.3 2.4 %collective-permute-start.5 = (bf16[4,32,256]{2,1,0:T(8,128)(2,1)S(1)}, bf16[4,32,256]{2,1,0:T(8,128)(2,1)S(1)}, u32[]{:S(2)}, u32[]{:S(2)}) collective-permute-start(bf16[4,32,256]{2,1,0:T(8,128)(2,1)S(1)} %get-tuple-element.28), channel_id=1, source_target_pairs={{0,24},{1,25},{2,26},{3,27},{4,28},{5,29},{6,30},{7,31},{8,16},{9,... | collective-permute-start | bytes 196616 | tf_op jit(solution)/shard_map/ppermute | solution.py:415
  34.7 0.1 collective-permute-start.4
  34.9 0.8 %collective-permute-done.3 = bf16[4,32,256]{2,1,0:T(8,128)(2,1)S(1)} collective-permute-done((bf16[4,32,256]{2,1,0:T(8,128)(2,1)S(1)}, bf16[4,32,256]{2,1,0:T(8,128)(2,1)S(1)}, u32[]{:S(2)}, u32[]{:S(2)}) %collective-permute-start.3) | collective-permute-done | bytes 65568 | tf_op jit(solution)/shard_map/ppermute | solution.py:415
  35.6 2.7 %collective-permute-done.5 = bf16[4,32,256]{2,1,0:T(8,128)(2,1)S(1)} collective-permute-done((bf16[4,32,256]{2,1,0:T(8,128)(2,1)S(1)}, bf16[4,32,256]{2,1,0:T(8,128)(2,1)S(1)}, u32[]{:S(2)}, u32[]{:S(2)}) %collective-permute-start.5) | collective-permute-done | bytes 65568 | tf_op jit(solution)/shard_map/ppermute | solution.py:415
  38.3 0.9 %collective-permute-done.4 = bf16[4,32,256]{2,1,0:T(8,128)(2,1)S(1)} collective-permute-done((bf16[4,32,256]{2,1,0:T(8,128)(2,1)S(1)}, bf16[4,32,256]{2,1,0:T(8,128)(2,1)S(1)}, u32[]{:S(2)}, u32[]{:S(2)}) %collective-permute-start.4) | collective-permute-done | bytes 65568 | tf_op jit(solution)/shard_map/ppermute | solution.py:415
  39.3 0.1 collective-permute-start.6
  39.4 0.7 %collective-permute-start.8 = (bf16[32,256]{1,0:T(8,128)(2,1)S(1)}, bf16[32,256]{1,0:T(8,128)(2,1)S(1)}, u32[]{:S(2)}, u32[]{:S(2)}) collective-permute-start(bf16[32,256]{1,0:T(8,128)(2,1)S(1)} %get-tuple-element.31), channel_id=1, source_target_pairs={{0,6},{1,7},{2,4},{3,5},{4,2},{5,3},{6,0},{7,1},{8,14},{9,15},{10,... | collective-permute-start | bytes 49160 | tf_op jit(solution)/shard_map/ppermute | solution.py:415
  40.1 2.8 %collective-permute-start.7 = (bf16[32,256]{1,0:T(8,128)(2,1)S(1)}, bf16[32,256]{1,0:T(8,128)(2,1)S(1)}, u32[]{:S(2)}, u32[]{:S(2)}) collective-permute-start(bf16[32,256]{1,0:T(8,128)(2,1)S(1)} %get-tuple-element.32), channel_id=1, source_target_pairs={{0,4},{1,5},{2,6},{3,7},{4,0},{5,1},{6,2},{7,3},{8,12},{9,13},{10,... | collective-permute-start | bytes 49160 | tf_op jit(solution)/shard_map/ppermute | solution.py:415
  42.9 0.4 collective-permute-done.6
  43.3 1.7 %collective-permute-done.8 = bf16[32,256]{1,0:T(8,128)(2,1)S(1)} collective-permute-done((bf16[32,256]{1,0:T(8,128)(2,1)S(1)}, bf16[32,256]{1,0:T(8,128)(2,1)S(1)}, u32[]{:S(2)}, u32[]{:S(2)}) %collective-permute-start.8) | collective-permute-done | bytes 16416 | tf_op jit(solution)/shard_map/ppermute | solution.py:415
  45.0 0.1 reshape.20
  45.1 0.2 copy.6
  45.3 0.7 %reshape.21 = f32[4,16,128]{2,1,0:T(8,128)} reshape(f32[4,16,8,16]{3,2,1,0:T(8,128)S(1)} %copy.6) | data formatting | bytes 65536 | tf_op jit(solution)/shard_map/reshape | solution.py:488
  (6 shorter events, 0.1 us)
Async XLA Ops:
  4.0 17.2 %collective-permute-start = (bf16[198,16,128]{2,1,0:T(8,128)(2,1)S(1)}, bf16[198,16,128]{2,1,0:T(8,128)(2,1)S(1)}, u32[]{:S(2)}, u32[]{:S(2)}) collective-permute-start(bf16[198,16,128]{2,1,0:T(8,128)(2,1)S(1)} %get-tuple-element.20), channel_id=1, source_target_pairs={{0,1},{1,2},{2,3},{3,4},{4,5},{5,6},{6,7},{7,8},{8,9},{9,10},{10,1... | collective-permute-start | bytes 2433032 | tf_op jit(solution)/shard_map/ppermute | solution.py:445
  4.5 16.7 %collective-permute-start.1 = (f32[8,8,128]{2,1,0:T(8,128)S(1)}, f32[8,8,128]{2,1,0:T(8,128)S(1)}, u32[]{:S(2)}, u32[]{:S(2)}) collective-permute-start(f32[8,8,128]{2,1,0:T(8,128)S(1)} %get-tuple-element.19.refs_6_), channel_id=1, source_target_pairs={{1,0},{2,1},{3,2},{4,3},{5,4},{6,5},{7,6},{8,7},{9,8},{10,9},{11,1... | collective-permute-start | bytes 98312 | tf_op jit(solution)/shard_map/ppermute | solution.py:446
  29.6 1.6 %collective-permute-start.2 = (bf16[4,4,32,256]{3,2,1,0:T(8,128)(2,1)S(1)}, bf16[4,4,32,256]{3,2,1,0:T(8,128)(2,1)S(1)}, u32[]{:S(2)}, u32[]{:S(2)}) collective-permute-start(bf16[4,4,32,256]{3,2,1,0:T(8,128)(2,1)S(1)} %get-tuple-element.22), channel_id=1, source_target_pairs={{0,1},{1,0},{2,3},{3,2},{4,5},{5,4},{6,7},{7,6},{8,9},{9,8},{10,11... | collective-permute-start | bytes 786440 | tf_op jit(solution)/shard_map/ppermute | solution.py:415
  31.3 4.3 %collective-permute-start.3 = (bf16[4,32,256]{2,1,0:T(8,128)(2,1)S(1)}, bf16[4,32,256]{2,1,0:T(8,128)(2,1)S(1)}, u32[]{:S(2)}, u32[]{:S(2)}) collective-permute-start(bf16[4,32,256]{2,1,0:T(8,128)(2,1)S(1)} %get-tuple-element.27), channel_id=1, source_target_pairs={{0,8},{1,9},{2,10},{3,11},{4,12},{5,13},{6,14},{7,15},{8,0},{9,1},... | collective-permute-start | bytes 196616 | tf_op jit(solution)/shard_map/ppermute | solution.py:415
  32.3 6.0 %collective-permute-start.5 = (bf16[4,32,256]{2,1,0:T(8,128)(2,1)S(1)}, bf16[4,32,256]{2,1,0:T(8,128)(2,1)S(1)}, u32[]{:S(2)}, u32[]{:S(2)}) collective-permute-start(bf16[4,32,256]{2,1,0:T(8,128)(2,1)S(1)} %get-tuple-element.28), channel_id=1, source_target_pairs={{0,24},{1,25},{2,26},{3,27},{4,28},{5,29},{6,30},{7,31},{8,16},{9,... | collective-permute-start | bytes 196616 | tf_op jit(solution)/shard_map/ppermute | solution.py:415
  34.7 4.5 %collective-permute-start.4 = (bf16[4,32,256]{2,1,0:T(8,128)(2,1)S(1)}, bf16[4,32,256]{2,1,0:T(8,128)(2,1)S(1)}, u32[]{:S(2)}, u32[]{:S(2)}) collective-permute-start(bf16[4,32,256]{2,1,0:T(8,128)(2,1)S(1)} %get-tuple-element.29), channel_id=1, source_target_pairs={{0,16},{1,17},{2,18},{3,19},{4,20},{5,21},{6,22},{7,23},{8,24},{9,... | collective-permute-start | bytes 196616 | tf_op jit(solution)/shard_map/ppermute | solution.py:415
  39.3 4.0 %collective-permute-start.6 = (bf16[32,256]{1,0:T(8,128)(2,1)S(1)}, bf16[32,256]{1,0:T(8,128)(2,1)S(1)}, u32[]{:S(2)}, u32[]{:S(2)}) collective-permute-start(bf16[32,256]{1,0:T(8,128)(2,1)S(1)} %get-tuple-element.30), channel_id=1, source_target_pairs={{0,2},{1,3},{2,0},{3,1},{4,6},{5,7},{6,4},{7,5},{8,10},{9,11},{10,... | collective-permute-start | bytes 49160 | tf_op jit(solution)/shard_map/ppermute | solution.py:415
  39.4 5.6 %collective-permute-start.8 = (bf16[32,256]{1,0:T(8,128)(2,1)S(1)}, bf16[32,256]{1,0:T(8,128)(2,1)S(1)}, u32[]{:S(2)}, u32[]{:S(2)}) collective-permute-start(bf16[32,256]{1,0:T(8,128)(2,1)S(1)} %get-tuple-element.31), channel_id=1, source_target_pairs={{0,6},{1,7},{2,4},{3,5},{4,2},{5,3},{6,0},{7,1},{8,14},{9,15},{10,... | collective-permute-start | bytes 49160 | tf_op jit(solution)/shard_map/ppermute | solution.py:415
  40.1 4.9 %collective-permute-start.7 = (bf16[32,256]{1,0:T(8,128)(2,1)S(1)}, bf16[32,256]{1,0:T(8,128)(2,1)S(1)}, u32[]{:S(2)}, u32[]{:S(2)}) collective-permute-start(bf16[32,256]{1,0:T(8,128)(2,1)S(1)} %get-tuple-element.32), channel_id=1, source_target_pairs={{0,4},{1,5},{2,6},{3,7},{4,0},{5,1},{6,2},{7,3},{8,12},{9,13},{10,... | collective-permute-start | bytes 49160 | tf_op jit(solution)/shard_map/ppermute | solution.py:415

commit v4 on v3

--- a/solution.py
+++ b/solution.py
@@ -8,6 +8,7 @@
 AXES = ("band", "slab")
 LANES = 128
 GROUP = 16
+SUBLANES = 8
 F32 = jnp.float32
 BF16 = jnp.bfloat16
 VMEM = pl.BlockSpec(memory_space=pltpu.VMEM)
@@ -23,6 +24,7 @@
         self.bands, self.comps, self.planes, self.rows, cells = shape
         self.inner = self.planes - 2
         self.tiles = cells // LANES
+        self.pitch = self.tiles + 1
 
 
 def row(ref, s, q, c, x, y):
@@ -117,8 +119,8 @@
 
 
 def transposed(s, source, zt):
-    depth = source.shape[0] // s.tiles
-    return source[pl.ds(zt, depth, stride=s.tiles), :].T.astype(BF16)
+    depth = source.shape[0] // s.pitch
+    return source[pl.ds(zt, depth, stride=s.pitch), :].astype(BF16).T
 
 
 def put(s, target, zt, slot, block):
@@ -128,10 +130,22 @@
 def diagonal_products(s, left, right):
     wide = s.bands * GROUP
     full = lax.dot_general(left, right, (((1,), (1,)), ((), ())), preferred_element_type=F32)
-    full = full.reshape(s.bands, GROUP, wide)
-    cell = lax.broadcasted_iota(jnp.int32, full.shape, 1)
-    lane = lax.broadcasted_iota(jnp.int32, full.shape, 2)
-    return jnp.sum(jnp.where(cell == lane % GROUP, full, 0.0), 1)
+    lane = lax.broadcasted_iota(jnp.int32, (SUBLANES, wide), 1)
+    sublane = lax.broadcasted_iota(jnp.int32, (SUBLANES, wide), 0)
+    upper = lane % GROUP >= SUBLANES
+    skew = (sublane - lane) % SUBLANES
+    blocks = []
+    for first in range(0, s.bands, SUBLANES):
+        mixed = None
+        for k in range(SUBLANES):
+            top = (first + k) * GROUP
+            part = jnp.where(upper, full[top + SUBLANES : top + GROUP], full[top : top + SUBLANES])
+            part = pltpu.roll(part, k, 0) if k else part
+            mixed = part if mixed is None else jnp.where(skew == k, part, mixed)
+        for bit in (1, 2, 4):
+            mixed = jnp.where((lane & bit) != 0, pltpu.roll(mixed, SUBLANES - bit, 0), mixed)
+        blocks.append(mixed)
+    return jnp.concatenate(blocks, 0)
 
 
 def slot_of(s, place, q, n_band):
@@ -151,7 +165,7 @@
 
 
 def set_row(s, ref, entry, value):
-    ref[pl.ds(entry * s.tiles, s.tiles), :] = value
+    ref[pl.ds(entry * s.pitch, s.tiles), :] = value
 
 
 def shift_matrix():
@@ -242,8 +256,8 @@
     matrix[...] = shift_matrix()
     used = local_depth(s)
     for ref in pads:
-        tail = ref.shape[0] - used * s.tiles
-        ref[pl.ds(used * s.tiles, tail), :] = jnp.zeros((tail, LANES), F32)
+        tail = ref.shape[0] - used * s.pitch
+        ref[pl.ds(used * s.pitch, tail), :] = jnp.zeros((tail, LANES), F32)
 
     def shifted(z_ref, q, y):
         values = [row(x_ref, s, q, c, x + 1, y) for x in range(n) for c in range(6)]
@@ -330,18 +344,18 @@
                     value = above_ref[(i - 9) // 2 * n + x] * (-0.25, 0.25, 0.25, -0.25)[i - 9]
                 set_row(s, pads[k], entry, value)
         for zt in range(s.tiles):
-            both = [pads[k][pl.ds(zt, half, stride=s.tiles), :] for k in range(2)]
+            both = [pads[k][pl.ds(zt, half, stride=s.pitch), :] for k in range(2)]
             factors[zt] = jnp.concatenate(both, 0).T.astype(BF16).reshape(LANES // GROUP, GROUP, LANES)
     used = n * 15
     for ref in pads:
-        tail = (half - used) * s.tiles
-        ref[pl.ds(used * s.tiles, tail), :] = jnp.zeros((tail, LANES), F32)
+        tail = (half - used) * s.pitch
+        ref[pl.ds(used * s.pitch, tail), :] = jnp.zeros((tail, LANES), F32)
 
     def turn(sr, sd, q, pairs):
         for t in pairs:
             for source, target, slot in ((sr, rt, slot_of(s, place, q, n_band)), (sd, dt, q)):
-                both = [source[pl.ds(2 * t + k, half, stride=s.tiles), :] for k in range(2)]
-                put(s, target, t, slot, jnp.concatenate(both, 0).T.astype(BF16))
+                both = [source[pl.ds(2 * t + k, half, stride=s.pitch), :] for k in range(2)]
+                put(s, target, t, slot, jnp.concatenate(both, 0).astype(BF16).T)
 
     def band(q, sr, sd, between):
         entry = 0
@@ -453,7 +467,7 @@
         out_specs=(VMEM,) * 4,
         scratch_shapes=[pltpu.VMEM(x.shape, F32), pltpu.SemaphoreType.DMA((s.bands,)), pltpu.VMEM((2 * LANES, 2 * LANES), BF16)]
         + [pltpu.VMEM((rows, n, 6, tiles, LANES), F32)] * 2
-        + [pltpu.VMEM((depth * tiles, LANES), F32)] * 4,
+        + [pltpu.VMEM((depth * s.pitch, LANES), F32)] * 4,
         compiler_params=LOCAL,
         cost_estimate=pl.CostEstimate(flops=2 * 10**9, bytes_accessed=2 * 10**7, transcendentals=0),
     )(place, x, coefs)
@@ -475,7 +489,7 @@
         out_specs=(VMEM, VMEM),
         scratch_shapes=[pltpu.VMEM((n, 10, tiles, LANES), F32), pltpu.VMEM((tiles, groups, GROUP, LANES), BF16)]
         + [pltpu.VMEM((tiles // 2, groups, s.bands, GROUP, LANES), BF16)] * 2
-        + [pltpu.VMEM((LANES // 2 * tiles, LANES), F32)] * 4,
+        + [pltpu.VMEM((LANES // 2 * s.pitch, LANES), F32)] * 4,
         compiler_params=BOUNDARY,
     )(place, local_rt, local_dt, drive, field, coefs, down, from_below, from_above)
 

time: 46.2 us -> 43.7 us (0.946)
  Pallas kernels: 23 us -> 19.5 us
  waiting for transfers between devices: 8.05 us -> 9.03 us
    pallas_call x1, Pallas kernels: 8.3 us -> 6.24 us  [body(): pl.pallas_call(lambda *refs: boundary_kernel(s, n_band, scale, *refs), ou...]
    pallas_call x1, Pallas kernels: 10.6 us -> 9.21 us  [body(): pl.pallas_call(lambda *refs: local_kernel(s, n_band, *refs), out_shape=(t...]
    ppermute x1, waiting for transfers between devices: 0.01 us -> 0.92 us  [body(): from_below = lax.ppermute(up, AXES, step)]
  transfers between devices with their start and end apart: 9 -> 9, of which waited for: 6 -> 7; matrix products, arithmetic and copies ran while one was open for 0% -> 0% of each run, Pallas kernels for 23% -> 21%
where the time goes in v4:
time: 43.7 us; the launch traced here: 43.5 us
  Pallas kernels  19.5 us (45%)
  starting transfers between devices  13.7 us (31%)
  waiting for transfers between devices  9.03 us (21%)
  local copies, waits for them, and re-layouts  1.04 us (2%)
    pallas_call x1, Pallas kernels, body(): pl.pallas_call(lambda *refs: local_kernel(s, n_band, *refs), out_shape=(t...  9.21 us
    ppermute x7, waiting for transfers between devices, exchange(): return lax.ppermute(value, AXES, [(i, i ^ distance) for i in range(size)])  8.11 us
    ppermute x7, starting transfers between devices, exchange(): return lax.ppermute(value, AXES, [(i, i ^ distance) for i in range(size)])  7.17 us
    pallas_call x1, Pallas kernels, body(): pl.pallas_call(lambda *refs: boundary_kernel(s, n_band, scale, *refs), ou...  6.24 us
    ppermute x1, starting transfers between devices, body(): from_above = lax.ppermute(down, AXES, [(j, i) for i, j in step])  5.99 us
    pallas_call x1, Pallas kernels, body(): pl.pallas_call(lambda *refs: edge_kernel(s, *refs), out_shape=(jax.ShapeD...  4.02 us
    ppermute x1, waiting for transfers between devices, body(): from_below = lax.ppermute(up, AXES, step)  0.92 us
  transfers between devices with their start and end apart: 9, of which 7 were waited for; matrix products, arithmetic and copies ran while one was open for 0% of the time, Pallas kernels for 21%

profile of v4, /device:TPU:0, one launch (start us, length us, event | category | flops | bytes accessed | tf_op | source)
XLA Modules:
  0.0 43.5 jit_solution(14619422251276952714)
XLA Ops:
  0.0 4.0 %shard_map.17 = (bf16[198,16,128]{2,1,0:T(8,128)(2,1)S(1)}, f32[8,8,128]{2,1,0:T(8,128)S(1)}, f32[4,4,9,8,128]{4,3,2,1,0:T(8,128)S(1)}) custom-call(f32[16,6,6,32,128]{4,3,2,1,0:T(8,128)} %bitcast.45), custom_call_target="tpu_custom_call" | custom-call | tf_op jit(solution)/shard_map/pallas_call | solution.py:450
  4.0 0.5 %collective-permute-start = (bf16[198,16,128]{2,1,0:T(8,128)(2,1)S(1)}, bf16[198,16,128]{2,1,0:T(8,128)(2,1)S(1)}, u32[]{:S(2)}, u32[]{:S(2)}) collective-permute-start(bf16[198,16,128]{2,1,0:T(8,128)(2,1)S(1)} %get-tuple-element.20), channel_id=1, source_target_pairs={{0,1},{1,2},{2,3},{3,4},{4,5},{5,6},{6,7},{7,8},{8,9},{9,10},{10,1... | collective-permute-start | bytes 2433032 | tf_op jit(solution)/shard_map/ppermute | solution.py:459
  4.5 6.0 %collective-permute-start.1 = (f32[8,8,128]{2,1,0:T(8,128)S(1)}, f32[8,8,128]{2,1,0:T(8,128)S(1)}, u32[]{:S(2)}, u32[]{:S(2)}) collective-permute-start(f32[8,8,128]{2,1,0:T(8,128)S(1)} %get-tuple-element.19.refs_6_), channel_id=1, source_target_pairs={{1,0},{2,1},{3,2},{4,3},{5,4},{6,5},{7,6},{8,7},{9,8},{10,9},{11,1... | collective-permute-start | bytes 98312 | tf_op jit(solution)/shard_map/ppermute | solution.py:460
  10.5 0.1 pad_add_fusion.refs_0_
  10.6 9.2 %shard_map.18 = (bf16[8,8,16,16,128]{4,3,2,1,0:T(8,128)(2,1)S(1)}, bf16[8,8,16,16,128]{4,3,2,1,0:T(8,128)(2,1)S(1)}, f32[16,4,9,8,128]{4,3,2,1,0:T(8,128)S(1)}, f32[16,4,6,8,128]{4,3,2,1,0:T(8,128)S(1)}) custom-call(s32[2]{0:T(128)S(1)} %pad_add_fusion.refs_0_, f32[16,6,6,32,128]{4,3,2,1,0:T(8,128)} %bitcast.46, ...), custom_call_target="tpu_custom_call" | custom-call | flops 2000000000 | bytes 20000000 | tf_op jit(solution)/shard_map/pallas_call | solution.py:463
  19.8 0.9 %collective-permute-done.refs_7_ = bf16[198,16,128]{2,1,0:T(8,128)(2,1)S(1)} collective-permute-done((bf16[198,16,128]{2,1,0:T(8,128)(2,1)S(1)}, bf16[198,16,128]{2,1,0:T(8,128)(2,1)S(1)}, u32[]{:S(2)}, u32[]{:S(2)}) %collective-permute-start) | collective-permute-done | bytes 811040 | tf_op jit(solution)/shard_map/ppermute | solution.py:459
  20.7 6.2 %shard_map.19 = (f32[4,4,32,256]{3,2,1,0:T(8,128)S(1)}, bf16[4,4,32,256]{3,2,1,0:T(8,128)(2,1)S(1)}) custom-call(s32[2]{0:T(128)S(1)} %pad_add_fusion.refs_0_, bf16[8,8,16,16,128]{4,3,2,1,0:T(8,128)(2,1)S(1)} %get-tuple-element.15.refs_1_, bf16[8,8,16,16,128]{4,3,2,1,0:T(8,128)(2,1)S(1)} %get-tuple-element.16.refs_2_, ...), custom_call_target="tpu_custom_call" | custom-call | tf_op jit(solution)/shard_map/pallas_call | solution.py:485
  27.0 0.1 collective-permute-start.2
  27.1 1.5 %collective-permute-done.2 = bf16[4,4,32,256]{3,2,1,0:T(8,128)(2,1)S(1)} collective-permute-done((bf16[4,4,32,256]{3,2,1,0:T(8,128)(2,1)S(1)}, bf16[4,4,32,256]{3,2,1,0:T(8,128)(2,1)S(1)}, u32[]{:S(2)}, u32[]{:S(2)}) %collective-permute-start.2) | collective-permute-done | bytes 262176 | tf_op jit(solution)/shard_map/ppermute | solution.py:429
  28.6 0.1 fusion.8
  28.7 1.1 %collective-permute-start.3 = (bf16[4,32,256]{2,1,0:T(8,128)(2,1)S(1)}, bf16[4,32,256]{2,1,0:T(8,128)(2,1)S(1)}, u32[]{:S(2)}, u32[]{:S(2)}) collective-permute-start(bf16[4,32,256]{2,1,0:T(8,128)(2,1)S(1)} %get-tuple-element.27), channel_id=1, source_target_pairs={{0,8},{1,9},{2,10},{3,11},{4,12},{5,13},{6,14},{7,15},{8,0},{9,1},... | collective-permute-start | bytes 196616 | tf_op jit(solution)/shard_map/ppermute | solution.py:429
  29.8 2.4 %collective-permute-start.5 = (bf16[4,32,256]{2,1,0:T(8,128)(2,1)S(1)}, bf16[4,32,256]{2,1,0:T(8,128)(2,1)S(1)}, u32[]{:S(2)}, u32[]{:S(2)}) collective-permute-start(bf16[4,32,256]{2,1,0:T(8,128)(2,1)S(1)} %get-tuple-element.28), channel_id=1, source_target_pairs={{0,24},{1,25},{2,26},{3,27},{4,28},{5,29},{6,30},{7,31},{8,16},{9,... | collective-permute-start | bytes 196616 | tf_op jit(solution)/shard_map/ppermute | solution.py:429
  32.2 0.1 collective-permute-start.4
  32.3 0.8 %collective-permute-done.3 = bf16[4,32,256]{2,1,0:T(8,128)(2,1)S(1)} collective-permute-done((bf16[4,32,256]{2,1,0:T(8,128)(2,1)S(1)}, bf16[4,32,256]{2,1,0:T(8,128)(2,1)S(1)}, u32[]{:S(2)}, u32[]{:S(2)}) %collective-permute-start.3) | collective-permute-done | bytes 65568 | tf_op jit(solution)/shard_map/ppermute | solution.py:429
  33.1 2.8 %collective-permute-done.5 = bf16[4,32,256]{2,1,0:T(8,128)(2,1)S(1)} collective-permute-done((bf16[4,32,256]{2,1,0:T(8,128)(2,1)S(1)}, bf16[4,32,256]{2,1,0:T(8,128)(2,1)S(1)}, u32[]{:S(2)}, u32[]{:S(2)}) %collective-permute-start.5) | collective-permute-done | bytes 65568 | tf_op jit(solution)/shard_map/ppermute | solution.py:429
  35.8 0.9 %collective-permute-done.4 = bf16[4,32,256]{2,1,0:T(8,128)(2,1)S(1)} collective-permute-done((bf16[4,32,256]{2,1,0:T(8,128)(2,1)S(1)}, bf16[4,32,256]{2,1,0:T(8,128)(2,1)S(1)}, u32[]{:S(2)}, u32[]{:S(2)}) %collective-permute-start.4) | collective-permute-done | bytes 65568 | tf_op jit(solution)/shard_map/ppermute | solution.py:429
  36.8 0.1 collective-permute-start.6
  36.9 0.7 %collective-permute-start.8 = (bf16[32,256]{1,0:T(8,128)(2,1)S(1)}, bf16[32,256]{1,0:T(8,128)(2,1)S(1)}, u32[]{:S(2)}, u32[]{:S(2)}) collective-permute-start(bf16[32,256]{1,0:T(8,128)(2,1)S(1)} %get-tuple-element.31), channel_id=1, source_target_pairs={{0,6},{1,7},{2,4},{3,5},{4,2},{5,3},{6,0},{7,1},{8,14},{9,15},{10,... | collective-permute-start | bytes 49160 | tf_op jit(solution)/shard_map/ppermute | solution.py:429
  37.6 2.8 %collective-permute-start.7 = (bf16[32,256]{1,0:T(8,128)(2,1)S(1)}, bf16[32,256]{1,0:T(8,128)(2,1)S(1)}, u32[]{:S(2)}, u32[]{:S(2)}) collective-permute-start(bf16[32,256]{1,0:T(8,128)(2,1)S(1)} %get-tuple-element.32), channel_id=1, source_target_pairs={{0,4},{1,5},{2,6},{3,7},{4,0},{5,1},{6,2},{7,3},{8,12},{9,13},{10,... | collective-permute-start | bytes 49160 | tf_op jit(solution)/shard_map/ppermute | solution.py:429
  40.3 0.4 collective-permute-done.6
  40.7 1.7 %collective-permute-done.8 = bf16[32,256]{1,0:T(8,128)(2,1)S(1)} collective-permute-done((bf16[32,256]{1,0:T(8,128)(2,1)S(1)}, bf16[32,256]{1,0:T(8,128)(2,1)S(1)}, u32[]{:S(2)}, u32[]{:S(2)}) %collective-permute-start.8) | collective-permute-done | bytes 16416 | tf_op jit(solution)/shard_map/ppermute | solution.py:429
  42.5 0.1 reshape.20
  42.6 0.2 copy.6
  42.8 0.7 %reshape.21 = f32[4,16,128]{2,1,0:T(8,128)} reshape(f32[4,16,8,16]{3,2,1,0:T(8,128)S(1)} %copy.6) | data formatting | bytes 65536 | tf_op jit(solution)/shard_map/reshape | solution.py:502
  (6 shorter events, 0.1 us)
Async XLA Ops:
  4.0 16.7 %collective-permute-start = (bf16[198,16,128]{2,1,0:T(8,128)(2,1)S(1)}, bf16[198,16,128]{2,1,0:T(8,128)(2,1)S(1)}, u32[]{:S(2)}, u32[]{:S(2)}) collective-permute-start(bf16[198,16,128]{2,1,0:T(8,128)(2,1)S(1)} %get-tuple-element.20), channel_id=1, source_target_pairs={{0,1},{1,2},{2,3},{3,4},{4,5},{5,6},{6,7},{7,8},{8,9},{9,10},{10,1... | collective-permute-start | bytes 2433032 | tf_op jit(solution)/shard_map/ppermute | solution.py:459
  4.5 15.3 %collective-permute-start.1 = (f32[8,8,128]{2,1,0:T(8,128)S(1)}, f32[8,8,128]{2,1,0:T(8,128)S(1)}, u32[]{:S(2)}, u32[]{:S(2)}) collective-permute-start(f32[8,8,128]{2,1,0:T(8,128)S(1)} %get-tuple-element.19.refs_6_), channel_id=1, source_target_pairs={{1,0},{2,1},{3,2},{4,3},{5,4},{6,5},{7,6},{8,7},{9,8},{10,9},{11,1... | collective-permute-start | bytes 98312 | tf_op jit(solution)/shard_map/ppermute | solution.py:460
  27.0 1.6 %collective-permute-start.2 = (bf16[4,4,32,256]{3,2,1,0:T(8,128)(2,1)S(1)}, bf16[4,4,32,256]{3,2,1,0:T(8,128)(2,1)S(1)}, u32[]{:S(2)}, u32[]{:S(2)}) collective-permute-start(bf16[4,4,32,256]{3,2,1,0:T(8,128)(2,1)S(1)} %get-tuple-element.22), channel_id=1, source_target_pairs={{0,1},{1,0},{2,3},{3,2},{4,5},{5,4},{6,7},{7,6},{8,9},{9,8},{10,11... | collective-permute-start | bytes 786440 | tf_op jit(solution)/shard_map/ppermute | solution.py:429
  28.7 4.3 %collective-permute-start.3 = (bf16[4,32,256]{2,1,0:T(8,128)(2,1)S(1)}, bf16[4,32,256]{2,1,0:T(8,128)(2,1)S(1)}, u32[]{:S(2)}, u32[]{:S(2)}) collective-permute-start(bf16[4,32,256]{2,1,0:T(8,128)(2,1)S(1)} %get-tuple-element.27), channel_id=1, source_target_pairs={{0,8},{1,9},{2,10},{3,11},{4,12},{5,13},{6,14},{7,15},{8,0},{9,1},... | collective-permute-start | bytes 196616 | tf_op jit(solution)/shard_map/ppermute | solution.py:429
  29.8 6.0 %collective-permute-start.5 = (bf16[4,32,256]{2,1,0:T(8,128)(2,1)S(1)}, bf16[4,32,256]{2,1,0:T(8,128)(2,1)S(1)}, u32[]{:S(2)}, u32[]{:S(2)}) collective-permute-start(bf16[4,32,256]{2,1,0:T(8,128)(2,1)S(1)} %get-tuple-element.28), channel_id=1, source_target_pairs={{0,24},{1,25},{2,26},{3,27},{4,28},{5,29},{6,30},{7,31},{8,16},{9,... | collective-permute-start | bytes 196616 | tf_op jit(solution)/shard_map/ppermute | solution.py:429
  32.2 4.5 %collective-permute-start.4 = (bf16[4,32,256]{2,1,0:T(8,128)(2,1)S(1)}, bf16[4,32,256]{2,1,0:T(8,128)(2,1)S(1)}, u32[]{:S(2)}, u32[]{:S(2)}) collective-permute-start(bf16[4,32,256]{2,1,0:T(8,128)(2,1)S(1)} %get-tuple-element.29), channel_id=1, source_target_pairs={{0,16},{1,17},{2,18},{3,19},{4,20},{5,21},{6,22},{7,23},{8,24},{9,... | collective-permute-start | bytes 196616 | tf_op jit(solution)/shard_map/ppermute | solution.py:429
  36.8 4.0 %collective-permute-start.6 = (bf16[32,256]{1,0:T(8,128)(2,1)S(1)}, bf16[32,256]{1,0:T(8,128)(2,1)S(1)}, u32[]{:S(2)}, u32[]{:S(2)}) collective-permute-start(bf16[32,256]{1,0:T(8,128)(2,1)S(1)} %get-tuple-element.30), channel_id=1, source_target_pairs={{0,2},{1,3},{2,0},{3,1},{4,6},{5,7},{6,4},{7,5},{8,10},{9,11},{10,... | collective-permute-start | bytes 49160 | tf_op jit(solution)/shard_map/ppermute | solution.py:429
  36.9 5.6 %collective-permute-start.8 = (bf16[32,256]{1,0:T(8,128)(2,1)S(1)}, bf16[32,256]{1,0:T(8,128)(2,1)S(1)}, u32[]{:S(2)}, u32[]{:S(2)}) collective-permute-start(bf16[32,256]{1,0:T(8,128)(2,1)S(1)} %get-tuple-element.31), channel_id=1, source_target_pairs={{0,6},{1,7},{2,4},{3,5},{4,2},{5,3},{6,0},{7,1},{8,14},{9,15},{10,... | collective-permute-start | bytes 49160 | tf_op jit(solution)/shard_map/ppermute | solution.py:429
  37.6 4.9 %collective-permute-start.7 = (bf16[32,256]{1,0:T(8,128)(2,1)S(1)}, bf16[32,256]{1,0:T(8,128)(2,1)S(1)}, u32[]{:S(2)}, u32[]{:S(2)}) collective-permute-start(bf16[32,256]{1,0:T(8,128)(2,1)S(1)} %get-tuple-element.32), channel_id=1, source_target_pairs={{0,4},{1,5},{2,6},{3,7},{4,0},{5,1},{6,2},{7,3},{8,12},{9,13},{10,... | collective-permute-start | bytes 49160 | tf_op jit(solution)/shard_map/ppermute | solution.py:429

commit v5 on v4

--- a/solution.py
+++ b/solution.py
@@ -193,13 +193,14 @@
     return out
 
 
-def local_band(s, q, z_ref, x_ref, coefs, drive_ref, field_ref, sr, sd, before, between):
+def local_band(s, q, z_ref, x_ref, coefs, drive_ref, field_ref, sr, sd, before, begin, between):
     n, last = (s.inner, s.rows - 1)
     entry = 0
     for y in range(s.rows):
         before(y)
         behind, here = ([row(x_ref, s, q, c, x, y) for c in range(6)] for x in range(2))
         for x in range(n):
+            held = begin(y * n + x)
             ahead = [row(x_ref, s, q, c, x + 2, y) for c in range(6)]
             f = here
             dx = [p - m for p, m in zip(ahead, behind)]
@@ -241,7 +242,7 @@
                     set_row(s, sd, entry, b)
                     entry += 1
             behind, here = (here, ahead)
-        between(y)
+            between(y * n + x, held)
 
 
 def local_kernel(s, n_band, place, x_hbm, coefs, rt, dt, drive_ref, field_ref, x_ref, sems, matrix, *rest):
@@ -283,11 +284,19 @@
             def before(y):
                 shifted(z_refs[1 - k], ahead, y)
 
-            def between(y):
-                if used:
-                    turn(*other, behind, range(y * s.tiles // s.rows, (y + 1) * s.tiles // s.rows))
-
-            local_band(s, q, z_refs[k], x_ref, coefs, drive_ref, field_ref, *pads[2 * k : 2 * k + 2], before, between)
+            def begin(step):
+                steps = s.rows * n
+                items = range(step * 2 * s.tiles // steps, (step + 1) * 2 * s.tiles // steps if used else 0)
+                return [(item, transposed(s, other[item % 2], item // 2)) for item in items]
+
+            def between(step, held):
+                for item, block in held:
+                    if item % 2:
+                        put(s, dt, item // 2, behind, block)
+                    else:
+                        put(s, rt, item // 2, slot_of(s, place, behind, n_band), block)
+
+            local_band(s, q, z_refs[k], x_ref, coefs, drive_ref, field_ref, *pads[2 * k : 2 * k + 2], before, begin, between)
         return carry
 
     fetch(0).wait()
@@ -309,7 +318,7 @@
     return rows
 
 
-def boundary_kernel(s, n_band, scale, place, local_rt, local_dt, drive_ref, field_ref, coefs, down_ref, up_ref, above_ref, keep_ref, send_ref, tots, factors, rt, dt, *pads):
+def boundary_kernel(s, n_band, scale, place, local_rt, local_dt, drive_ref, field_ref, coefs, down_ref, up_ref, above_ref, send_ref, rt, dt, factors, tots, *pads):
     n = s.inner
     half = LANES // 2
     zero = jnp.zeros((s.tiles, LANES), F32)
@@ -396,33 +405,38 @@
     steps = s.tiles // 2
     lax.fori_loop(0, s.bands // 2, pair, 0)
     turn(*pads[2:4], s.bands - 1, range(steps))
+    products(s, n_band, scale, 1, place, local_rt, local_dt, rt, dt, factors, send_ref)
+
+
+def products(s, n_band, scale, core, place, local_rt, local_dt, rt, dt, factors, out_ref):
     wide = s.bands * GROUP
+    half = LANES // 2
+    share = s.bands // n_band
     lane = lax.broadcasted_iota(jnp.int32, (wide, LANES), 1)
-    share = s.bands // n_band
+    wanted = (lane >= half) == ((core ^ place[1]) % 2 == 1)
 
     def tile(r, carry):
-        for core in range(2):
-            zt = (r * 2 + core) ^ place[1]
-            wanted = (lane >= half) == ((core ^ place[1]) % 2 == 1)
-            parts = []
-            for g in range(LANES // GROUP):
-                left = rt[zt // 2, g].reshape(wide, LANES)
-                left = jnp.where(wanted, left, jnp.zeros_like(left))
-                right = dt[zt // 2, g].reshape(wide, LANES)
-                if s.rows > 1:
-                    scaled = local_rt[zt, g] * factors[zt, g][None]
-                    left = jnp.concatenate([scaled.reshape(wide, -1), left], 1)
-                    right = jnp.concatenate([local_dt[zt, g].reshape(wide, -1), right], 1)
-                parts.append(diagonal_products(s, left, right) * scale)
-            for b in range(n_band):
-                block = jnp.concatenate([p[b * share : (b + 1) * share] for p in parts], 0)
-                if core == 0:
-                    keep_ref[r, b] = block
-                else:
-                    send_ref[r, b] = block.astype(BF16)
+        zt = (r * 2 + core) ^ place[1]
+        parts = []
+        for g in range(LANES // GROUP):
+            left = rt[zt // 2, g].reshape(wide, LANES)
+            left = jnp.where(wanted, left, jnp.zeros_like(left))
+            right = dt[zt // 2, g].reshape(wide, LANES)
+            if s.rows > 1:
+                scaled = local_rt[zt, g] * factors[zt, g][None]
+                left = jnp.concatenate([scaled.reshape(wide, -1), left], 1)
+                right = jnp.concatenate([local_dt[zt, g].reshape(wide, -1), right], 1)
+            parts.append(diagonal_products(s, left, right) * scale)
+        for b in range(n_band):
+            block = jnp.concatenate([p[b * share : (b + 1) * share] for p in parts], 0)
+            out_ref[r, b] = block.astype(out_ref.dtype)
         return carry
 
-    lax.fori_loop(0, s.tiles // 2, tile, 0)
+    lax.fori_loop(0, s.tiles // 2, tile, 0, unroll=4)
+
+
+def farthest_first(size):
+    return sorted(range(1, size), key=lambda d: (-d.bit_count(), d))
 
 
 def exchange(value, distance, size):
@@ -482,21 +496,29 @@
 
     shape = (tiles // 2, n_band, groups * share, wide)
     scale = 1.0 / (n * rows * devices)
-    keep, send = pl.pallas_call(
+    blocks = jax.ShapeDtypeStruct((tiles // 2, groups, s.bands, GROUP, LANES), BF16)
+    send, rt, dt, factors = pl.pallas_call(
         lambda *refs: boundary_kernel(s, n_band, scale, *refs),
-        out_shape=(jax.ShapeDtypeStruct(shape, F32), jax.ShapeDtypeStruct(shape, BF16)),
+        out_shape=(jax.ShapeDtypeStruct(shape, BF16), blocks, blocks, jax.ShapeDtypeStruct((tiles, groups, GROUP, LANES), BF16)),
         in_specs=[SMEM] + [VMEM] * 8,
-        out_specs=(VMEM, VMEM),
-        scratch_shapes=[pltpu.VMEM((n, 10, tiles, LANES), F32), pltpu.VMEM((tiles, groups, GROUP, LANES), BF16)]
-        + [pltpu.VMEM((tiles // 2, groups, s.bands, GROUP, LANES), BF16)] * 2
-        + [pltpu.VMEM((LANES // 2 * s.pitch, LANES), F32)] * 4,
+        out_specs=(VMEM,) * 4,
+        scratch_shapes=[pltpu.VMEM((n, 10, tiles, LANES), F32)] + [pltpu.VMEM((LANES // 2 * s.pitch, LANES), F32)] * 4,
         compiler_params=BOUNDARY,
     )(place, local_rt, local_dt, drive, field, coefs, down, from_below, from_above)
-
-    value = keep + exchange(send, 1, devices).astype(F32)
-    parts = [exchange(value[:, d].astype(BF16), d * n_slab, devices) for d in range(1, n_band)]
+    arrived = exchange(send, 1, devices)
+    keep = pl.pallas_call(
+        lambda place, *refs: products(s, n_band, scale, 0, place, *refs),
+        out_shape=jax.ShapeDtypeStruct(shape, F32),
+        in_specs=[SMEM] + [VMEM] * 5,
+        out_specs=VMEM,
+        compiler_params=BOUNDARY,
+        cost_estimate=pl.CostEstimate(flops=2 * 10**9, bytes_accessed=2 * 10**7, transcendentals=0),
+    )(place, local_rt, local_dt, rt, dt, factors)
+
+    value = keep + arrived.astype(F32)
+    parts = [exchange(value[:, d].astype(BF16), d * n_slab, devices) for d in farthest_first(n_band)]
     value = sum([p.astype(F32) for p in parts], value[:, 0])
-    parts = [exchange(value[e].astype(BF16), 2 * e, devices) for e in range(1, tiles // 2)]
+    parts = [exchange(value[e].astype(BF16), 2 * e, devices) for e in range(tiles // 2 - 1, 0, -1)]
     value = sum([p.astype(F32) for p in parts], value[0])
     value = value.reshape(groups, share, s.bands, GROUP).transpose(1, 2, 0, 3)
     return value.reshape(share, s.bands, groups * GROUP)

time: 43.7 us -> 42 us (0.961)
  waiting for transfers between devices: 9.03 us -> 6.41 us
  starting transfers between devices: 13.7 us -> 14.6 us
    ppermute x7, waiting for transfers between devices: 8.11 us -> 5.49 us  [exchange(): return lax.ppermute(value, AXES, [(i, i ^ distance) for i in range(size)])]
    pallas_call x0 -> x1, Pallas kernels: none -> 1.92 us  [body(): pl.pallas_call(lambda place, *refs: products(s, n_band, scale, 0, place,...]
    pallas_call x1, Pallas kernels: 6.24 us -> 4.4 us  [body(): pl.pallas_call(lambda *refs: boundary_kernel(s, n_band, scale, *refs), ou...]
    ppermute x7, starting transfers between devices: 7.17 us -> 8.08 us  [exchange(): return lax.ppermute(value, AXES, [(i, i ^ distance) for i in range(size)])]
  transfers between devices with their start and end apart: 9 -> 9, of which waited for: 7 -> 6; matrix products, arithmetic and copies ran while one was open for 0% -> 0% of each run, Pallas kernels for 21% -> 27%
where the time goes in v5:
time: 42 us; the launch traced here: 41.9 us
  Pallas kernels  19.5 us (46%)
  starting transfers between devices  14.6 us (35%)
  waiting for transfers between devices  6.41 us (15%)
  local copies, waits for them, and re-layouts  1.04 us (2%)
    pallas_call x1, Pallas kernels, body(): pl.pallas_call(lambda *refs: local_kernel(s, n_band, *refs), out_shape=(t...  9.21 us
    ppermute x7, starting transfers between devices, exchange(): return lax.ppermute(value, AXES, [(i, i ^ distance) for i in range(size)])  8.08 us
    ppermute x1, starting transfers between devices, body(): from_above = lax.ppermute(down, AXES, [(j, i) for i, j in step])  5.99 us
    ppermute x7, waiting for transfers between devices, exchange(): return lax.ppermute(value, AXES, [(i, i ^ distance) for i in range(size)])  5.49 us
    pallas_call x1, Pallas kernels, body(): pl.pallas_call(lambda *refs: boundary_kernel(s, n_band, scale, *refs), ou...  4.4 us
    pallas_call x1, Pallas kernels, body(): pl.pallas_call(lambda *refs: edge_kernel(s, *refs), out_shape=(jax.ShapeD...  4.02 us
    pallas_call x1, Pallas kernels, body(): pl.pallas_call(lambda place, *refs: products(s, n_band, scale, 0, place,...  1.92 us
    ppermute x1, waiting for transfers between devices, body(): from_below = lax.ppermute(up, AXES, step)  0.92 us
  transfers between devices with their start and end apart: 9, of which 6 were waited for; matrix products, arithmetic and copies ran while one was open for 0% of the time, Pallas kernels for 27%

profile of v5, /device:TPU:0, one launch (start us, length us, event | category | flops | bytes accessed | tf_op | source)
XLA Modules:
  0.0 41.9 jit_solution(2268483150567722120)
XLA Ops:
  0.0 4.0 %shard_map.17 = (bf16[198,16,128]{2,1,0:T(8,128)(2,1)S(1)}, f32[8,8,128]{2,1,0:T(8,128)S(1)}, f32[4,4,9,8,128]{4,3,2,1,0:T(8,128)S(1)}) custom-call(f32[16,6,6,32,128]{4,3,2,1,0:T(8,128)} %bitcast.45), custom_call_target="tpu_custom_call" | custom-call | tf_op jit(solution)/shard_map/pallas_call | solution.py:464
  4.0 0.5 %collective-permute-start = (bf16[198,16,128]{2,1,0:T(8,128)(2,1)S(1)}, bf16[198,16,128]{2,1,0:T(8,128)(2,1)S(1)}, u32[]{:S(2)}, u32[]{:S(2)}) collective-permute-start(bf16[198,16,128]{2,1,0:T(8,128)(2,1)S(1)} %get-tuple-element.22), channel_id=1, source_target_pairs={{0,1},{1,2},{2,3},{3,4},{4,5},{5,6},{6,7},{7,8},{8,9},{9,10},{10,1... | collective-permute-start | bytes 2433032 | tf_op jit(solution)/shard_map/ppermute | solution.py:473
  4.5 6.0 %collective-permute-start.1 = (f32[8,8,128]{2,1,0:T(8,128)S(1)}, f32[8,8,128]{2,1,0:T(8,128)S(1)}, u32[]{:S(2)}, u32[]{:S(2)}) collective-permute-start(f32[8,8,128]{2,1,0:T(8,128)S(1)} %get-tuple-element.21.refs_6_), channel_id=1, source_target_pairs={{1,0},{2,1},{3,2},{4,3},{5,4},{6,5},{7,6},{8,7},{9,8},{10,9},{11,1... | collective-permute-start | bytes 98312 | tf_op jit(solution)/shard_map/ppermute | solution.py:474
  10.5 0.1 pad_add_fusion.refs_0_.place
  10.6 9.2 %shard_map.18 = (bf16[8,8,16,16,128]{4,3,2,1,0:T(8,128)(2,1)S(1)}, bf16[8,8,16,16,128]{4,3,2,1,0:T(8,128)(2,1)S(1)}, f32[16,4,9,8,128]{4,3,2,1,0:T(8,128)S(1)}, f32[16,4,6,8,128]{4,3,2,1,0:T(8,128)S(1)}) custom-call(s32[2]{0:T(128)S(1)} %pad_add_fusion.refs_0_.place, f32[16,6,6,32,128]{4,3,2,1,0:T(8,128)} %bitcast.46, ...), custom_call_target="tpu_custom_call" | custom-call | flops 2000000000 | bytes 20000000 | tf_op jit(solution)/shard_map/pallas_call | solution.py:477
  19.8 0.0 collective-permute-done.1.refs_8_
  19.8 0.9 %collective-permute-done.refs_7_ = bf16[198,16,128]{2,1,0:T(8,128)(2,1)S(1)} collective-permute-done((bf16[198,16,128]{2,1,0:T(8,128)(2,1)S(1)}, bf16[198,16,128]{2,1,0:T(8,128)(2,1)S(1)}, u32[]{:S(2)}, u32[]{:S(2)}) %collective-permute-start) | collective-permute-done | bytes 811040 | tf_op jit(solution)/shard_map/ppermute | solution.py:473
  20.7 4.4 %shard_map.19 = (bf16[4,4,32,256]{3,2,1,0:T(8,128)(2,1)S(1)}, bf16[4,8,16,16,128]{4,3,2,1,0:T(8,128)(2,1)S(1)}, bf16[4,8,16,16,128]{4,3,2,1,0:T(8,128)(2,1)S(1)}, bf16[8,8,16,128]{3,2,1,0:T(8,128)(2,1)S(1)}) custom-call(s32[2]{0:T(128)S(1)} %pad_add_fusion.refs_0_.place, bf16[8,8,16,16,128]{4,3,2,1,0:T(8,128)(2,1)S(1)} %get-tuple-element.17.refs_1_.refs_0_, ...), custom_call_target="tpu_custom_call" | custom-call | tf_op jit(solution)/shard_map/pallas_call | solution.py:500
  25.2 0.1 collective-permute-start.2
  25.2 1.9 %shard_map.20 = f32[4,4,32,256]{3,2,1,0:T(8,128)S(1)} custom-call(s32[2]{0:T(128)S(1)} %pad_add_fusion.refs_0_.place, bf16[8,8,16,16,128]{4,3,2,1,0:T(8,128)(2,1)S(1)} %get-tuple-element.17.refs_1_.refs_0_, bf16[8,8,16,16,128]{4,3,2,1,0:T(8,128)(2,1)S(1)} %get-tuple-element.18.refs_2_.refs_1_, bf16[4,8,16,16,128]{4,3,2,1,0:T(8,128)(2,1)S(1)} %get-tuple-element.23.refs_2_, ...), custom_call_target="tpu_custom_call" | custom-call | flops 2000000000 | bytes 20000000 | tf_op jit(solution)/shard_map/pallas_call | solution.py:509
  27.2 0.1 fusion.8
  27.3 2.0 %collective-permute-start.3 = (bf16[4,32,256]{2,1,0:T(8,128)(2,1)S(1)}, bf16[4,32,256]{2,1,0:T(8,128)(2,1)S(1)}, u32[]{:S(2)}, u32[]{:S(2)}) collective-permute-start(bf16[4,32,256]{2,1,0:T(8,128)(2,1)S(1)} %get-tuple-element.31), channel_id=1, source_target_pairs={{0,24},{1,25},{2,26},{3,27},{4,28},{5,29},{6,30},{7,31},{8,16},{9,... | collective-permute-start | bytes 196616 | tf_op jit(solution)/shard_map/ppermute | solution.py:443
  29.3 0.5 %collective-permute-start.5 = (bf16[4,32,256]{2,1,0:T(8,128)(2,1)S(1)}, bf16[4,32,256]{2,1,0:T(8,128)(2,1)S(1)}, u32[]{:S(2)}, u32[]{:S(2)}) collective-permute-start(bf16[4,32,256]{2,1,0:T(8,128)(2,1)S(1)} %get-tuple-element.32), channel_id=1, source_target_pairs={{0,16},{1,17},{2,18},{3,19},{4,20},{5,21},{6,22},{7,23},{8,24},{9,... | collective-permute-start | bytes 196616 | tf_op jit(solution)/shard_map/ppermute | solution.py:443
  29.8 1.0 %collective-permute-start.4 = (bf16[4,32,256]{2,1,0:T(8,128)(2,1)S(1)}, bf16[4,32,256]{2,1,0:T(8,128)(2,1)S(1)}, u32[]{:S(2)}, u32[]{:S(2)}) collective-permute-start(bf16[4,32,256]{2,1,0:T(8,128)(2,1)S(1)} %get-tuple-element.33), channel_id=1, source_target_pairs={{0,8},{1,9},{2,10},{3,11},{4,12},{5,13},{6,14},{7,15},{8,0},{9,1},... | collective-permute-start | bytes 196616 | tf_op jit(solution)/shard_map/ppermute | solution.py:443
  30.8 2.0 %collective-permute-done.3 = bf16[4,32,256]{2,1,0:T(8,128)(2,1)S(1)} collective-permute-done((bf16[4,32,256]{2,1,0:T(8,128)(2,1)S(1)}, bf16[4,32,256]{2,1,0:T(8,128)(2,1)S(1)}, u32[]{:S(2)}, u32[]{:S(2)}) %collective-permute-start.3) | collective-permute-done | bytes 65568 | tf_op jit(solution)/shard_map/ppermute | solution.py:443
  32.8 1.3 %collective-permute-done.5 = bf16[4,32,256]{2,1,0:T(8,128)(2,1)S(1)} collective-permute-done((bf16[4,32,256]{2,1,0:T(8,128)(2,1)S(1)}, bf16[4,32,256]{2,1,0:T(8,128)(2,1)S(1)}, u32[]{:S(2)}, u32[]{:S(2)}) %collective-permute-start.5) | collective-permute-done | bytes 65568 | tf_op jit(solution)/shard_map/ppermute | solution.py:443
  34.2 0.5 %collective-permute-done.4 = bf16[4,32,256]{2,1,0:T(8,128)(2,1)S(1)} collective-permute-done((bf16[4,32,256]{2,1,0:T(8,128)(2,1)S(1)}, bf16[4,32,256]{2,1,0:T(8,128)(2,1)S(1)}, u32[]{:S(2)}, u32[]{:S(2)}) %collective-permute-start.4) | collective-permute-done | bytes 65568 | tf_op jit(solution)/shard_map/ppermute | solution.py:443
  34.7 0.4 %collective-permute-start.6 = (bf16[32,256]{1,0:T(8,128)(2,1)S(1)}, bf16[32,256]{1,0:T(8,128)(2,1)S(1)}, u32[]{:S(2)}, u32[]{:S(2)}) collective-permute-start(bf16[32,256]{1,0:T(8,128)(2,1)S(1)} %get-tuple-element.34), channel_id=1, source_target_pairs={{0,6},{1,7},{2,4},{3,5},{4,2},{5,3},{6,0},{7,1},{8,14},{9,15},{10,... | collective-permute-start | bytes 49160 | tf_op jit(solution)/shard_map/ppermute | solution.py:443
  35.1 4.0 %collective-permute-start.7 = (bf16[32,256]{1,0:T(8,128)(2,1)S(1)}, bf16[32,256]{1,0:T(8,128)(2,1)S(1)}, u32[]{:S(2)}, u32[]{:S(2)}) collective-permute-start(bf16[32,256]{1,0:T(8,128)(2,1)S(1)} %get-tuple-element.36), channel_id=1, source_target_pairs={{0,4},{1,5},{2,6},{3,7},{4,0},{5,1},{6,2},{7,3},{8,12},{9,13},{10,... | collective-permute-start | bytes 49160 | tf_op jit(solution)/shard_map/ppermute | solution.py:443
  39.1 1.1 %collective-permute-done.6 = bf16[32,256]{1,0:T(8,128)(2,1)S(1)} collective-permute-done((bf16[32,256]{1,0:T(8,128)(2,1)S(1)}, bf16[32,256]{1,0:T(8,128)(2,1)S(1)}, u32[]{:S(2)}, u32[]{:S(2)}) %collective-permute-start.6) | collective-permute-done | bytes 16416 | tf_op jit(solution)/shard_map/ppermute | solution.py:443
  40.3 0.6 %collective-permute-done.7 = bf16[32,256]{1,0:T(8,128)(2,1)S(1)} collective-permute-done((bf16[32,256]{1,0:T(8,128)(2,1)S(1)}, bf16[32,256]{1,0:T(8,128)(2,1)S(1)}, u32[]{:S(2)}, u32[]{:S(2)}) %collective-permute-start.7) | collective-permute-done | bytes 16416 | tf_op jit(solution)/shard_map/ppermute | solution.py:443
  40.9 0.1 reshape.20
  41.0 0.2 copy.6
  41.1 0.7 %reshape.21 = f32[4,16,128]{2,1,0:T(8,128)} reshape(f32[4,16,8,16]{3,2,1,0:T(8,128)S(1)} %copy.6) | data formatting | bytes 65536 | tf_op jit(solution)/shard_map/reshape | solution.py:524
  (7 shorter events, 0.1 us)
Async XLA Ops:
  4.0 16.7 %collective-permute-start = (bf16[198,16,128]{2,1,0:T(8,128)(2,1)S(1)}, bf16[198,16,128]{2,1,0:T(8,128)(2,1)S(1)}, u32[]{:S(2)}, u32[]{:S(2)}) collective-permute-start(bf16[198,16,128]{2,1,0:T(8,128)(2,1)S(1)} %get-tuple-element.22), channel_id=1, source_target_pairs={{0,1},{1,2},{2,3},{3,4},{4,5},{5,6},{6,7},{7,8},{8,9},{9,10},{10,1... | collective-permute-start | bytes 2433032 | tf_op jit(solution)/shard_map/ppermute | solution.py:473
  4.5 15.3 %collective-permute-start.1 = (f32[8,8,128]{2,1,0:T(8,128)S(1)}, f32[8,8,128]{2,1,0:T(8,128)S(1)}, u32[]{:S(2)}, u32[]{:S(2)}) collective-permute-start(f32[8,8,128]{2,1,0:T(8,128)S(1)} %get-tuple-element.21.refs_6_), channel_id=1, source_target_pairs={{1,0},{2,1},{3,2},{4,3},{5,4},{6,5},{7,6},{8,7},{9,8},{10,9},{11,1... | collective-permute-start | bytes 98312 | tf_op jit(solution)/shard_map/ppermute | solution.py:474
  25.2 2.0 %collective-permute-start.2 = (bf16[4,4,32,256]{3,2,1,0:T(8,128)(2,1)S(1)}, bf16[4,4,32,256]{3,2,1,0:T(8,128)(2,1)S(1)}, u32[]{:S(2)}, u32[]{:S(2)}) collective-permute-start(bf16[4,4,32,256]{3,2,1,0:T(8,128)(2,1)S(1)} %get-tuple-element.26), channel_id=1, source_target_pairs={{0,1},{1,0},{2,3},{3,2},{4,5},{5,4},{6,7},{7,6},{8,9},{9,8},{10,11... | collective-permute-start | bytes 786440 | tf_op jit(solution)/shard_map/ppermute | solution.py:443
  27.3 5.5 %collective-permute-start.3 = (bf16[4,32,256]{2,1,0:T(8,128)(2,1)S(1)}, bf16[4,32,256]{2,1,0:T(8,128)(2,1)S(1)}, u32[]{:S(2)}, u32[]{:S(2)}) collective-permute-start(bf16[4,32,256]{2,1,0:T(8,128)(2,1)S(1)} %get-tuple-element.31), channel_id=1, source_target_pairs={{0,24},{1,25},{2,26},{3,27},{4,28},{5,29},{6,30},{7,31},{8,16},{9,... | collective-permute-start | bytes 196616 | tf_op jit(solution)/shard_map/ppermute | solution.py:443
  29.3 4.8 %collective-permute-start.5 = (bf16[4,32,256]{2,1,0:T(8,128)(2,1)S(1)}, bf16[4,32,256]{2,1,0:T(8,128)(2,1)S(1)}, u32[]{:S(2)}, u32[]{:S(2)}) collective-permute-start(bf16[4,32,256]{2,1,0:T(8,128)(2,1)S(1)} %get-tuple-element.32), channel_id=1, source_target_pairs={{0,16},{1,17},{2,18},{3,19},{4,20},{5,21},{6,22},{7,23},{8,24},{9,... | collective-permute-start | bytes 196616 | tf_op jit(solution)/shard_map/ppermute | solution.py:443
  29.8 4.8 %collective-permute-start.4 = (bf16[4,32,256]{2,1,0:T(8,128)(2,1)S(1)}, bf16[4,32,256]{2,1,0:T(8,128)(2,1)S(1)}, u32[]{:S(2)}, u32[]{:S(2)}) collective-permute-start(bf16[4,32,256]{2,1,0:T(8,128)(2,1)S(1)} %get-tuple-element.33), channel_id=1, source_target_pairs={{0,8},{1,9},{2,10},{3,11},{4,12},{5,13},{6,14},{7,15},{8,0},{9,1},... | collective-permute-start | bytes 196616 | tf_op jit(solution)/shard_map/ppermute | solution.py:443
  34.7 5.6 %collective-permute-start.6 = (bf16[32,256]{1,0:T(8,128)(2,1)S(1)}, bf16[32,256]{1,0:T(8,128)(2,1)S(1)}, u32[]{:S(2)}, u32[]{:S(2)}) collective-permute-start(bf16[32,256]{1,0:T(8,128)(2,1)S(1)} %get-tuple-element.34), channel_id=1, source_target_pairs={{0,6},{1,7},{2,4},{3,5},{4,2},{5,3},{6,0},{7,1},{8,14},{9,15},{10,... | collective-permute-start | bytes 49160 | tf_op jit(solution)/shard_map/ppermute | solution.py:443
  35.1 5.2 %collective-permute-start.8 = (bf16[32,256]{1,0:T(8,128)(2,1)S(1)}, bf16[32,256]{1,0:T(8,128)(2,1)S(1)}, u32[]{:S(2)}, u32[]{:S(2)}) collective-permute-start(bf16[32,256]{1,0:T(8,128)(2,1)S(1)} %get-tuple-element.35), channel_id=1, source_target_pairs={{0,2},{1,3},{2,0},{3,1},{4,6},{5,7},{6,4},{7,5},{8,10},{9,11},{10,... | collective-permute-start | bytes 49160 | tf_op jit(solution)/shard_map/ppermute | solution.py:443
  35.1 5.7 %collective-permute-start.7 = (bf16[32,256]{1,0:T(8,128)(2,1)S(1)}, bf16[32,256]{1,0:T(8,128)(2,1)S(1)}, u32[]{:S(2)}, u32[]{:S(2)}) collective-permute-start(bf16[32,256]{1,0:T(8,128)(2,1)S(1)} %get-tuple-element.36), channel_id=1, source_target_pairs={{0,4},{1,5},{2,6},{3,7},{4,0},{5,1},{6,2},{7,3},{8,12},{9,13},{10,... | collective-permute-start | bytes 49160 | tf_op jit(solution)/shard_map/ppermute | solution.py:443

commit v6 on v5

--- a/solution.py
+++ b/solution.py
@@ -310,6 +310,18 @@
         dt[...] = jnp.zeros_like(dt)
 
 
+def factor_kernel(s, above_ref, factors, held):
+    n = s.inner
+    for entry in range(LANES):
+        x, i = divmod(entry - (s.rows - 2) * n * 9, 13)
+        value = jnp.ones((s.tiles, LANES), F32)
+        if 0 <= x < n and i >= 9:
+            value = above_ref[(i - 9) // 2 * n + x] * (-0.25, 0.25, 0.25, -0.25)[i - 9]
+        set_row(s, held, entry, value)
+    for zt in range(s.tiles):
+        factors[zt] = transposed(s, held, zt).reshape(LANES // GROUP, GROUP, LANES)
+
+
 def halo_pair(s, up_ref, index):
     rows = []
     for p in range(s.inner // 2):
@@ -318,7 +330,7 @@
     return rows
 
 
-def boundary_kernel(s, n_band, scale, place, local_rt, local_dt, drive_ref, field_ref, coefs, down_ref, up_ref, above_ref, send_ref, rt, dt, factors, tots, *pads):
+def boundary_kernel(s, n_band, scale, place, local_rt, local_dt, drive_ref, field_ref, coefs, down_ref, up_ref, above_ref, factors, send_ref, rt, dt, tots, *pads):
     n = s.inner
     half = LANES // 2
     zero = jnp.zeros((s.tiles, LANES), F32)
@@ -343,33 +355,25 @@
         for c in range(3):
             tots[x, 4 + c] = j[c] * -0.5
             tots[x, 7 + c] = behind[c] * -0.5
-    if s.rows > 1:
-        for k in range(2):
-            for entry in range(half):
-                e = k * half + entry - (s.rows - 2) * n * 9
-                x, i = divmod(e, 13)
-                value = jnp.ones((s.tiles, LANES), F32)
-                if 0 <= x < n and i >= 9:
-                    value = above_ref[(i - 9) // 2 * n + x] * (-0.25, 0.25, 0.25, -0.25)[i - 9]
-                set_row(s, pads[k], entry, value)
-        for zt in range(s.tiles):
-            both = [pads[k][pl.ds(zt, half, stride=s.pitch), :] for k in range(2)]
-            factors[zt] = jnp.concatenate(both, 0).T.astype(BF16).reshape(LANES // GROUP, GROUP, LANES)
     used = n * 15
     for ref in pads:
         tail = (half - used) * s.pitch
         ref[pl.ds(used * s.pitch, tail), :] = jnp.zeros((tail, LANES), F32)
 
+    def turned(source, t):
+        both = [source[pl.ds(2 * t + k, half, stride=s.pitch), :] for k in range(2)]
+        return jnp.concatenate(both, 0).astype(BF16).T
+
     def turn(sr, sd, q, pairs):
         for t in pairs:
-            for source, target, slot in ((sr, rt, slot_of(s, place, q, n_band)), (sd, dt, q)):
-                both = [source[pl.ds(2 * t + k, half, stride=s.pitch), :] for k in range(2)]
-                put(s, target, t, slot, jnp.concatenate(both, 0).astype(BF16).T)
-
-    def band(q, sr, sd, between):
+            put(s, rt, t, slot_of(s, place, q, n_band), turned(sr, t))
+            put(s, dt, t, q, turned(sd, t))
+
+    def band(q, sr, sd, begin, between):
         entry = 0
         h_all = [halo_pair(s, up_ref, q * s.comps + c) for c in range(6)]
         for x in range(n):
+            held = begin(x)
             f = [field_ref[q, x, c] for c in range(6)]
             h = [h_all[c][x] for c in range(6)]
             da, dc, ea, ec = ([], [], [], [])
@@ -392,14 +396,23 @@
                 set_row(s, sr, entry, a)
                 set_row(s, sd, entry, b)
                 entry += 1
-            between(x)
+            between(held)
 
     def pair(p, carry):
         for k in range(2):
             q = 2 * p + k
             before = lax.rem(q + s.bands - 1, s.bands)
             other = pads[2 - 2 * k : 4 - 2 * k]
-            band(q, *pads[2 * k : 2 * k + 2], lambda x: turn(*other, before, range(x * steps // n, (x + 1) * steps // n)))
+
+            def begin(x):
+                return [(t, turned(other[0], t), turned(other[1], t)) for t in range(x * steps // n, (x + 1) * steps // n)]
+
+            def between(held):
+                for t, left, right in held:
+                    put(s, rt, t, slot_of(s, place, before, n_band), left)
+                    put(s, dt, t, before, right)
+
+            band(q, *pads[2 * k : 2 * k + 2], begin, between)
         return carry
 
     steps = s.tiles // 2
@@ -497,14 +510,22 @@
     shape = (tiles // 2, n_band, groups * share, wide)
     scale = 1.0 / (n * rows * devices)
     blocks = jax.ShapeDtypeStruct((tiles // 2, groups, s.bands, GROUP, LANES), BF16)
-    send, rt, dt, factors = pl.pallas_call(
+    factors = pl.pallas_call(
+        lambda *refs: factor_kernel(s, *refs),
+        out_shape=jax.ShapeDtypeStruct((tiles, groups, GROUP, LANES), BF16),
+        in_specs=[VMEM],
+        out_specs=VMEM,
+        scratch_shapes=[pltpu.VMEM((LANES * s.pitch, LANES), F32)],
+        compiler_params=BOUNDARY,
+    )(from_above)
+    send, rt, dt = pl.pallas_call(
         lambda *refs: boundary_kernel(s, n_band, scale, *refs),
-        out_shape=(jax.ShapeDtypeStruct(shape, BF16), blocks, blocks, jax.ShapeDtypeStruct((tiles, groups, GROUP, LANES), BF16)),
-        in_specs=[SMEM] + [VMEM] * 8,
-        out_specs=(VMEM,) * 4,
+        out_shape=(jax.ShapeDtypeStruct(shape, BF16), blocks, blocks),
+        in_specs=[SMEM] + [VMEM] * 9,
+        out_specs=(VMEM,) * 3,
         scratch_shapes=[pltpu.VMEM((n, 10, tiles, LANES), F32)] + [pltpu.VMEM((LANES // 2 * s.pitch, LANES), F32)] * 4,
         compiler_params=BOUNDARY,
-    )(place, local_rt, local_dt, drive, field, coefs, down, from_below, from_above)
+    )(place, local_rt, local_dt, drive, field, coefs, down, from_below, from_above, factors)
     arrived = exchange(send, 1, devices)
     keep = pl.pallas_call(
         lambda place, *refs: products(s, n_band, scale, 0, place, *refs),
@@ -518,7 +539,7 @@
     value = keep + arrived.astype(F32)
     parts = [exchange(value[:, d].astype(BF16), d * n_slab, devices) for d in farthest_first(n_band)]
     value = sum([p.astype(F32) for p in parts], value[:, 0])
-    parts = [exchange(value[e].astype(BF16), 2 * e, devices) for e in range(tiles // 2 - 1, 0, -1)]
+    parts = [exchange(value[e].astype(BF16), 2 * e, devices) for e in range(1, tiles // 2)]
     value = sum([p.astype(F32) for p in parts], value[0])
     value = value.reshape(groups, share, s.bands, GROUP).transpose(1, 2, 0, 3)
     return value.reshape(share, s.bands, groups * GROUP)

time: 42 us -> 41.4 us (0.986)
  starting transfers between devices: 14.6 us -> 13.7 us
    ppermute x7, starting transfers between devices: 8.08 us -> 7.17 us  [exchange(): return lax.ppermute(value, AXES, [(i, i ^ distance) for i in range(size)])]
    ppermute x7, waiting for transfers between devices: 5.49 us -> 5.93 us  [exchange(): return lax.ppermute(value, AXES, [(i, i ^ distance) for i in range(size)])]
where the time goes in v6:
time: 41.4 us; the launch traced here: 41.3 us
  Pallas kernels  19.6 us (47%)
  starting transfers between devices  13.7 us (33%)
  waiting for transfers between devices  6.68 us (16%)
  local copies, waits for them, and re-layouts  1.04 us (3%)
    pallas_call x1, Pallas kernels, body(): pl.pallas_call(lambda *refs: local_kernel(s, n_band, *refs), out_shape=(t...  9.21 us
    ppermute x7, starting transfers between devices, exchange(): return lax.ppermute(value, AXES, [(i, i ^ distance) for i in range(size)])  7.17 us
    ppermute x1, starting transfers between devices, body(): from_above = lax.ppermute(down, AXES, [(j, i) for i, j in step])  5.99 us
    ppermute x7, waiting for transfers between devices, exchange(): return lax.ppermute(value, AXES, [(i, i ^ distance) for i in range(size)])  5.93 us
    pallas_call x1, Pallas kernels, body(): pl.pallas_call(lambda *refs: boundary_kernel(s, n_band, scale, *refs), ou...  4.25 us
    pallas_call x1, Pallas kernels, body(): pl.pallas_call(lambda *refs: edge_kernel(s, *refs), out_shape=(jax.ShapeD...  4.02 us
    pallas_call x1, Pallas kernels, body(): pl.pallas_call(lambda place, *refs: products(s, n_band, scale, 0, place,...  1.94 us
  transfers between devices with their start and end apart: 9, of which 6 were waited for; matrix products, arithmetic and copies ran while one was open for 0% of the time, Pallas kernels for 27%

profile of v6, /device:TPU:0, one launch (start us, length us, event | category | flops | bytes accessed | tf_op | source)
XLA Modules:
  0.0 41.3 jit_solution(7596826152137391379)
XLA Ops:
  0.0 4.0 %shard_map.17 = (bf16[198,16,128]{2,1,0:T(8,128)(2,1)S(1)}, f32[8,8,128]{2,1,0:T(8,128)S(1)}, f32[4,4,9,8,128]{4,3,2,1,0:T(8,128)S(1)}) custom-call(f32[16,6,6,32,128]{4,3,2,1,0:T(8,128)} %bitcast.45), custom_call_target="tpu_custom_call" | custom-call | tf_op jit(solution)/shard_map/pallas_call | solution.py:477
  4.0 0.5 %collective-permute-start = (bf16[198,16,128]{2,1,0:T(8,128)(2,1)S(1)}, bf16[198,16,128]{2,1,0:T(8,128)(2,1)S(1)}, u32[]{:S(2)}, u32[]{:S(2)}) collective-permute-start(bf16[198,16,128]{2,1,0:T(8,128)(2,1)S(1)} %get-tuple-element.21), channel_id=1, source_target_pairs={{0,1},{1,2},{2,3},{3,4},{4,5},{5,6},{6,7},{7,8},{8,9},{9,10},{10,1... | collective-permute-start | bytes 2433032 | tf_op jit(solution)/shard_map/ppermute | solution.py:486
  4.5 6.0 %collective-permute-start.1 = (f32[8,8,128]{2,1,0:T(8,128)S(1)}, f32[8,8,128]{2,1,0:T(8,128)S(1)}, u32[]{:S(2)}, u32[]{:S(2)}) collective-permute-start(f32[8,8,128]{2,1,0:T(8,128)S(1)} %get-tuple-element.20.refs_6_), channel_id=1, source_target_pairs={{1,0},{2,1},{3,2},{4,3},{5,4},{6,5},{7,6},{8,7},{9,8},{10,9},{11,1... | collective-permute-start | bytes 98312 | tf_op jit(solution)/shard_map/ppermute | solution.py:487
  10.5 0.1 pad_add_fusion.refs_0_.place
  10.6 9.2 %shard_map.18 = (bf16[8,8,16,16,128]{4,3,2,1,0:T(8,128)(2,1)S(1)}, bf16[8,8,16,16,128]{4,3,2,1,0:T(8,128)(2,1)S(1)}, f32[16,4,9,8,128]{4,3,2,1,0:T(8,128)S(1)}, f32[16,4,6,8,128]{4,3,2,1,0:T(8,128)S(1)}) custom-call(s32[2]{0:T(128)S(1)} %pad_add_fusion.refs_0_.place, f32[16,6,6,32,128]{4,3,2,1,0:T(8,128)} %bitcast.46, ...), custom_call_target="tpu_custom_call" | custom-call | flops 2000000000 | bytes 20000000 | tf_op jit(solution)/shard_map/pallas_call | solution.py:490
  19.8 0.2 shard_map.19.refs_9_.refs_4_
  20.0 0.8 %collective-permute-done.refs_7_ = bf16[198,16,128]{2,1,0:T(8,128)(2,1)S(1)} collective-permute-done((bf16[198,16,128]{2,1,0:T(8,128)(2,1)S(1)}, bf16[198,16,128]{2,1,0:T(8,128)(2,1)S(1)}, u32[]{:S(2)}, u32[]{:S(2)}) %collective-permute-start) | collective-permute-done | bytes 811040 | tf_op jit(solution)/shard_map/ppermute | solution.py:486
  20.7 4.2 %shard_map.20 = (bf16[4,4,32,256]{3,2,1,0:T(8,128)(2,1)S(1)}, bf16[4,8,16,16,128]{4,3,2,1,0:T(8,128)(2,1)S(1)}, bf16[4,8,16,16,128]{4,3,2,1,0:T(8,128)(2,1)S(1)}) custom-call(s32[2]{0:T(128)S(1)} %pad_add_fusion.refs_0_.place, bf16[8,8,16,16,128]{4,3,2,1,0:T(8,128)(2,1)S(1)} %get-tuple-element.16.refs_1_.refs_0_, ...), custom_call_target="tpu_custom_call" | custom-call | tf_op jit(solution)/shard_map/pallas_call | solution.py:521
  25.0 0.1 collective-permute-start.2
  25.1 1.9 %shard_map.21 = f32[4,4,32,256]{3,2,1,0:T(8,128)S(1)} custom-call(s32[2]{0:T(128)S(1)} %pad_add_fusion.refs_0_.place, bf16[8,8,16,16,128]{4,3,2,1,0:T(8,128)(2,1)S(1)} %get-tuple-element.16.refs_1_.refs_0_, bf16[8,8,16,16,128]{4,3,2,1,0:T(8,128)(2,1)S(1)} %get-tuple-element.17.refs_2_.refs_1_, bf16[4,8,16,16,128]{4,3,2,1,0:T(8,128)(2,1)S(1)} %get-tuple-element.22.refs_2_, ...), custom_call_target="tpu_custom_call" | custom-call | flops 2000000000 | bytes 20000000 | tf_op jit(solution)/shard_map/pallas_call | solution.py:530
  27.0 0.1 fusion.8
  27.2 2.0 %collective-permute-start.3 = (bf16[4,32,256]{2,1,0:T(8,128)(2,1)S(1)}, bf16[4,32,256]{2,1,0:T(8,128)(2,1)S(1)}, u32[]{:S(2)}, u32[]{:S(2)}) collective-permute-start(bf16[4,32,256]{2,1,0:T(8,128)(2,1)S(1)} %get-tuple-element.29), channel_id=1, source_target_pairs={{0,24},{1,25},{2,26},{3,27},{4,28},{5,29},{6,30},{7,31},{8,16},{9,... | collective-permute-start | bytes 196616 | tf_op jit(solution)/shard_map/ppermute | solution.py:456
  29.2 0.5 %collective-permute-start.5 = (bf16[4,32,256]{2,1,0:T(8,128)(2,1)S(1)}, bf16[4,32,256]{2,1,0:T(8,128)(2,1)S(1)}, u32[]{:S(2)}, u32[]{:S(2)}) collective-permute-start(bf16[4,32,256]{2,1,0:T(8,128)(2,1)S(1)} %get-tuple-element.30), channel_id=1, source_target_pairs={{0,16},{1,17},{2,18},{3,19},{4,20},{5,21},{6,22},{7,23},{8,24},{9,... | collective-permute-start | bytes 196616 | tf_op jit(solution)/shard_map/ppermute | solution.py:456
  29.7 1.0 %collective-permute-start.4 = (bf16[4,32,256]{2,1,0:T(8,128)(2,1)S(1)}, bf16[4,32,256]{2,1,0:T(8,128)(2,1)S(1)}, u32[]{:S(2)}, u32[]{:S(2)}) collective-permute-start(bf16[4,32,256]{2,1,0:T(8,128)(2,1)S(1)} %get-tuple-element.31), channel_id=1, source_target_pairs={{0,8},{1,9},{2,10},{3,11},{4,12},{5,13},{6,14},{7,15},{8,0},{9,1},... | collective-permute-start | bytes 196616 | tf_op jit(solution)/shard_map/ppermute | solution.py:456
  30.7 2.0 %collective-permute-done.3 = bf16[4,32,256]{2,1,0:T(8,128)(2,1)S(1)} collective-permute-done((bf16[4,32,256]{2,1,0:T(8,128)(2,1)S(1)}, bf16[4,32,256]{2,1,0:T(8,128)(2,1)S(1)}, u32[]{:S(2)}, u32[]{:S(2)}) %collective-permute-start.3) | collective-permute-done | bytes 65568 | tf_op jit(solution)/shard_map/ppermute | solution.py:456
  32.7 1.3 %collective-permute-done.5 = bf16[4,32,256]{2,1,0:T(8,128)(2,1)S(1)} collective-permute-done((bf16[4,32,256]{2,1,0:T(8,128)(2,1)S(1)}, bf16[4,32,256]{2,1,0:T(8,128)(2,1)S(1)}, u32[]{:S(2)}, u32[]{:S(2)}) %collective-permute-start.5) | collective-permute-done | bytes 65568 | tf_op jit(solution)/shard_map/ppermute | solution.py:456
  34.0 0.5 %collective-permute-done.4 = bf16[4,32,256]{2,1,0:T(8,128)(2,1)S(1)} collective-permute-done((bf16[4,32,256]{2,1,0:T(8,128)(2,1)S(1)}, bf16[4,32,256]{2,1,0:T(8,128)(2,1)S(1)}, u32[]{:S(2)}, u32[]{:S(2)}) %collective-permute-start.4) | collective-permute-done | bytes 65568 | tf_op jit(solution)/shard_map/ppermute | solution.py:456
  34.6 0.8 %collective-permute-start.8 = (bf16[32,256]{1,0:T(8,128)(2,1)S(1)}, bf16[32,256]{1,0:T(8,128)(2,1)S(1)}, u32[]{:S(2)}, u32[]{:S(2)}) collective-permute-start(bf16[32,256]{1,0:T(8,128)(2,1)S(1)} %get-tuple-element.33), channel_id=1, source_target_pairs={{0,6},{1,7},{2,4},{3,5},{4,2},{5,3},{6,0},{7,1},{8,14},{9,15},{10,... | collective-permute-start | bytes 49160 | tf_op jit(solution)/shard_map/ppermute | solution.py:456
  35.4 2.7 %collective-permute-start.7 = (bf16[32,256]{1,0:T(8,128)(2,1)S(1)}, bf16[32,256]{1,0:T(8,128)(2,1)S(1)}, u32[]{:S(2)}, u32[]{:S(2)}) collective-permute-start(bf16[32,256]{1,0:T(8,128)(2,1)S(1)} %get-tuple-element.34), channel_id=1, source_target_pairs={{0,4},{1,5},{2,6},{3,7},{4,0},{5,1},{6,2},{7,3},{8,12},{9,13},{10,... | collective-permute-start | bytes 49160 | tf_op jit(solution)/shard_map/ppermute | solution.py:456
  38.1 0.3 collective-permute-done.6
  38.4 1.9 %collective-permute-done.8 = bf16[32,256]{1,0:T(8,128)(2,1)S(1)} collective-permute-done((bf16[32,256]{1,0:T(8,128)(2,1)S(1)}, bf16[32,256]{1,0:T(8,128)(2,1)S(1)}, u32[]{:S(2)}, u32[]{:S(2)}) %collective-permute-start.8) | collective-permute-done | bytes 16416 | tf_op jit(solution)/shard_map/ppermute | solution.py:456
  40.3 0.1 reshape.20
  40.4 0.2 copy.6
  40.6 0.7 %reshape.21 = f32[4,16,128]{2,1,0:T(8,128)} reshape(f32[4,16,8,16]{3,2,1,0:T(8,128)S(1)} %copy.6) | data formatting | bytes 65536 | tf_op jit(solution)/shard_map/reshape | solution.py:545
  (8 shorter events, 0.1 us)
Async XLA Ops:
  4.0 16.7 %collective-permute-start = (bf16[198,16,128]{2,1,0:T(8,128)(2,1)S(1)}, bf16[198,16,128]{2,1,0:T(8,128)(2,1)S(1)}, u32[]{:S(2)}, u32[]{:S(2)}) collective-permute-start(bf16[198,16,128]{2,1,0:T(8,128)(2,1)S(1)} %get-tuple-element.21), channel_id=1, source_target_pairs={{0,1},{1,2},{2,3},{3,4},{4,5},{5,6},{6,7},{7,8},{8,9},{9,10},{10,1... | collective-permute-start | bytes 2433032 | tf_op jit(solution)/shard_map/ppermute | solution.py:486
  4.5 15.3 %collective-permute-start.1 = (f32[8,8,128]{2,1,0:T(8,128)S(1)}, f32[8,8,128]{2,1,0:T(8,128)S(1)}, u32[]{:S(2)}, u32[]{:S(2)}) collective-permute-start(f32[8,8,128]{2,1,0:T(8,128)S(1)} %get-tuple-element.20.refs_6_), channel_id=1, source_target_pairs={{1,0},{2,1},{3,2},{4,3},{5,4},{6,5},{7,6},{8,7},{9,8},{10,9},{11,1... | collective-permute-start | bytes 98312 | tf_op jit(solution)/shard_map/ppermute | solution.py:487
  25.0 2.0 %collective-permute-start.2 = (bf16[4,4,32,256]{3,2,1,0:T(8,128)(2,1)S(1)}, bf16[4,4,32,256]{3,2,1,0:T(8,128)(2,1)S(1)}, u32[]{:S(2)}, u32[]{:S(2)}) collective-permute-start(bf16[4,4,32,256]{3,2,1,0:T(8,128)(2,1)S(1)} %get-tuple-element.24), channel_id=1, source_target_pairs={{0,1},{1,0},{2,3},{3,2},{4,5},{5,4},{6,7},{7,6},{8,9},{9,8},{10,11... | collective-permute-start | bytes 786440 | tf_op jit(solution)/shard_map/ppermute | solution.py:456
  27.2 5.5 %collective-permute-start.3 = (bf16[4,32,256]{2,1,0:T(8,128)(2,1)S(1)}, bf16[4,32,256]{2,1,0:T(8,128)(2,1)S(1)}, u32[]{:S(2)}, u32[]{:S(2)}) collective-permute-start(bf16[4,32,256]{2,1,0:T(8,128)(2,1)S(1)} %get-tuple-element.29), channel_id=1, source_target_pairs={{0,24},{1,25},{2,26},{3,27},{4,28},{5,29},{6,30},{7,31},{8,16},{9,... | collective-permute-start | bytes 196616 | tf_op jit(solution)/shard_map/ppermute | solution.py:456
  29.2 4.8 %collective-permute-start.5 = (bf16[4,32,256]{2,1,0:T(8,128)(2,1)S(1)}, bf16[4,32,256]{2,1,0:T(8,128)(2,1)S(1)}, u32[]{:S(2)}, u32[]{:S(2)}) collective-permute-start(bf16[4,32,256]{2,1,0:T(8,128)(2,1)S(1)} %get-tuple-element.30), channel_id=1, source_target_pairs={{0,16},{1,17},{2,18},{3,19},{4,20},{5,21},{6,22},{7,23},{8,24},{9,... | collective-permute-start | bytes 196616 | tf_op jit(solution)/shard_map/ppermute | solution.py:456
  29.7 4.8 %collective-permute-start.4 = (bf16[4,32,256]{2,1,0:T(8,128)(2,1)S(1)}, bf16[4,32,256]{2,1,0:T(8,128)(2,1)S(1)}, u32[]{:S(2)}, u32[]{:S(2)}) collective-permute-start(bf16[4,32,256]{2,1,0:T(8,128)(2,1)S(1)} %get-tuple-element.31), channel_id=1, source_target_pairs={{0,8},{1,9},{2,10},{3,11},{4,12},{5,13},{6,14},{7,15},{8,0},{9,1},... | collective-permute-start | bytes 196616 | tf_op jit(solution)/shard_map/ppermute | solution.py:456
  34.5 3.8 %collective-permute-start.6 = (bf16[32,256]{1,0:T(8,128)(2,1)S(1)}, bf16[32,256]{1,0:T(8,128)(2,1)S(1)}, u32[]{:S(2)}, u32[]{:S(2)}) collective-permute-start(bf16[32,256]{1,0:T(8,128)(2,1)S(1)} %get-tuple-element.32), channel_id=1, source_target_pairs={{0,2},{1,3},{2,0},{3,1},{4,6},{5,7},{6,4},{7,5},{8,10},{9,11},{10,... | collective-permute-start | bytes 49160 | tf_op jit(solution)/shard_map/ppermute | solution.py:456
  34.6 5.6 %collective-permute-start.8 = (bf16[32,256]{1,0:T(8,128)(2,1)S(1)}, bf16[32,256]{1,0:T(8,128)(2,1)S(1)}, u32[]{:S(2)}, u32[]{:S(2)}) collective-permute-start(bf16[32,256]{1,0:T(8,128)(2,1)S(1)} %get-tuple-element.33), channel_id=1, source_target_pairs={{0,6},{1,7},{2,4},{3,5},{4,2},{5,3},{6,0},{7,1},{8,14},{9,15},{10,... | collective-permute-start | bytes 49160 | tf_op jit(solution)/shard_map/ppermute | solution.py:456
  35.4 4.8 %collective-permute-start.7 = (bf16[32,256]{1,0:T(8,128)(2,1)S(1)}, bf16[32,256]{1,0:T(8,128)(2,1)S(1)}, u32[]{:S(2)}, u32[]{:S(2)}) collective-permute-start(bf16[32,256]{1,0:T(8,128)(2,1)S(1)} %get-tuple-element.34), channel_id=1, source_target_pairs={{0,4},{1,5},{2,6},{3,7},{4,0},{5,1},{6,2},{7,3},{8,12},{9,13},{10,... | collective-permute-start | bytes 49160 | tf_op jit(solution)/shard_map/ppermute | solution.py:456

commit v7 on v6

--- a/solution.py
+++ b/solution.py
@@ -27,6 +27,9 @@
         self.pitch = self.tiles + 1
 
 
+TOTALS = (1, 4, 3, 5)
+
+
 def row(ref, s, q, c, x, y):
     if s.rows == 1:
         return ref[q, c, x]
@@ -43,7 +46,7 @@
     return after - before
 
 
-def edge_kernel(s, x_hbm, up_ref, down_ref, coefs, x_ref, sums, sems):
+def edge_kernel(s, x_hbm, up_ref, rest_ref, down_ref, coefs, x_ref, sums, sems):
     last = s.rows - 1
     n = s.inner
     whole, inside = (pl.ds(4, 2), pl.ds(0, 4))
@@ -55,12 +58,17 @@
     for copy in copies:
         copy.start()
 
-    def band(q, carry):
-        for c in range(s.comps):
-            for p in range(n // 2):
-                pair = [row(x_ref, s, q, c, 1 + 2 * p + k, last) for k in range(2)]
-                up_ref[(q * s.comps + c) * (n // 2) + p] = jnp.concatenate(pair, 0).astype(BF16)
-        return carry
+    def pack(first, count):
+        target, start = (up_ref, 0) if first < s.bands // 2 else (rest_ref, s.bands // 2)
+
+        def band(q, carry):
+            for c in range(s.comps):
+                for p in range(n // 2):
+                    pair = [row(x_ref, s, q, c, 1 + 2 * p + k, last) for k in range(2)]
+                    target[((q - start) * s.comps + c) * (n // 2) + p] = jnp.concatenate(pair, 0).astype(BF16)
+            return carry
+
+        lax.fori_loop(first, first + count, band, 0)
 
     def total_of(first, count, c, x):
         for y in range(s.rows):
@@ -86,9 +94,9 @@
     for first in range(0, s.bands, share):
         for copy in copies[2 * first : 2 * (first + share)]:
             copy.wait()
-        lax.fori_loop(first, first + share, band, 0)
+        pack(first, share)
         add(first, share)
-    currents = [[], [], []]
+    extras = [[], [], []] + [[sums[c, x + 1, last] for x in range(n)] for c in TOTALS]
     for x in range(n):
         down_ref[x] = sums[3, x + 1, 0]
         down_ref[n + x] = sums[5, x + 1, 0]
@@ -111,11 +119,11 @@
                 coefs[x, y, 3 + d] = (v[d] + b[d]) * -0.25
                 coefs[x, y, 6 + d] = j[d]
                 if y == last:
-                    currents[d].append(j[d])
-    base = s.bands * s.comps * (n // 2)
-    for c in range(3):
+                    extras[d].append(j[d])
+    base = s.bands // 2 * s.comps * (n // 2)
+    for c, values in enumerate(extras):
         for p in range(n // 2):
-            up_ref[base + c * (n // 2) + p] = jnp.concatenate(currents[c][2 * p : 2 * p + 2], 0).astype(BF16)
+            up_ref[base + c * (n // 2) + p] = jnp.concatenate(values[2 * p : 2 * p + 2], 0).astype(BF16)
 
 
 def transposed(s, source, zt):
@@ -146,11 +154,6 @@
             mixed = jnp.where((lane & bit) != 0, pltpu.roll(mixed, SUBLANES - bit, 0), mixed)
         blocks.append(mixed)
     return jnp.concatenate(blocks, 0)
-
-
-def slot_of(s, place, q, n_band):
-    share = s.bands // n_band
-    return (q // share ^ place[0]) * share + q % share
 
 
 def cross(a, b):
@@ -245,7 +248,7 @@
             between(y * n + x, held)
 
 
-def local_kernel(s, n_band, place, x_hbm, coefs, rt, dt, drive_ref, field_ref, x_ref, sems, matrix, *rest):
+def local_kernel(s, x_hbm, coefs, rt, dt, drive_ref, field_ref, x_ref, sems, matrix, *rest):
     n = s.inner
     z_refs, pads = (rest[:2], rest[2:])
 
@@ -267,7 +270,7 @@
 
     def turn(sr, sd, q, tiles):
         for zt in tiles:
-            put(s, rt, zt, slot_of(s, place, q, n_band), transposed(s, sr, zt))
+            put(s, rt, zt, q, transposed(s, sr, zt))
             put(s, dt, zt, q, transposed(s, sd, zt))
 
     def pair(p, carry):
@@ -294,7 +297,7 @@
                     if item % 2:
                         put(s, dt, item // 2, behind, block)
                     else:
-                        put(s, rt, item // 2, slot_of(s, place, behind, n_band), block)
+                        put(s, rt, item // 2, behind, block)
 
             local_band(s, q, z_refs[k], x_ref, coefs, drive_ref, field_ref, *pads[2 * k : 2 * k + 2], before, begin, between)
         return carry
@@ -330,20 +333,13 @@
     return rows
 
 
-def boundary_kernel(s, n_band, scale, place, local_rt, local_dt, drive_ref, field_ref, coefs, down_ref, up_ref, above_ref, factors, send_ref, rt, dt, tots, *pads):
+def first_kernel(s, drive_ref, field_ref, coefs, down_ref, up_ref, above_ref, rt, dt, tots, *pads):
     n = s.inner
-    half = LANES // 2
-    zero = jnp.zeros((s.tiles, LANES), F32)
-    kinds = (1, 4, 3, 5)
-
-    def add(q, totals):
-        rows = sum([halo_pair(s, up_ref, q * s.comps + c) for c in kinds], [])
-        return [t + r for t, r in zip(totals, rows)]
-
-    totals = lax.fori_loop(0, s.bands, add, [zero] * (4 * n))
-    behinds = [halo_pair(s, up_ref, s.bands * s.comps + c) for c in range(3)]
+    base = s.bands // 2 * s.comps
+    behinds = [halo_pair(s, up_ref, base + c) for c in range(3)]
+    totals = [halo_pair(s, up_ref, base + 3 + k) for k in range(len(TOTALS))]
     for x in range(n):
-        vy, my, bx, bz = (totals[k * n + x] for k in range(4))
+        vy, my, bx, bz = (total[x] for total in totals)
         tots[x, 0] = coefs[x, 0, 1]
         tots[x, 1] = coefs[x, 0, 4]
         tots[x, 2] = (vy - my) * -0.25
@@ -355,6 +351,18 @@
         for c in range(3):
             tots[x, 4 + c] = j[c] * -0.5
             tots[x, 7 + c] = behind[c] * -0.5
+    boundary_bands(s, 0, drive_ref, field_ref, up_ref, tots, rt, dt, pads)
+
+
+def second_kernel(s, n_band, scale, place, local_rt, local_dt, drive_ref, field_ref, up_ref, tots, factors, rt_0, dt_0, send_ref, rt, dt, *pads):
+    boundary_bands(s, s.bands // 2, drive_ref, field_ref, up_ref, tots, rt, dt, pads)
+    products(s, n_band, scale, 1, place, local_rt, local_dt, factors, rt_0, dt_0, rt, dt, send_ref)
+
+
+def boundary_bands(s, first, drive_ref, field_ref, up_ref, tots, rt, dt, pads):
+    n = s.inner
+    count = s.bands // 2
+    half = LANES // 2
     used = n * 15
     for ref in pads:
         tail = (half - used) * s.pitch
@@ -366,22 +374,23 @@
 
     def turn(sr, sd, q, pairs):
         for t in pairs:
-            put(s, rt, t, slot_of(s, place, q, n_band), turned(sr, t))
+            put(s, rt, t, q, turned(sr, t))
             put(s, dt, t, q, turned(sd, t))
 
     def band(q, sr, sd, begin, between):
         entry = 0
         h_all = [halo_pair(s, up_ref, q * s.comps + c) for c in range(6)]
+        k = first + q
         for x in range(n):
             held = begin(x)
-            f = [field_ref[q, x, c] for c in range(6)]
+            f = [field_ref[k, x, c] for c in range(6)]
             h = [h_all[c][x] for c in range(6)]
             da, dc, ea, ec = ([], [], [], [])
             for c in range(3):
                 p = tots[x, 0] * (h[c] + h[c + 3])
                 m = tots[x, 1] * (h[c] - h[c + 3])
-                da.append(drive_ref[q, x, c] - (p + m))
-                dc.append(drive_ref[q, x, 3 + c] - (p - m))
+                da.append(drive_ref[k, x, c] - (p + m))
+                dc.append(drive_ref[k, x, 3 + c] - (p - m))
                 p = tots[x, 2] * (f[c] + f[c + 3])
                 m = tots[x, 3] * (f[c] - f[c + 3])
                 ea.append(p + m)
@@ -389,7 +398,7 @@
             behind = cross([tots[x, 7 + c] for c in range(3)], h[3:6])
             dc[0] = dc[0] - behind[2] * 0.5
             dc[2] = dc[2] + behind[0] * 0.5
-            j = [drive_ref[q, x, 6] - h[5] * 0.5, drive_ref[q, x, 7], drive_ref[q, x, 8] + h[3] * 0.5]
+            j = [drive_ref[k, x, 6] - h[5] * 0.5, drive_ref[k, x, 7], drive_ref[k, x, 8] + h[3] * 0.5]
             left = f + j + h
             right = da + dc + cross([tots[x, 4 + c] for c in range(3)], f[3:6]) + ea + ec
             for a, b in zip(left, right):
@@ -401,7 +410,7 @@
     def pair(p, carry):
         for k in range(2):
             q = 2 * p + k
-            before = lax.rem(q + s.bands - 1, s.bands)
+            before = lax.rem(q + count - 1, count)
             other = pads[2 - 2 * k : 4 - 2 * k]
 
             def begin(x):
@@ -409,19 +418,18 @@
 
             def between(held):
                 for t, left, right in held:
-                    put(s, rt, t, slot_of(s, place, before, n_band), left)
+                    put(s, rt, t, before, left)
                     put(s, dt, t, before, right)
 
             band(q, *pads[2 * k : 2 * k + 2], begin, between)
         return carry
 
     steps = s.tiles // 2
-    lax.fori_loop(0, s.bands // 2, pair, 0)
-    turn(*pads[2:4], s.bands - 1, range(steps))
-    products(s, n_band, scale, 1, place, local_rt, local_dt, rt, dt, factors, send_ref)
-
-
-def products(s, n_band, scale, core, place, local_rt, local_dt, rt, dt, factors, out_ref):
+    lax.fori_loop(0, count // 2, pair, 0)
+    turn(*pads[2:4], count - 1, range(steps))
+
+
+def products(s, n_band, scale, core, place, local_rt, local_dt, factors, rt_0, dt_0, rt_1, dt_1, out_ref):
     wide = s.bands * GROUP
     half = LANES // 2
     share = s.bands // n_band
@@ -432,9 +440,9 @@
         zt = (r * 2 + core) ^ place[1]
         parts = []
         for g in range(LANES // GROUP):
-            left = rt[zt // 2, g].reshape(wide, LANES)
+            left = jnp.concatenate([ref[zt // 2, g].reshape(wide // 2, LANES) for ref in (rt_0, rt_1)], 0)
             left = jnp.where(wanted, left, jnp.zeros_like(left))
-            right = dt[zt // 2, g].reshape(wide, LANES)
+            right = jnp.concatenate([ref[zt // 2, g].reshape(wide // 2, LANES) for ref in (dt_0, dt_1)], 0)
             if s.rows > 1:
                 scaled = local_rt[zt, g] * factors[zt, g][None]
                 left = jnp.concatenate([scaled.reshape(wide, -1), left], 1)
@@ -442,7 +450,7 @@
             parts.append(diagonal_products(s, left, right) * scale)
         for b in range(n_band):
             block = jnp.concatenate([p[b * share : (b + 1) * share] for p in parts], 0)
-            out_ref[r, b] = block.astype(out_ref.dtype)
+            out_ref[r, b ^ place[0]] = block.astype(out_ref.dtype)
         return carry
 
     lax.fori_loop(0, s.tiles // 2, tile, 0, unroll=4)
@@ -472,44 +480,48 @@
     groups = LANES // GROUP
     wide = s.bands * GROUP
     share = s.bands // n_band
-    rows_up = (s.bands * s.comps + 3) * (n // 2)
-
-    up, down, coefs = pl.pallas_call(
+    rows_up = s.bands // 2 * s.comps * (n // 2)
+    rows_first = rows_up + (3 + len(TOTALS)) * (n // 2)
+
+    up, rest, down, coefs = pl.pallas_call(
         lambda *refs: edge_kernel(s, *refs),
-        out_shape=(jax.ShapeDtypeStruct((rows_up, 2 * tiles, LANES), BF16), vector(2 * n), vector(n, rows, 9)),
+        out_shape=tuple(jax.ShapeDtypeStruct((count, 2 * tiles, LANES), BF16) for count in (rows_first, rows_up)) + (vector(2 * n), vector(n, rows, 9)),
         in_specs=[HBM],
-        out_specs=(VMEM,) * 3,
+        out_specs=(VMEM,) * 4,
         scratch_shapes=[pltpu.VMEM(x.shape, F32), pltpu.VMEM((s.comps, s.planes, rows, tiles, LANES), F32), pltpu.SemaphoreType.DMA((s.bands, 2))],
         compiler_params=EDGE,
     )(x)
     step = [(i, (i + 1) % devices) for i in range(devices)]
     from_below = lax.ppermute(up, AXES, step)
+    rest_below = lax.ppermute(rest, AXES, step)
     from_above = lax.ppermute(down, AXES, [(j, i) for i, j in step])
 
     turned = jax.ShapeDtypeStruct((tiles, groups, s.bands, GROUP, depth), BF16)
     local_rt, local_dt, drive, field = pl.pallas_call(
-        lambda *refs: local_kernel(s, n_band, *refs),
+        lambda *refs: local_kernel(s, *refs),
         out_shape=(turned, turned, vector(s.bands, n, 9), vector(s.bands, n, 6)),
-        in_specs=[SMEM, HBM, VMEM],
+        in_specs=[HBM, VMEM],
         out_specs=(VMEM,) * 4,
         scratch_shapes=[pltpu.VMEM(x.shape, F32), pltpu.SemaphoreType.DMA((s.bands,)), pltpu.VMEM((2 * LANES, 2 * LANES), BF16)]
         + [pltpu.VMEM((rows, n, 6, tiles, LANES), F32)] * 2
         + [pltpu.VMEM((depth * s.pitch, LANES), F32)] * 4,
         compiler_params=LOCAL,
         cost_estimate=pl.CostEstimate(flops=2 * 10**9, bytes_accessed=2 * 10**7, transcendentals=0),
-    )(place, x, coefs)
+    )(x, coefs)
     if rows == 1:
         two = lax.ppermute(down, AXES, [(i, (i + 2) % devices) for i in range(devices)])
         two = two.reshape(2, n // 2, 2 * tiles, LANES) * 0.5
-        base = s.bands * s.comps * (n // 2)
-        behind = from_below[base:].astype(F32).reshape(3, n // 2, 2 * tiles, LANES)
+        base = rows_up
+        end = base + 3 * (n // 2)
+        behind = from_below[base:end].astype(F32).reshape(3, n // 2, 2 * tiles, LANES)
         behind = jnp.stack([behind[0] - two[1], behind[1], behind[2] + two[0]])
         behind = behind.reshape(3 * (n // 2), 2 * tiles, LANES).astype(BF16)
-        from_below = jnp.concatenate([from_below[:base], behind], 0)
+        from_below = jnp.concatenate([from_below[:base], behind, from_below[end:]], 0)
 
     shape = (tiles // 2, n_band, groups * share, wide)
     scale = 1.0 / (n * rows * devices)
-    blocks = jax.ShapeDtypeStruct((tiles // 2, groups, s.bands, GROUP, LANES), BF16)
+    blocks = jax.ShapeDtypeStruct((tiles // 2, groups, s.bands // 2, GROUP, LANES), BF16)
+    staging = [pltpu.VMEM((LANES // 2 * s.pitch, LANES), F32)] * 4
     factors = pl.pallas_call(
         lambda *refs: factor_kernel(s, *refs),
         out_shape=jax.ShapeDtypeStruct((tiles, groups, GROUP, LANES), BF16),
@@ -518,23 +530,31 @@
         scratch_shapes=[pltpu.VMEM((LANES * s.pitch, LANES), F32)],
         compiler_params=BOUNDARY,
     )(from_above)
-    send, rt, dt = pl.pallas_call(
-        lambda *refs: boundary_kernel(s, n_band, scale, *refs),
+    rt_0, dt_0, tots = pl.pallas_call(
+        lambda *refs: first_kernel(s, *refs),
+        out_shape=(blocks, blocks, vector(n, 10)),
+        in_specs=[VMEM] * 6,
+        out_specs=(VMEM,) * 3,
+        scratch_shapes=staging,
+        compiler_params=BOUNDARY,
+    )(drive, field, coefs, down, from_below, from_above)
+    send, rt_1, dt_1 = pl.pallas_call(
+        lambda *refs: second_kernel(s, n_band, scale, *refs),
         out_shape=(jax.ShapeDtypeStruct(shape, BF16), blocks, blocks),
         in_specs=[SMEM] + [VMEM] * 9,
         out_specs=(VMEM,) * 3,
-        scratch_shapes=[pltpu.VMEM((n, 10, tiles, LANES), F32)] + [pltpu.VMEM((LANES // 2 * s.pitch, LANES), F32)] * 4,
+        scratch_shapes=staging,
         compiler_params=BOUNDARY,
-    )(place, local_rt, local_dt, drive, field, coefs, down, from_below, from_above, factors)
+    )(place, local_rt, local_dt, drive, field, rest_below, tots, factors, rt_0, dt_0)
     arrived = exchange(send, 1, devices)
     keep = pl.pallas_call(
         lambda place, *refs: products(s, n_band, scale, 0, place, *refs),
         out_shape=jax.ShapeDtypeStruct(shape, F32),
-        in_specs=[SMEM] + [VMEM] * 5,
+        in_specs=[SMEM] + [VMEM] * 7,
         out_specs=VMEM,
         compiler_params=BOUNDARY,
         cost_estimate=pl.CostEstimate(flops=2 * 10**9, bytes_accessed=2 * 10**7, transcendentals=0),
-    )(place, local_rt, local_dt, rt, dt, factors)
+    )(place, local_rt, local_dt, factors, rt_0, dt_0, rt_1, dt_1)
 
     value = keep + arrived.astype(F32)
     parts = [exchange(value[:, d].astype(BF16), d * n_slab, devices) for d in farthest_first(n_band)]

time: 41.4 us -> 40.5 us (0.978)
  Pallas kernels: 19.6 us -> 18.9 us
    ppermute x0 -> x1, starting transfers between devices: none -> 2.69 us  [body(): rest_below = lax.ppermute(rest, AXES, step)]
    ppermute x1, starting transfers between devices: 5.99 us -> 3.36 us  [body(): from_above = lax.ppermute(down, AXES, [(j, i) for i, j in step])]
    ppermute x1, waiting for transfers between devices: 0.75 us -> 0.01 us  [body(): from_below = lax.ppermute(up, AXES, step)]
    pallas_call x3 -> x4, Pallas kernels: 17.5 us -> 16.8 us  [the longest x1 8.68 us: body(): pl.pallas_call(lambda *refs: local_kernel(s, *refs), out_shape=(turned, t...]
    ppermute x0 -> x1, waiting for transfers between devices: none -> 0.42 us  [body(): rest_below = lax.ppermute(rest, AXES, step)]
  transfers between devices with their start and end apart: 9 -> 10, of which waited for: 6 -> 6; matrix products, arithmetic and copies ran while one was open for 0% -> 0% of each run, Pallas kernels for 27% -> 29%
where the time goes in v7:
time: 40.5 us; the launch traced here: 40.4 us
  Pallas kernels  18.9 us (47%)
  starting transfers between devices  13.7 us (34%)
  waiting for transfers between devices  6.35 us (16%)
  local copies, waits for them, and re-layouts  1.04 us (3%)
    pallas_call x1, Pallas kernels, body(): pl.pallas_call(lambda *refs: local_kernel(s, *refs), out_shape=(turned, t...  8.68 us
    ppermute x7, starting transfers between devices, exchange(): return lax.ppermute(value, AXES, [(i, i ^ distance) for i in range(size)])  7.17 us
    ppermute x7, waiting for transfers between devices, exchange(): return lax.ppermute(value, AXES, [(i, i ^ distance) for i in range(size)])  5.93 us
    pallas_call x1, Pallas kernels, body(): pl.pallas_call(lambda *refs: edge_kernel(s, *refs), out_shape=tuple((jax....  4.02 us
    ppermute x1, starting transfers between devices, body(): from_above = lax.ppermute(down, AXES, [(j, i) for i, j in step])  3.36 us
    pallas_call x1, Pallas kernels, body(): pl.pallas_call(lambda *refs: second_kernel(s, n_band, scale, *refs), out_...  2.99 us
    ppermute x1, starting transfers between devices, body(): rest_below = lax.ppermute(rest, AXES, step)  2.69 us
    pallas_call x1, Pallas kernels, body(): pl.pallas_call(lambda place, *refs: products(s, n_band, scale, 0, place,...  1.91 us
  transfers between devices with their start and end apart: 10, of which 6 were waited for; matrix products, arithmetic and copies ran while one was open for 0% of the time, Pallas kernels for 29%

profile of v7, /device:TPU:0, one launch (start us, length us, event | category | flops | bytes accessed | tf_op | source)
XLA Modules:
  0.0 40.4 jit_solution(12454790278392229829)
XLA Ops:
  0.0 4.0 %shard_map.17 = (bf16[110,16,128]{2,1,0:T(8,128)(2,1)S(1)}, bf16[96,16,128]{2,1,0:T(8,128)(2,1)S(1)}, f32[8,8,128]{2,1,0:T(8,128)S(1)}, f32[4,4,9,8,128]{4,3,2,1,0:T(8,128)S(1)}) custom-call(f32[16,6,6,32,128]{4,3,2,1,0:T(8,128)} %bitcast.45), custom_call_target="tpu_custom_call" | custom-call | tf_op jit(solution)/shard_map/pallas_call | solution.py:486
  4.0 0.5 %collective-permute-start.1 = (bf16[110,16,128]{2,1,0:T(8,128)(2,1)S(1)}, bf16[110,16,128]{2,1,0:T(8,128)(2,1)S(1)}, u32[]{:S(2)}, u32[]{:S(2)}) collective-permute-start(bf16[110,16,128]{2,1,0:T(8,128)(2,1)S(1)} %get-tuple-element.25), channel_id=1, source_target_pairs={{0,1},{1,2},{2,3},{3,4},{4,5},{5,6},{6,7},{7,8},{8,9},{9,10},{10,1... | collective-permute-start | bytes 1351688 | tf_op jit(solution)/shard_map/ppermute | solution.py:495
  4.5 2.7 %collective-permute-start.2 = (bf16[96,16,128]{2,1,0:T(8,128)(2,1)S(1)}, bf16[96,16,128]{2,1,0:T(8,128)(2,1)S(1)}, u32[]{:S(2)}, u32[]{:S(2)}) collective-permute-start(bf16[96,16,128]{2,1,0:T(8,128)(2,1)S(1)} %get-tuple-element.28), channel_id=1, source_target_pairs={{0,1},{1,2},{2,3},{3,4},{4,5},{5,6},{6,7},{7,8},{8,9},{9,10},{10,1... | collective-permute-start | bytes 1179656 | tf_op jit(solution)/shard_map/ppermute | solution.py:496
  7.2 3.4 %collective-permute-start = (f32[8,8,128]{2,1,0:T(8,128)S(1)}, f32[8,8,128]{2,1,0:T(8,128)S(1)}, u32[]{:S(2)}, u32[]{:S(2)}) collective-permute-start(f32[8,8,128]{2,1,0:T(8,128)S(1)} %get-tuple-element.22.refs_3_), channel_id=1, source_target_pairs={{1,0},{2,1},{3,2},{4,3},{5,4},{6,5},{7,6},{8,7},{9,8},{10,9},{11,1... | collective-permute-start | bytes 98312 | tf_op jit(solution)/shard_map/ppermute | solution.py:497
  10.6 8.7 %shard_map.18 = (bf16[8,8,16,16,128]{4,3,2,1,0:T(8,128)(2,1)S(1)}, bf16[8,8,16,16,128]{4,3,2,1,0:T(8,128)(2,1)S(1)}, f32[16,4,9,8,128]{4,3,2,1,0:T(8,128)S(1)}, f32[16,4,6,8,128]{4,3,2,1,0:T(8,128)S(1)}) custom-call(f32[16,6,6,32,128]{4,3,2,1,0:T(8,128)} %bitcast.46, f32[4,4,9,8,128]{4,3,2,1,0:T(8,128)S(1)} %get-tuple-element.19.refs_1_.refs_2_), custom_call_target="tpu_custom_call" | custom-call | flops 2000000000 | bytes 20000000 | tf_op jit(solution)/shard_map/pallas_call | solution.py:500
  19.4 0.2 shard_map.19.refs_7_.refs_2_
  19.5 1.1 %shard_map.20 = (bf16[4,8,8,16,128]{4,3,2,1,0:T(8,128)(2,1)S(1)}, bf16[4,8,8,16,128]{4,3,2,1,0:T(8,128)(2,1)S(1)}, f32[4,10,8,128]{3,2,1,0:T(8,128)S(1)}) custom-call(f32[16,4,9,8,128]{4,3,2,1,0:T(8,128)S(1)} %get-tuple-element.23.refs_0_.refs_3_, f32[16,4,6,8,128]{4,3,2,1,0:T(8,128)S(1)} %get-tuple-element.24.refs_1_.refs_4_, ...), custom_call_target="tpu_custom_call" | custom-call | tf_op jit(solution)/shard_map/pallas_call | solution.py:533
  20.7 0.4 %collective-permute-done.2.refs_5_ = bf16[96,16,128]{2,1,0:T(8,128)(2,1)S(1)} collective-permute-done((bf16[96,16,128]{2,1,0:T(8,128)(2,1)S(1)}, bf16[96,16,128]{2,1,0:T(8,128)(2,1)S(1)}, u32[]{:S(2)}, u32[]{:S(2)}) %collective-permute-start.2) | collective-permute-done | bytes 393248 | tf_op jit(solution)/shard_map/ppermute | solution.py:496
  21.1 3.0 %shard_map.21 = (bf16[4,4,32,256]{3,2,1,0:T(8,128)(2,1)S(1)}, bf16[4,8,8,16,128]{4,3,2,1,0:T(8,128)(2,1)S(1)}, bf16[4,8,8,16,128]{4,3,2,1,0:T(8,128)(2,1)S(1)}) custom-call(s32[2]{0:T(128)S(1)} %pad_add_fusion.refs_0_.place, bf16[8,8,16,16,128]{4,3,2,1,0:T(8,128)(2,1)S(1)} %get-tuple-element.20.refs_1_.refs_0_, ...), custom_call_target="tpu_custom_call" | custom-call | tf_op jit(solution)/shard_map/pallas_call | solution.py:541
  24.2 1.9 %shard_map.22 = f32[4,4,32,256]{3,2,1,0:T(8,128)S(1)} custom-call(s32[2]{0:T(128)S(1)} %pad_add_fusion.refs_0_.place, bf16[8,8,16,16,128]{4,3,2,1,0:T(8,128)(2,1)S(1)} %get-tuple-element.20.refs_1_.refs_0_, bf16[8,8,16,16,128]{4,3,2,1,0:T(8,128)(2,1)S(1)} %get-tuple-element.21.refs_2_.refs_1_, bf16[8,8,16,128]{3,2,1,0:T(8,128)(2,1)S(1)} %shard_map.19.refs_7_.refs_2_, ...), custom_call_target="tpu_custom_call" | custom-call | flops 2000000000 | bytes 20000000 | tf_op jit(solution)/shard_map/pallas_call | solution.py:550
  26.1 0.1 fusion.8
  26.2 2.0 %collective-permute-start.4 = (bf16[4,32,256]{2,1,0:T(8,128)(2,1)S(1)}, bf16[4,32,256]{2,1,0:T(8,128)(2,1)S(1)}, u32[]{:S(2)}, u32[]{:S(2)}) collective-permute-start(bf16[4,32,256]{2,1,0:T(8,128)(2,1)S(1)} %get-tuple-element.37), channel_id=1, source_target_pairs={{0,24},{1,25},{2,26},{3,27},{4,28},{5,29},{6,30},{7,31},{8,16},{9,... | collective-permute-start | bytes 196616 | tf_op jit(solution)/shard_map/ppermute | solution.py:464
  28.3 0.5 %collective-permute-start.6 = (bf16[4,32,256]{2,1,0:T(8,128)(2,1)S(1)}, bf16[4,32,256]{2,1,0:T(8,128)(2,1)S(1)}, u32[]{:S(2)}, u32[]{:S(2)}) collective-permute-start(bf16[4,32,256]{2,1,0:T(8,128)(2,1)S(1)} %get-tuple-element.38), channel_id=1, source_target_pairs={{0,16},{1,17},{2,18},{3,19},{4,20},{5,21},{6,22},{7,23},{8,24},{9,... | collective-permute-start | bytes 196616 | tf_op jit(solution)/shard_map/ppermute | solution.py:464
  28.8 1.0 %collective-permute-start.5 = (bf16[4,32,256]{2,1,0:T(8,128)(2,1)S(1)}, bf16[4,32,256]{2,1,0:T(8,128)(2,1)S(1)}, u32[]{:S(2)}, u32[]{:S(2)}) collective-permute-start(bf16[4,32,256]{2,1,0:T(8,128)(2,1)S(1)} %get-tuple-element.39), channel_id=1, source_target_pairs={{0,8},{1,9},{2,10},{3,11},{4,12},{5,13},{6,14},{7,15},{8,0},{9,1},... | collective-permute-start | bytes 196616 | tf_op jit(solution)/shard_map/ppermute | solution.py:464
  29.8 2.0 %collective-permute-done.4 = bf16[4,32,256]{2,1,0:T(8,128)(2,1)S(1)} collective-permute-done((bf16[4,32,256]{2,1,0:T(8,128)(2,1)S(1)}, bf16[4,32,256]{2,1,0:T(8,128)(2,1)S(1)}, u32[]{:S(2)}, u32[]{:S(2)}) %collective-permute-start.4) | collective-permute-done | bytes 65568 | tf_op jit(solution)/shard_map/ppermute | solution.py:464
  31.8 1.3 %collective-permute-done.6 = bf16[4,32,256]{2,1,0:T(8,128)(2,1)S(1)} collective-permute-done((bf16[4,32,256]{2,1,0:T(8,128)(2,1)S(1)}, bf16[4,32,256]{2,1,0:T(8,128)(2,1)S(1)}, u32[]{:S(2)}, u32[]{:S(2)}) %collective-permute-start.6) | collective-permute-done | bytes 65568 | tf_op jit(solution)/shard_map/ppermute | solution.py:464
  33.1 0.5 %collective-permute-done.5 = bf16[4,32,256]{2,1,0:T(8,128)(2,1)S(1)} collective-permute-done((bf16[4,32,256]{2,1,0:T(8,128)(2,1)S(1)}, bf16[4,32,256]{2,1,0:T(8,128)(2,1)S(1)}, u32[]{:S(2)}, u32[]{:S(2)}) %collective-permute-start.5) | collective-permute-done | bytes 65568 | tf_op jit(solution)/shard_map/ppermute | solution.py:464
  33.7 0.8 %collective-permute-start.9 = (bf16[32,256]{1,0:T(8,128)(2,1)S(1)}, bf16[32,256]{1,0:T(8,128)(2,1)S(1)}, u32[]{:S(2)}, u32[]{:S(2)}) collective-permute-start(bf16[32,256]{1,0:T(8,128)(2,1)S(1)} %get-tuple-element.41), channel_id=1, source_target_pairs={{0,6},{1,7},{2,4},{3,5},{4,2},{5,3},{6,0},{7,1},{8,14},{9,15},{10,... | collective-permute-start | bytes 49160 | tf_op jit(solution)/shard_map/ppermute | solution.py:464
  34.5 2.7 %collective-permute-start.8 = (bf16[32,256]{1,0:T(8,128)(2,1)S(1)}, bf16[32,256]{1,0:T(8,128)(2,1)S(1)}, u32[]{:S(2)}, u32[]{:S(2)}) collective-permute-start(bf16[32,256]{1,0:T(8,128)(2,1)S(1)} %get-tuple-element.42), channel_id=1, source_target_pairs={{0,4},{1,5},{2,6},{3,7},{4,0},{5,1},{6,2},{7,3},{8,12},{9,13},{10,... | collective-permute-start | bytes 49160 | tf_op jit(solution)/shard_map/ppermute | solution.py:464
  37.2 0.3 collective-permute-done.7
  37.4 1.9 %collective-permute-done.9 = bf16[32,256]{1,0:T(8,128)(2,1)S(1)} collective-permute-done((bf16[32,256]{1,0:T(8,128)(2,1)S(1)}, bf16[32,256]{1,0:T(8,128)(2,1)S(1)}, u32[]{:S(2)}, u32[]{:S(2)}) %collective-permute-start.9) | collective-permute-done | bytes 16416 | tf_op jit(solution)/shard_map/ppermute | solution.py:464
  39.3 0.1 reshape.20
  39.5 0.2 copy.6
  39.6 0.7 %reshape.21 = f32[4,16,128]{2,1,0:T(8,128)} reshape(f32[4,16,8,16]{3,2,1,0:T(8,128)S(1)} %copy.6) | data formatting | bytes 65536 | tf_op jit(solution)/shard_map/reshape | solution.py:565
  (11 shorter events, 0.3 us)
Async XLA Ops:
  4.0 15.5 %collective-permute-start.1 = (bf16[110,16,128]{2,1,0:T(8,128)(2,1)S(1)}, bf16[110,16,128]{2,1,0:T(8,128)(2,1)S(1)}, u32[]{:S(2)}, u32[]{:S(2)}) collective-permute-start(bf16[110,16,128]{2,1,0:T(8,128)(2,1)S(1)} %get-tuple-element.25), channel_id=1, source_target_pairs={{0,1},{1,2},{2,3},{3,4},{4,5},{5,6},{6,7},{7,8},{8,9},{9,10},{10,1... | collective-permute-start | bytes 1351688 | tf_op jit(solution)/shard_map/ppermute | solution.py:495
  4.5 16.6 %collective-permute-start.2 = (bf16[96,16,128]{2,1,0:T(8,128)(2,1)S(1)}, bf16[96,16,128]{2,1,0:T(8,128)(2,1)S(1)}, u32[]{:S(2)}, u32[]{:S(2)}) collective-permute-start(bf16[96,16,128]{2,1,0:T(8,128)(2,1)S(1)} %get-tuple-element.28), channel_id=1, source_target_pairs={{0,1},{1,2},{2,3},{3,4},{4,5},{5,6},{6,7},{7,8},{8,9},{9,10},{10,1... | collective-permute-start | bytes 1179656 | tf_op jit(solution)/shard_map/ppermute | solution.py:496
  7.2 12.1 %collective-permute-start = (f32[8,8,128]{2,1,0:T(8,128)S(1)}, f32[8,8,128]{2,1,0:T(8,128)S(1)}, u32[]{:S(2)}, u32[]{:S(2)}) collective-permute-start(f32[8,8,128]{2,1,0:T(8,128)S(1)} %get-tuple-element.22.refs_3_), channel_id=1, source_target_pairs={{1,0},{2,1},{3,2},{4,3},{5,4},{6,5},{7,6},{8,7},{9,8},{10,9},{11,1... | collective-permute-start | bytes 98312 | tf_op jit(solution)/shard_map/ppermute | solution.py:497
  24.1 2.0 %collective-permute-start.3 = (bf16[4,4,32,256]{3,2,1,0:T(8,128)(2,1)S(1)}, bf16[4,4,32,256]{3,2,1,0:T(8,128)(2,1)S(1)}, u32[]{:S(2)}, u32[]{:S(2)}) collective-permute-start(bf16[4,4,32,256]{3,2,1,0:T(8,128)(2,1)S(1)} %get-tuple-element.32), channel_id=1, source_target_pairs={{0,1},{1,0},{2,3},{3,2},{4,5},{5,4},{6,7},{7,6},{8,9},{9,8},{10,11... | collective-permute-start | bytes 786440 | tf_op jit(solution)/shard_map/ppermute | solution.py:464
  26.2 5.5 %collective-permute-start.4 = (bf16[4,32,256]{2,1,0:T(8,128)(2,1)S(1)}, bf16[4,32,256]{2,1,0:T(8,128)(2,1)S(1)}, u32[]{:S(2)}, u32[]{:S(2)}) collective-permute-start(bf16[4,32,256]{2,1,0:T(8,128)(2,1)S(1)} %get-tuple-element.37), channel_id=1, source_target_pairs={{0,24},{1,25},{2,26},{3,27},{4,28},{5,29},{6,30},{7,31},{8,16},{9,... | collective-permute-start | bytes 196616 | tf_op jit(solution)/shard_map/ppermute | solution.py:464
  28.3 4.8 %collective-permute-start.6 = (bf16[4,32,256]{2,1,0:T(8,128)(2,1)S(1)}, bf16[4,32,256]{2,1,0:T(8,128)(2,1)S(1)}, u32[]{:S(2)}, u32[]{:S(2)}) collective-permute-start(bf16[4,32,256]{2,1,0:T(8,128)(2,1)S(1)} %get-tuple-element.38), channel_id=1, source_target_pairs={{0,16},{1,17},{2,18},{3,19},{4,20},{5,21},{6,22},{7,23},{8,24},{9,... | collective-permute-start | bytes 196616 | tf_op jit(solution)/shard_map/ppermute | solution.py:464
  28.8 4.8 %collective-permute-start.5 = (bf16[4,32,256]{2,1,0:T(8,128)(2,1)S(1)}, bf16[4,32,256]{2,1,0:T(8,128)(2,1)S(1)}, u32[]{:S(2)}, u32[]{:S(2)}) collective-permute-start(bf16[4,32,256]{2,1,0:T(8,128)(2,1)S(1)} %get-tuple-element.39), channel_id=1, source_target_pairs={{0,8},{1,9},{2,10},{3,11},{4,12},{5,13},{6,14},{7,15},{8,0},{9,1},... | collective-permute-start | bytes 196616 | tf_op jit(solution)/shard_map/ppermute | solution.py:464
  33.6 3.8 %collective-permute-start.7 = (bf16[32,256]{1,0:T(8,128)(2,1)S(1)}, bf16[32,256]{1,0:T(8,128)(2,1)S(1)}, u32[]{:S(2)}, u32[]{:S(2)}) collective-permute-start(bf16[32,256]{1,0:T(8,128)(2,1)S(1)} %get-tuple-element.40), channel_id=1, source_target_pairs={{0,2},{1,3},{2,0},{3,1},{4,6},{5,7},{6,4},{7,5},{8,10},{9,11},{10,... | collective-permute-start | bytes 49160 | tf_op jit(solution)/shard_map/ppermute | solution.py:464
  33.7 5.6 %collective-permute-start.9 = (bf16[32,256]{1,0:T(8,128)(2,1)S(1)}, bf16[32,256]{1,0:T(8,128)(2,1)S(1)}, u32[]{:S(2)}, u32[]{:S(2)}) collective-permute-start(bf16[32,256]{1,0:T(8,128)(2,1)S(1)} %get-tuple-element.41), channel_id=1, source_target_pairs={{0,6},{1,7},{2,4},{3,5},{4,2},{5,3},{6,0},{7,1},{8,14},{9,15},{10,... | collective-permute-start | bytes 49160 | tf_op jit(solution)/shard_map/ppermute | solution.py:464
  34.5 4.8 %collective-permute-start.8 = (bf16[32,256]{1,0:T(8,128)(2,1)S(1)}, bf16[32,256]{1,0:T(8,128)(2,1)S(1)}, u32[]{:S(2)}, u32[]{:S(2)}) collective-permute-start(bf16[32,256]{1,0:T(8,128)(2,1)S(1)} %get-tuple-element.42), channel_id=1, source_target_pairs={{0,4},{1,5},{2,6},{3,7},{4,0},{5,1},{6,2},{7,3},{8,12},{9,13},{10,... | collective-permute-start | bytes 49160 | tf_op jit(solution)/shard_map/ppermute | solution.py:464

commit v8 on v7

--- a/solution.py
+++ b/solution.py
@@ -24,6 +24,7 @@
         self.bands, self.comps, self.planes, self.rows, cells = shape
         self.inner = self.planes - 2
         self.tiles = cells // LANES
+        self.first = self.bands // 2
         self.pitch = self.tiles + 1
 
 
@@ -46,7 +47,7 @@
     return after - before
 
 
-def edge_kernel(s, x_hbm, up_ref, rest_ref, down_ref, coefs, x_ref, sums, sems):
+def edge_kernel(s, x_hbm, up_ref, rest_ref, down_ref, sent_ref, coefs, x_ref, sums, sems):
     last = s.rows - 1
     n = s.inner
     whole, inside = (pl.ds(4, 2), pl.ds(0, 4))
@@ -59,7 +60,7 @@
         copy.start()
 
     def pack(first, count):
-        target, start = (up_ref, 0) if first < s.bands // 2 else (rest_ref, s.bands // 2)
+        target, start = (up_ref, 0) if first < s.first else (rest_ref, s.first)
 
         def band(q, carry):
             for c in range(s.comps):
@@ -96,6 +97,9 @@
             copy.wait()
         pack(first, share)
         add(first, share)
+    for i in range(2 * n // 2):
+        c, x = (3 + 2 * (2 * i // n), 2 * i % n + 1)
+        sent_ref[i] = jnp.concatenate([sums[c, x, 0], sums[c, x + 1, 0]], 0).astype(BF16)
     extras = [[], [], []] + [[sums[c, x + 1, last] for x in range(n)] for c in TOTALS]
     for x in range(n):
         down_ref[x] = sums[3, x + 1, 0]
@@ -120,7 +124,7 @@
                 coefs[x, y, 6 + d] = j[d]
                 if y == last:
                     extras[d].append(j[d])
-    base = s.bands // 2 * s.comps * (n // 2)
+    base = s.first * s.comps * (n // 2)
     for c, values in enumerate(extras):
         for p in range(n // 2):
             up_ref[base + c * (n // 2) + p] = jnp.concatenate(values[2 * p : 2 * p + 2], 0).astype(BF16)
@@ -315,11 +319,12 @@
 
 def factor_kernel(s, above_ref, factors, held):
     n = s.inner
+    above = halo_pair(s, above_ref, 0) + halo_pair(s, above_ref, 1)
     for entry in range(LANES):
         x, i = divmod(entry - (s.rows - 2) * n * 9, 13)
         value = jnp.ones((s.tiles, LANES), F32)
         if 0 <= x < n and i >= 9:
-            value = above_ref[(i - 9) // 2 * n + x] * (-0.25, 0.25, 0.25, -0.25)[i - 9]
+            value = above[(i - 9) // 2 * n + x] * (-0.25, 0.25, 0.25, -0.25)[i - 9]
         set_row(s, held, entry, value)
     for zt in range(s.tiles):
         factors[zt] = transposed(s, held, zt).reshape(LANES // GROUP, GROUP, LANES)
@@ -335,7 +340,7 @@
 
 def first_kernel(s, drive_ref, field_ref, coefs, down_ref, up_ref, above_ref, rt, dt, tots, *pads):
     n = s.inner
-    base = s.bands // 2 * s.comps
+    base = s.first * s.comps
     behinds = [halo_pair(s, up_ref, base + c) for c in range(3)]
     totals = [halo_pair(s, up_ref, base + 3 + k) for k in range(len(TOTALS))]
     for x in range(n):
@@ -346,22 +351,22 @@
         tots[x, 3] = (vy + my) * -0.25
         j = [coefs[x, 0, 6] - bz * 0.5, coefs[x, 0, 7], coefs[x, 0, 8] + bx * 0.5]
         if s.rows == 1:
-            j = [j[0] + above_ref[n + x] * 0.5, j[1], j[2] - above_ref[x] * 0.5]
+            above_x, above_z = (halo_pair(s, above_ref, k)[x] for k in range(2))
+            j = [j[0] + above_z * 0.5, j[1], j[2] - above_x * 0.5]
         behind = [behinds[0][x] + down_ref[n + x] * 0.5, behinds[1][x], behinds[2][x] - down_ref[x] * 0.5]
         for c in range(3):
             tots[x, 4 + c] = j[c] * -0.5
             tots[x, 7 + c] = behind[c] * -0.5
-    boundary_bands(s, 0, drive_ref, field_ref, up_ref, tots, rt, dt, pads)
+    boundary_bands(s, 0, s.first, drive_ref, field_ref, up_ref, tots, rt, dt, pads)
 
 
 def second_kernel(s, n_band, scale, place, local_rt, local_dt, drive_ref, field_ref, up_ref, tots, factors, rt_0, dt_0, send_ref, rt, dt, *pads):
-    boundary_bands(s, s.bands // 2, drive_ref, field_ref, up_ref, tots, rt, dt, pads)
+    boundary_bands(s, s.first, s.bands - s.first, drive_ref, field_ref, up_ref, tots, rt, dt, pads)
     products(s, n_band, scale, 1, place, local_rt, local_dt, factors, rt_0, dt_0, rt, dt, send_ref)
 
 
-def boundary_bands(s, first, drive_ref, field_ref, up_ref, tots, rt, dt, pads):
+def boundary_bands(s, first, count, drive_ref, field_ref, up_ref, tots, rt, dt, pads):
     n = s.inner
-    count = s.bands // 2
     half = LANES // 2
     used = n * 15
     for ref in pads:
@@ -425,7 +430,7 @@
         return carry
 
     steps = s.tiles // 2
-    lax.fori_loop(0, count // 2, pair, 0)
+    lax.fori_loop(0, count // 2, pair, 0, unroll=2)
     turn(*pads[2:4], count - 1, range(steps))
 
 
@@ -440,9 +445,9 @@
         zt = (r * 2 + core) ^ place[1]
         parts = []
         for g in range(LANES // GROUP):
-            left = jnp.concatenate([ref[zt // 2, g].reshape(wide // 2, LANES) for ref in (rt_0, rt_1)], 0)
+            left = jnp.concatenate([ref[zt // 2, g].reshape(-1, LANES) for ref in (rt_0, rt_1)], 0)
             left = jnp.where(wanted, left, jnp.zeros_like(left))
-            right = jnp.concatenate([ref[zt // 2, g].reshape(wide // 2, LANES) for ref in (dt_0, dt_1)], 0)
+            right = jnp.concatenate([ref[zt // 2, g].reshape(-1, LANES) for ref in (dt_0, dt_1)], 0)
             if s.rows > 1:
                 scaled = local_rt[zt, g] * factors[zt, g][None]
                 left = jnp.concatenate([scaled.reshape(wide, -1), left], 1)
@@ -480,21 +485,22 @@
     groups = LANES // GROUP
     wide = s.bands * GROUP
     share = s.bands // n_band
-    rows_up = s.bands // 2 * s.comps * (n // 2)
-    rows_first = rows_up + (3 + len(TOTALS)) * (n // 2)
-
-    up, rest, down, coefs = pl.pallas_call(
+    per_band = s.comps * (n // 2)
+    rows_first = s.first * per_band + (3 + len(TOTALS)) * (n // 2)
+    rows_rest = (s.bands - s.first) * per_band
+
+    up, rest, down, sent, coefs = pl.pallas_call(
         lambda *refs: edge_kernel(s, *refs),
-        out_shape=tuple(jax.ShapeDtypeStruct((count, 2 * tiles, LANES), BF16) for count in (rows_first, rows_up)) + (vector(2 * n), vector(n, rows, 9)),
+        out_shape=tuple(jax.ShapeDtypeStruct((count, 2 * tiles, LANES), BF16) for count in (rows_first, rows_rest)) + (vector(2 * n), jax.ShapeDtypeStruct((n, 2 * tiles, LANES), BF16), vector(n, rows, 9)),
         in_specs=[HBM],
-        out_specs=(VMEM,) * 4,
+        out_specs=(VMEM,) * 5,
         scratch_shapes=[pltpu.VMEM(x.shape, F32), pltpu.VMEM((s.comps, s.planes, rows, tiles, LANES), F32), pltpu.SemaphoreType.DMA((s.bands, 2))],
         compiler_params=EDGE,
     )(x)
     step = [(i, (i + 1) % devices) for i in range(devices)]
     from_below = lax.ppermute(up, AXES, step)
     rest_below = lax.ppermute(rest, AXES, step)
-    from_above = lax.ppermute(down, AXES, [(j, i) for i, j in step])
+    from_above = lax.ppermute(sent, AXES, [(j, i) for i, j in step])
 
     turned = jax.ShapeDtypeStruct((tiles, groups, s.bands, GROUP, depth), BF16)
     local_rt, local_dt, drive, field = pl.pallas_call(
@@ -511,7 +517,7 @@
     if rows == 1:
         two = lax.ppermute(down, AXES, [(i, (i + 2) % devices) for i in range(devices)])
         two = two.reshape(2, n // 2, 2 * tiles, LANES) * 0.5
-        base = rows_up
+        base = s.first * per_band
         end = base + 3 * (n // 2)
         behind = from_below[base:end].astype(F32).reshape(3, n // 2, 2 * tiles, LANES)
         behind = jnp.stack([behind[0] - two[1], behind[1], behind[2] + two[0]])
@@ -520,7 +526,7 @@
 
     shape = (tiles // 2, n_band, groups * share, wide)
     scale = 1.0 / (n * rows * devices)
-    blocks = jax.ShapeDtypeStruct((tiles // 2, groups, s.bands // 2, GROUP, LANES), BF16)
+    blocks = [jax.ShapeDtypeStruct((tiles // 2, groups, count, GROUP, LANES), BF16) for count in (s.first, s.bands - s.first)]
     staging = [pltpu.VMEM((LANES // 2 * s.pitch, LANES), F32)] * 4
     factors = pl.pallas_call(
         lambda *refs: factor_kernel(s, *refs),
@@ -532,7 +538,7 @@
     )(from_above)
     rt_0, dt_0, tots = pl.pallas_call(
         lambda *refs: first_kernel(s, *refs),
-        out_shape=(blocks, blocks, vector(n, 10)),
+        out_shape=(blocks[0], blocks[0], vector(n, 10)),
         in_specs=[VMEM] * 6,
         out_specs=(VMEM,) * 3,
         scratch_shapes=staging,
@@ -540,7 +546,7 @@
     )(drive, field, coefs, down, from_below, from_above)
     send, rt_1, dt_1 = pl.pallas_call(
         lambda *refs: second_kernel(s, n_band, scale, *refs),
-        out_shape=(jax.ShapeDtypeStruct(shape, BF16), blocks, blocks),
+        out_shape=(jax.ShapeDtypeStruct(shape, BF16), blocks[1], blocks[1]),
         in_specs=[SMEM] + [VMEM] * 9,
         out_specs=(VMEM,) * 3,
         scratch_shapes=staging,

time: 40.5 us -> 40.4 us (level)
  no operation moved by 1% of the time
where the time goes in v8:
time: 40.4 us; the launch traced here: 40.2 us
  Pallas kernels  18.8 us (47%)
  starting transfers between devices  13.7 us (34%)
  waiting for transfers between devices  6.26 us (15%)
  local copies, waits for them, and re-layouts  1.04 us (3%)
    pallas_call x1, Pallas kernels, body(): pl.pallas_call(lambda *refs: local_kernel(s, *refs), out_shape=(turned, t...  8.68 us
    ppermute x7, starting transfers between devices, exchange(): return lax.ppermute(value, AXES, [(i, i ^ distance) for i in range(size)])  7.17 us
    ppermute x7, waiting for transfers between devices, exchange(): return lax.ppermute(value, AXES, [(i, i ^ distance) for i in range(size)])  5.98 us
    pallas_call x1, Pallas kernels, body(): pl.pallas_call(lambda *refs: edge_kernel(s, *refs), out_shape=tuple((jax....  4.02 us
    ppermute x1, starting transfers between devices, body(): from_above = lax.ppermute(sent, AXES, [(j, i) for i, j in step])  3.36 us
    pallas_call x1, Pallas kernels, body(): pl.pallas_call(lambda *refs: second_kernel(s, n_band, scale, *refs), out_...  2.95 us
    ppermute x1, starting transfers between devices, body(): rest_below = lax.ppermute(rest, AXES, step)  2.69 us
    pallas_call x1, Pallas kernels, body(): pl.pallas_call(lambda place, *refs: products(s, n_band, scale, 0, place,...  1.91 us
  transfers between devices with their start and end apart: 10, of which 6 were waited for; matrix products, arithmetic and copies ran while one was open for 0% of the time, Pallas kernels for 29%

profile of v8, /device:TPU:0, one launch (start us, length us, event | category | flops | bytes accessed | tf_op | source)
XLA Modules:
  0.0 40.2 jit_solution(12094487130513711919)
XLA Ops:
  0.0 4.0 %shard_map.17 = (bf16[110,16,128]{2,1,0:T(8,128)(2,1)S(1)}, bf16[96,16,128]{2,1,0:T(8,128)(2,1)S(1)}, f32[8,8,128]{2,1,0:T(8,128)S(1)}, bf16[4,16,128]{2,1,0:T(8,128)(2,1)S(1)}, f32[4,4,9,8,128]{4,3,2,1,0:T(8,128)S(1)}) custom-call(f32[16,6,6,32,128]{4,3,2,1,0:T(8,128)} %bitcast.45), custom_call_target="tpu_custom_call" | custom-call | tf_op jit(solution)/shard_map/pallas_call | solution.py:492
  4.0 0.5 %collective-permute-start.1 = (bf16[110,16,128]{2,1,0:T(8,128)(2,1)S(1)}, bf16[110,16,128]{2,1,0:T(8,128)(2,1)S(1)}, u32[]{:S(2)}, u32[]{:S(2)}) collective-permute-start(bf16[110,16,128]{2,1,0:T(8,128)(2,1)S(1)} %get-tuple-element.27), channel_id=1, source_target_pairs={{0,1},{1,2},{2,3},{3,4},{4,5},{5,6},{6,7},{7,8},{8,9},{9,10},{10,1... | collective-permute-start | bytes 1351688 | tf_op jit(solution)/shard_map/ppermute | solution.py:501
  4.5 2.7 %collective-permute-start.2 = (bf16[96,16,128]{2,1,0:T(8,128)(2,1)S(1)}, bf16[96,16,128]{2,1,0:T(8,128)(2,1)S(1)}, u32[]{:S(2)}, u32[]{:S(2)}) collective-permute-start(bf16[96,16,128]{2,1,0:T(8,128)(2,1)S(1)} %get-tuple-element.30), channel_id=1, source_target_pairs={{0,1},{1,2},{2,3},{3,4},{4,5},{5,6},{6,7},{7,8},{8,9},{9,10},{10,1... | collective-permute-start | bytes 1179656 | tf_op jit(solution)/shard_map/ppermute | solution.py:502
  7.2 3.4 %collective-permute-start = (bf16[4,16,128]{2,1,0:T(8,128)(2,1)S(1)}, bf16[4,16,128]{2,1,0:T(8,128)(2,1)S(1)}, u32[]{:S(2)}, u32[]{:S(2)}) collective-permute-start(bf16[4,16,128]{2,1,0:T(8,128)(2,1)S(1)} %get-tuple-element.23), channel_id=1, source_target_pairs={{1,0},{2,1},{3,2},{4,3},{5,4},{6,5},{7,6},{8,7},{9,8},{10,9},{11,1... | collective-permute-start | bytes 49160 | tf_op jit(solution)/shard_map/ppermute | solution.py:503
  10.6 8.7 %shard_map.18 = (bf16[8,8,16,16,128]{4,3,2,1,0:T(8,128)(2,1)S(1)}, bf16[8,8,16,16,128]{4,3,2,1,0:T(8,128)(2,1)S(1)}, f32[16,4,9,8,128]{4,3,2,1,0:T(8,128)S(1)}, f32[16,4,6,8,128]{4,3,2,1,0:T(8,128)S(1)}) custom-call(f32[16,6,6,32,128]{4,3,2,1,0:T(8,128)} %bitcast.46, f32[4,4,9,8,128]{4,3,2,1,0:T(8,128)S(1)} %get-tuple-element.20.refs_1_.refs_2_), custom_call_target="tpu_custom_call" | custom-call | flops 2000000000 | bytes 20000000 | tf_op jit(solution)/shard_map/pallas_call | solution.py:506
  19.4 0.2 shard_map.19.refs_7_.refs_2_
  19.5 1.1 %shard_map.20 = (bf16[4,8,8,16,128]{4,3,2,1,0:T(8,128)(2,1)S(1)}, bf16[4,8,8,16,128]{4,3,2,1,0:T(8,128)(2,1)S(1)}, f32[4,10,8,128]{3,2,1,0:T(8,128)S(1)}) custom-call(f32[16,4,9,8,128]{4,3,2,1,0:T(8,128)S(1)} %get-tuple-element.24.refs_0_.refs_3_, f32[16,4,6,8,128]{4,3,2,1,0:T(8,128)S(1)} %get-tuple-element.25.refs_1_.refs_4_, ...), custom_call_target="tpu_custom_call" | custom-call | tf_op jit(solution)/shard_map/pallas_call | solution.py:539
  20.6 0.3 collective-permute-done.2.refs_5_
  20.9 3.0 %shard_map.21 = (bf16[4,4,32,256]{3,2,1,0:T(8,128)(2,1)S(1)}, bf16[4,8,8,16,128]{4,3,2,1,0:T(8,128)(2,1)S(1)}, bf16[4,8,8,16,128]{4,3,2,1,0:T(8,128)(2,1)S(1)}) custom-call(s32[2]{0:T(128)S(1)} %pad_add_fusion.refs_0_.place, bf16[8,8,16,16,128]{4,3,2,1,0:T(8,128)(2,1)S(1)} %get-tuple-element.21.refs_1_.refs_0_, ...), custom_call_target="tpu_custom_call" | custom-call | tf_op jit(solution)/shard_map/pallas_call | solution.py:547
  24.0 1.9 %shard_map.22 = f32[4,4,32,256]{3,2,1,0:T(8,128)S(1)} custom-call(s32[2]{0:T(128)S(1)} %pad_add_fusion.refs_0_.place, bf16[8,8,16,16,128]{4,3,2,1,0:T(8,128)(2,1)S(1)} %get-tuple-element.21.refs_1_.refs_0_, bf16[8,8,16,16,128]{4,3,2,1,0:T(8,128)(2,1)S(1)} %get-tuple-element.22.refs_2_.refs_1_, bf16[8,8,16,128]{3,2,1,0:T(8,128)(2,1)S(1)} %shard_map.19.refs_7_.refs_2_, ...), custom_call_target="tpu_custom_call" | custom-call | flops 2000000000 | bytes 20000000 | tf_op jit(solution)/shard_map/pallas_call | solution.py:556
  25.9 0.1 fusion.8
  26.0 2.0 %collective-permute-start.4 = (bf16[4,32,256]{2,1,0:T(8,128)(2,1)S(1)}, bf16[4,32,256]{2,1,0:T(8,128)(2,1)S(1)}, u32[]{:S(2)}, u32[]{:S(2)}) collective-permute-start(bf16[4,32,256]{2,1,0:T(8,128)(2,1)S(1)} %get-tuple-element.39), channel_id=1, source_target_pairs={{0,24},{1,25},{2,26},{3,27},{4,28},{5,29},{6,30},{7,31},{8,16},{9,... | collective-permute-start | bytes 196616 | tf_op jit(solution)/shard_map/ppermute | solution.py:469
  28.0 0.5 %collective-permute-start.6 = (bf16[4,32,256]{2,1,0:T(8,128)(2,1)S(1)}, bf16[4,32,256]{2,1,0:T(8,128)(2,1)S(1)}, u32[]{:S(2)}, u32[]{:S(2)}) collective-permute-start(bf16[4,32,256]{2,1,0:T(8,128)(2,1)S(1)} %get-tuple-element.40), channel_id=1, source_target_pairs={{0,16},{1,17},{2,18},{3,19},{4,20},{5,21},{6,22},{7,23},{8,24},{9,... | collective-permute-start | bytes 196616 | tf_op jit(solution)/shard_map/ppermute | solution.py:469
  28.6 1.0 %collective-permute-start.5 = (bf16[4,32,256]{2,1,0:T(8,128)(2,1)S(1)}, bf16[4,32,256]{2,1,0:T(8,128)(2,1)S(1)}, u32[]{:S(2)}, u32[]{:S(2)}) collective-permute-start(bf16[4,32,256]{2,1,0:T(8,128)(2,1)S(1)} %get-tuple-element.41), channel_id=1, source_target_pairs={{0,8},{1,9},{2,10},{3,11},{4,12},{5,13},{6,14},{7,15},{8,0},{9,1},... | collective-permute-start | bytes 196616 | tf_op jit(solution)/shard_map/ppermute | solution.py:469
  29.6 2.0 %collective-permute-done.4 = bf16[4,32,256]{2,1,0:T(8,128)(2,1)S(1)} collective-permute-done((bf16[4,32,256]{2,1,0:T(8,128)(2,1)S(1)}, bf16[4,32,256]{2,1,0:T(8,128)(2,1)S(1)}, u32[]{:S(2)}, u32[]{:S(2)}) %collective-permute-start.4) | collective-permute-done | bytes 65568 | tf_op jit(solution)/shard_map/ppermute | solution.py:469
  31.5 1.3 %collective-permute-done.6 = bf16[4,32,256]{2,1,0:T(8,128)(2,1)S(1)} collective-permute-done((bf16[4,32,256]{2,1,0:T(8,128)(2,1)S(1)}, bf16[4,32,256]{2,1,0:T(8,128)(2,1)S(1)}, u32[]{:S(2)}, u32[]{:S(2)}) %collective-permute-start.6) | collective-permute-done | bytes 65568 | tf_op jit(solution)/shard_map/ppermute | solution.py:469
  32.9 0.5 %collective-permute-done.5 = bf16[4,32,256]{2,1,0:T(8,128)(2,1)S(1)} collective-permute-done((bf16[4,32,256]{2,1,0:T(8,128)(2,1)S(1)}, bf16[4,32,256]{2,1,0:T(8,128)(2,1)S(1)}, u32[]{:S(2)}, u32[]{:S(2)}) %collective-permute-start.5) | collective-permute-done | bytes 65568 | tf_op jit(solution)/shard_map/ppermute | solution.py:469
  33.5 0.9 %collective-permute-start.9 = (bf16[32,256]{1,0:T(8,128)(2,1)S(1)}, bf16[32,256]{1,0:T(8,128)(2,1)S(1)}, u32[]{:S(2)}, u32[]{:S(2)}) collective-permute-start(bf16[32,256]{1,0:T(8,128)(2,1)S(1)} %get-tuple-element.43), channel_id=1, source_target_pairs={{0,6},{1,7},{2,4},{3,5},{4,2},{5,3},{6,0},{7,1},{8,14},{9,15},{10,... | collective-permute-start | bytes 49160 | tf_op jit(solution)/shard_map/ppermute | solution.py:469
  34.3 2.6 %collective-permute-start.8 = (bf16[32,256]{1,0:T(8,128)(2,1)S(1)}, bf16[32,256]{1,0:T(8,128)(2,1)S(1)}, u32[]{:S(2)}, u32[]{:S(2)}) collective-permute-start(bf16[32,256]{1,0:T(8,128)(2,1)S(1)} %get-tuple-element.44), channel_id=1, source_target_pairs={{0,4},{1,5},{2,6},{3,7},{4,0},{5,1},{6,2},{7,3},{8,12},{9,13},{10,... | collective-permute-start | bytes 49160 | tf_op jit(solution)/shard_map/ppermute | solution.py:469
  37.0 0.3 collective-permute-done.7
  37.2 1.9 %collective-permute-done.9 = bf16[32,256]{1,0:T(8,128)(2,1)S(1)} collective-permute-done((bf16[32,256]{1,0:T(8,128)(2,1)S(1)}, bf16[32,256]{1,0:T(8,128)(2,1)S(1)}, u32[]{:S(2)}, u32[]{:S(2)}) %collective-permute-start.9) | collective-permute-done | bytes 16416 | tf_op jit(solution)/shard_map/ppermute | solution.py:469
  39.2 0.1 reshape.20
  39.3 0.2 copy.6
  39.5 0.7 %reshape.21 = f32[4,16,128]{2,1,0:T(8,128)} reshape(f32[4,16,8,16]{3,2,1,0:T(8,128)S(1)} %copy.6) | data formatting | bytes 65536 | tf_op jit(solution)/shard_map/reshape | solution.py:571
  (11 shorter events, 0.3 us)
Async XLA Ops:
  4.0 15.5 %collective-permute-start.1 = (bf16[110,16,128]{2,1,0:T(8,128)(2,1)S(1)}, bf16[110,16,128]{2,1,0:T(8,128)(2,1)S(1)}, u32[]{:S(2)}, u32[]{:S(2)}) collective-permute-start(bf16[110,16,128]{2,1,0:T(8,128)(2,1)S(1)} %get-tuple-element.27), channel_id=1, source_target_pairs={{0,1},{1,2},{2,3},{3,4},{4,5},{5,6},{6,7},{7,8},{8,9},{9,10},{10,1... | collective-permute-start | bytes 1351688 | tf_op jit(solution)/shard_map/ppermute | solution.py:501
  4.5 16.4 %collective-permute-start.2 = (bf16[96,16,128]{2,1,0:T(8,128)(2,1)S(1)}, bf16[96,16,128]{2,1,0:T(8,128)(2,1)S(1)}, u32[]{:S(2)}, u32[]{:S(2)}) collective-permute-start(bf16[96,16,128]{2,1,0:T(8,128)(2,1)S(1)} %get-tuple-element.30), channel_id=1, source_target_pairs={{0,1},{1,2},{2,3},{3,4},{4,5},{5,6},{6,7},{7,8},{8,9},{9,10},{10,1... | collective-permute-start | bytes 1179656 | tf_op jit(solution)/shard_map/ppermute | solution.py:502
  7.2 12.1 %collective-permute-start = (bf16[4,16,128]{2,1,0:T(8,128)(2,1)S(1)}, bf16[4,16,128]{2,1,0:T(8,128)(2,1)S(1)}, u32[]{:S(2)}, u32[]{:S(2)}) collective-permute-start(bf16[4,16,128]{2,1,0:T(8,128)(2,1)S(1)} %get-tuple-element.23), channel_id=1, source_target_pairs={{1,0},{2,1},{3,2},{4,3},{5,4},{6,5},{7,6},{8,7},{9,8},{10,9},{11,1... | collective-permute-start | bytes 49160 | tf_op jit(solution)/shard_map/ppermute | solution.py:503
  23.9 2.0 %collective-permute-start.3 = (bf16[4,4,32,256]{3,2,1,0:T(8,128)(2,1)S(1)}, bf16[4,4,32,256]{3,2,1,0:T(8,128)(2,1)S(1)}, u32[]{:S(2)}, u32[]{:S(2)}) collective-permute-start(bf16[4,4,32,256]{3,2,1,0:T(8,128)(2,1)S(1)} %get-tuple-element.34), channel_id=1, source_target_pairs={{0,1},{1,0},{2,3},{3,2},{4,5},{5,4},{6,7},{7,6},{8,9},{9,8},{10,11... | collective-permute-start | bytes 786440 | tf_op jit(solution)/shard_map/ppermute | solution.py:469
  26.0 5.5 %collective-permute-start.4 = (bf16[4,32,256]{2,1,0:T(8,128)(2,1)S(1)}, bf16[4,32,256]{2,1,0:T(8,128)(2,1)S(1)}, u32[]{:S(2)}, u32[]{:S(2)}) collective-permute-start(bf16[4,32,256]{2,1,0:T(8,128)(2,1)S(1)} %get-tuple-element.39), channel_id=1, source_target_pairs={{0,24},{1,25},{2,26},{3,27},{4,28},{5,29},{6,30},{7,31},{8,16},{9,... | collective-permute-start | bytes 196616 | tf_op jit(solution)/shard_map/ppermute | solution.py:469
  28.0 4.8 %collective-permute-start.6 = (bf16[4,32,256]{2,1,0:T(8,128)(2,1)S(1)}, bf16[4,32,256]{2,1,0:T(8,128)(2,1)S(1)}, u32[]{:S(2)}, u32[]{:S(2)}) collective-permute-start(bf16[4,32,256]{2,1,0:T(8,128)(2,1)S(1)} %get-tuple-element.40), channel_id=1, source_target_pairs={{0,16},{1,17},{2,18},{3,19},{4,20},{5,21},{6,22},{7,23},{8,24},{9,... | collective-permute-start | bytes 196616 | tf_op jit(solution)/shard_map/ppermute | solution.py:469
  28.6 4.8 %collective-permute-start.5 = (bf16[4,32,256]{2,1,0:T(8,128)(2,1)S(1)}, bf16[4,32,256]{2,1,0:T(8,128)(2,1)S(1)}, u32[]{:S(2)}, u32[]{:S(2)}) collective-permute-start(bf16[4,32,256]{2,1,0:T(8,128)(2,1)S(1)} %get-tuple-element.41), channel_id=1, source_target_pairs={{0,8},{1,9},{2,10},{3,11},{4,12},{5,13},{6,14},{7,15},{8,0},{9,1},... | collective-permute-start | bytes 196616 | tf_op jit(solution)/shard_map/ppermute | solution.py:469
  33.4 3.8 %collective-permute-start.7 = (bf16[32,256]{1,0:T(8,128)(2,1)S(1)}, bf16[32,256]{1,0:T(8,128)(2,1)S(1)}, u32[]{:S(2)}, u32[]{:S(2)}) collective-permute-start(bf16[32,256]{1,0:T(8,128)(2,1)S(1)} %get-tuple-element.42), channel_id=1, source_target_pairs={{0,2},{1,3},{2,0},{3,1},{4,6},{5,7},{6,4},{7,5},{8,10},{9,11},{10,... | collective-permute-start | bytes 49160 | tf_op jit(solution)/shard_map/ppermute | solution.py:469
  33.5 5.7 %collective-permute-start.9 = (bf16[32,256]{1,0:T(8,128)(2,1)S(1)}, bf16[32,256]{1,0:T(8,128)(2,1)S(1)}, u32[]{:S(2)}, u32[]{:S(2)}) collective-permute-start(bf16[32,256]{1,0:T(8,128)(2,1)S(1)} %get-tuple-element.43), channel_id=1, source_target_pairs={{0,6},{1,7},{2,4},{3,5},{4,2},{5,3},{6,0},{7,1},{8,14},{9,15},{10,... | collective-permute-start | bytes 49160 | tf_op jit(solution)/shard_map/ppermute | solution.py:469
  34.3 4.8 %collective-permute-start.8 = (bf16[32,256]{1,0:T(8,128)(2,1)S(1)}, bf16[32,256]{1,0:T(8,128)(2,1)S(1)}, u32[]{:S(2)}, u32[]{:S(2)}) collective-permute-start(bf16[32,256]{1,0:T(8,128)(2,1)S(1)} %get-tuple-element.44), channel_id=1, source_target_pairs={{0,4},{1,5},{2,6},{3,7},{4,0},{5,1},{6,2},{7,3},{8,12},{9,13},{10,... | collective-permute-start | bytes 49160 | tf_op jit(solution)/shard_map/ppermute | solution.py:469

commit v9 on v8

--- a/solution.py
+++ b/solution.py
@@ -309,7 +309,7 @@
     fetch(0).wait()
     for y in range(s.rows):
         shifted(z_refs[0], 0, y)
-    lax.fori_loop(0, s.bands // 2, pair, 0)
+    lax.fori_loop(0, s.bands // 2, pair, 0, unroll=2)
     if used:
         turn(*pads[2:4], s.bands - 1, range(s.tiles))
     else:
@@ -565,7 +565,9 @@
     value = keep + arrived.astype(F32)
     parts = [exchange(value[:, d].astype(BF16), d * n_slab, devices) for d in farthest_first(n_band)]
     value = sum([p.astype(F32) for p in parts], value[:, 0])
-    parts = [exchange(value[e].astype(BF16), 2 * e, devices) for e in range(1, tiles // 2)]
+    order = sorted(range(1, tiles // 2), key=lambda e: (e.bit_count(), -e))
+    parts = {e: exchange(value[e].astype(BF16), 2 * e, devices) for e in order}
+    parts = [parts[e] for e in sorted(parts)]
     value = sum([p.astype(F32) for p in parts], value[0])
     value = value.reshape(groups, share, s.bands, GROUP).transpose(1, 2, 0, 3)
     return value.reshape(share, s.bands, groups * GROUP)

time: 40.4 us -> 40.4 us (level)
  no operation moved by 1% of the time
where the time goes in v9:
time: 40.4 us; the launch traced here: 40.2 us
  Pallas kernels  18.8 us (47%)
  starting transfers between devices  13.7 us (34%)
  waiting for transfers between devices  6.26 us (15%)
  local copies, waits for them, and re-layouts  1.04 us (3%)
    pallas_call x1, Pallas kernels, body(): pl.pallas_call(lambda *refs: local_kernel(s, *refs), out_shape=(turned, t...  8.68 us
    ppermute x7, starting transfers between devices, exchange(): return lax.ppermute(value, AXES, [(i, i ^ distance) for i in range(size)])  7.17 us
    ppermute x7, waiting for transfers between devices, exchange(): return lax.ppermute(value, AXES, [(i, i ^ distance) for i in range(size)])  5.98 us
    pallas_call x1, Pallas kernels, body(): pl.pallas_call(lambda *refs: edge_kernel(s, *refs), out_shape=tuple((jax....  4.02 us
    ppermute x1, starting transfers between devices, body(): from_above = lax.ppermute(sent, AXES, [(j, i) for i, j in step])  3.36 us
    pallas_call x1, Pallas kernels, body(): pl.pallas_call(lambda *refs: second_kernel(s, n_band, scale, *refs), out_...  2.95 us
    ppermute x1, starting transfers between devices, body(): rest_below = lax.ppermute(rest, AXES, step)  2.69 us
    pallas_call x1, Pallas kernels, body(): pl.pallas_call(lambda place, *refs: products(s, n_band, scale, 0, place,...  1.91 us
  transfers between devices with their start and end apart: 10, of which 6 were waited for; matrix products, arithmetic and copies ran while one was open for 0% of the time, Pallas kernels for 29%

profile of v9, /device:TPU:0, one launch (start us, length us, event | category | flops | bytes accessed | tf_op | source)
XLA Modules:
  0.0 40.2 jit_solution(4303894251241766911)
XLA Ops:
  0.0 4.0 %shard_map.17 = (bf16[110,16,128]{2,1,0:T(8,128)(2,1)S(1)}, bf16[96,16,128]{2,1,0:T(8,128)(2,1)S(1)}, f32[8,8,128]{2,1,0:T(8,128)S(1)}, bf16[4,16,128]{2,1,0:T(8,128)(2,1)S(1)}, f32[4,4,9,8,128]{4,3,2,1,0:T(8,128)S(1)}) custom-call(f32[16,6,6,32,128]{4,3,2,1,0:T(8,128)} %bitcast.45), custom_call_target="tpu_custom_call" | custom-call | tf_op jit(solution)/shard_map/pallas_call | solution.py:492
  4.0 0.5 %collective-permute-start.1 = (bf16[110,16,128]{2,1,0:T(8,128)(2,1)S(1)}, bf16[110,16,128]{2,1,0:T(8,128)(2,1)S(1)}, u32[]{:S(2)}, u32[]{:S(2)}) collective-permute-start(bf16[110,16,128]{2,1,0:T(8,128)(2,1)S(1)} %get-tuple-element.27), channel_id=1, source_target_pairs={{0,1},{1,2},{2,3},{3,4},{4,5},{5,6},{6,7},{7,8},{8,9},{9,10},{10,1... | collective-permute-start | bytes 1351688 | tf_op jit(solution)/shard_map/ppermute | solution.py:501
  4.5 2.7 %collective-permute-start.2 = (bf16[96,16,128]{2,1,0:T(8,128)(2,1)S(1)}, bf16[96,16,128]{2,1,0:T(8,128)(2,1)S(1)}, u32[]{:S(2)}, u32[]{:S(2)}) collective-permute-start(bf16[96,16,128]{2,1,0:T(8,128)(2,1)S(1)} %get-tuple-element.30), channel_id=1, source_target_pairs={{0,1},{1,2},{2,3},{3,4},{4,5},{5,6},{6,7},{7,8},{8,9},{9,10},{10,1... | collective-permute-start | bytes 1179656 | tf_op jit(solution)/shard_map/ppermute | solution.py:502
  7.2 3.4 %collective-permute-start = (bf16[4,16,128]{2,1,0:T(8,128)(2,1)S(1)}, bf16[4,16,128]{2,1,0:T(8,128)(2,1)S(1)}, u32[]{:S(2)}, u32[]{:S(2)}) collective-permute-start(bf16[4,16,128]{2,1,0:T(8,128)(2,1)S(1)} %get-tuple-element.23), channel_id=1, source_target_pairs={{1,0},{2,1},{3,2},{4,3},{5,4},{6,5},{7,6},{8,7},{9,8},{10,9},{11,1... | collective-permute-start | bytes 49160 | tf_op jit(solution)/shard_map/ppermute | solution.py:503
  10.6 8.7 %shard_map.18 = (bf16[8,8,16,16,128]{4,3,2,1,0:T(8,128)(2,1)S(1)}, bf16[8,8,16,16,128]{4,3,2,1,0:T(8,128)(2,1)S(1)}, f32[16,4,9,8,128]{4,3,2,1,0:T(8,128)S(1)}, f32[16,4,6,8,128]{4,3,2,1,0:T(8,128)S(1)}) custom-call(f32[16,6,6,32,128]{4,3,2,1,0:T(8,128)} %bitcast.46, f32[4,4,9,8,128]{4,3,2,1,0:T(8,128)S(1)} %get-tuple-element.20.refs_1_.refs_2_), custom_call_target="tpu_custom_call" | custom-call | flops 2000000000 | bytes 20000000 | tf_op jit(solution)/shard_map/pallas_call | solution.py:506
  19.4 0.2 shard_map.19.refs_7_.refs_2_
  19.5 1.1 %shard_map.20 = (bf16[4,8,8,16,128]{4,3,2,1,0:T(8,128)(2,1)S(1)}, bf16[4,8,8,16,128]{4,3,2,1,0:T(8,128)(2,1)S(1)}, f32[4,10,8,128]{3,2,1,0:T(8,128)S(1)}) custom-call(f32[16,4,9,8,128]{4,3,2,1,0:T(8,128)S(1)} %get-tuple-element.24.refs_0_.refs_3_, f32[16,4,6,8,128]{4,3,2,1,0:T(8,128)S(1)} %get-tuple-element.25.refs_1_.refs_4_, ...), custom_call_target="tpu_custom_call" | custom-call | tf_op jit(solution)/shard_map/pallas_call | solution.py:539
  20.6 0.3 collective-permute-done.2.refs_5_
  20.9 3.0 %shard_map.21 = (bf16[4,4,32,256]{3,2,1,0:T(8,128)(2,1)S(1)}, bf16[4,8,8,16,128]{4,3,2,1,0:T(8,128)(2,1)S(1)}, bf16[4,8,8,16,128]{4,3,2,1,0:T(8,128)(2,1)S(1)}) custom-call(s32[2]{0:T(128)S(1)} %pad_add_fusion.refs_0_.place, bf16[8,8,16,16,128]{4,3,2,1,0:T(8,128)(2,1)S(1)} %get-tuple-element.21.refs_1_.refs_0_, ...), custom_call_target="tpu_custom_call" | custom-call | tf_op jit(solution)/shard_map/pallas_call | solution.py:547
  24.0 1.9 %shard_map.22 = f32[4,4,32,256]{3,2,1,0:T(8,128)S(1)} custom-call(s32[2]{0:T(128)S(1)} %pad_add_fusion.refs_0_.place, bf16[8,8,16,16,128]{4,3,2,1,0:T(8,128)(2,1)S(1)} %get-tuple-element.21.refs_1_.refs_0_, bf16[8,8,16,16,128]{4,3,2,1,0:T(8,128)(2,1)S(1)} %get-tuple-element.22.refs_2_.refs_1_, bf16[8,8,16,128]{3,2,1,0:T(8,128)(2,1)S(1)} %shard_map.19.refs_7_.refs_2_, ...), custom_call_target="tpu_custom_call" | custom-call | flops 2000000000 | bytes 20000000 | tf_op jit(solution)/shard_map/pallas_call | solution.py:556
  25.9 0.1 fusion.8
  26.0 2.0 %collective-permute-start.4 = (bf16[4,32,256]{2,1,0:T(8,128)(2,1)S(1)}, bf16[4,32,256]{2,1,0:T(8,128)(2,1)S(1)}, u32[]{:S(2)}, u32[]{:S(2)}) collective-permute-start(bf16[4,32,256]{2,1,0:T(8,128)(2,1)S(1)} %get-tuple-element.39), channel_id=1, source_target_pairs={{0,24},{1,25},{2,26},{3,27},{4,28},{5,29},{6,30},{7,31},{8,16},{9,... | collective-permute-start | bytes 196616 | tf_op jit(solution)/shard_map/ppermute | solution.py:469
  28.0 0.5 %collective-permute-start.6 = (bf16[4,32,256]{2,1,0:T(8,128)(2,1)S(1)}, bf16[4,32,256]{2,1,0:T(8,128)(2,1)S(1)}, u32[]{:S(2)}, u32[]{:S(2)}) collective-permute-start(bf16[4,32,256]{2,1,0:T(8,128)(2,1)S(1)} %get-tuple-element.40), channel_id=1, source_target_pairs={{0,16},{1,17},{2,18},{3,19},{4,20},{5,21},{6,22},{7,23},{8,24},{9,... | collective-permute-start | bytes 196616 | tf_op jit(solution)/shard_map/ppermute | solution.py:469
  28.6 1.0 %collective-permute-start.5 = (bf16[4,32,256]{2,1,0:T(8,128)(2,1)S(1)}, bf16[4,32,256]{2,1,0:T(8,128)(2,1)S(1)}, u32[]{:S(2)}, u32[]{:S(2)}) collective-permute-start(bf16[4,32,256]{2,1,0:T(8,128)(2,1)S(1)} %get-tuple-element.41), channel_id=1, source_target_pairs={{0,8},{1,9},{2,10},{3,11},{4,12},{5,13},{6,14},{7,15},{8,0},{9,1},... | collective-permute-start | bytes 196616 | tf_op jit(solution)/shard_map/ppermute | solution.py:469
  29.6 2.0 %collective-permute-done.4 = bf16[4,32,256]{2,1,0:T(8,128)(2,1)S(1)} collective-permute-done((bf16[4,32,256]{2,1,0:T(8,128)(2,1)S(1)}, bf16[4,32,256]{2,1,0:T(8,128)(2,1)S(1)}, u32[]{:S(2)}, u32[]{:S(2)}) %collective-permute-start.4) | collective-permute-done | bytes 65568 | tf_op jit(solution)/shard_map/ppermute | solution.py:469
  31.5 1.3 %collective-permute-done.6 = bf16[4,32,256]{2,1,0:T(8,128)(2,1)S(1)} collective-permute-done((bf16[4,32,256]{2,1,0:T(8,128)(2,1)S(1)}, bf16[4,32,256]{2,1,0:T(8,128)(2,1)S(1)}, u32[]{:S(2)}, u32[]{:S(2)}) %collective-permute-start.6) | collective-permute-done | bytes 65568 | tf_op jit(solution)/shard_map/ppermute | solution.py:469
  32.9 0.5 %collective-permute-done.5 = bf16[4,32,256]{2,1,0:T(8,128)(2,1)S(1)} collective-permute-done((bf16[4,32,256]{2,1,0:T(8,128)(2,1)S(1)}, bf16[4,32,256]{2,1,0:T(8,128)(2,1)S(1)}, u32[]{:S(2)}, u32[]{:S(2)}) %collective-permute-start.5) | collective-permute-done | bytes 65568 | tf_op jit(solution)/shard_map/ppermute | solution.py:469
  33.5 0.9 %collective-permute-start.9 = (bf16[32,256]{1,0:T(8,128)(2,1)S(1)}, bf16[32,256]{1,0:T(8,128)(2,1)S(1)}, u32[]{:S(2)}, u32[]{:S(2)}) collective-permute-start(bf16[32,256]{1,0:T(8,128)(2,1)S(1)} %get-tuple-element.43), channel_id=1, source_target_pairs={{0,6},{1,7},{2,4},{3,5},{4,2},{5,3},{6,0},{7,1},{8,14},{9,15},{10,... | collective-permute-start | bytes 49160 | tf_op jit(solution)/shard_map/ppermute | solution.py:469
  34.3 2.6 %collective-permute-start.8 = (bf16[32,256]{1,0:T(8,128)(2,1)S(1)}, bf16[32,256]{1,0:T(8,128)(2,1)S(1)}, u32[]{:S(2)}, u32[]{:S(2)}) collective-permute-start(bf16[32,256]{1,0:T(8,128)(2,1)S(1)} %get-tuple-element.44), channel_id=1, source_target_pairs={{0,4},{1,5},{2,6},{3,7},{4,0},{5,1},{6,2},{7,3},{8,12},{9,13},{10,... | collective-permute-start | bytes 49160 | tf_op jit(solution)/shard_map/ppermute | solution.py:469
  37.0 0.3 collective-permute-done.7
  37.2 1.9 %collective-permute-done.9 = bf16[32,256]{1,0:T(8,128)(2,1)S(1)} collective-permute-done((bf16[32,256]{1,0:T(8,128)(2,1)S(1)}, bf16[32,256]{1,0:T(8,128)(2,1)S(1)}, u32[]{:S(2)}, u32[]{:S(2)}) %collective-permute-start.9) | collective-permute-done | bytes 16416 | tf_op jit(solution)/shard_map/ppermute | solution.py:469
  39.2 0.1 reshape.20
  39.3 0.2 copy.6
  39.5 0.7 %reshape.21 = f32[4,16,128]{2,1,0:T(8,128)} reshape(f32[4,16,8,16]{3,2,1,0:T(8,128)S(1)} %copy.6) | data formatting | bytes 65536 | tf_op jit(solution)/shard_map/reshape | solution.py:573
  (11 shorter events, 0.3 us)
Async XLA Ops:
  4.0 15.5 %collective-permute-start.1 = (bf16[110,16,128]{2,1,0:T(8,128)(2,1)S(1)}, bf16[110,16,128]{2,1,0:T(8,128)(2,1)S(1)}, u32[]{:S(2)}, u32[]{:S(2)}) collective-permute-start(bf16[110,16,128]{2,1,0:T(8,128)(2,1)S(1)} %get-tuple-element.27), channel_id=1, source_target_pairs={{0,1},{1,2},{2,3},{3,4},{4,5},{5,6},{6,7},{7,8},{8,9},{9,10},{10,1... | collective-permute-start | bytes 1351688 | tf_op jit(solution)/shard_map/ppermute | solution.py:501
  4.5 16.4 %collective-permute-start.2 = (bf16[96,16,128]{2,1,0:T(8,128)(2,1)S(1)}, bf16[96,16,128]{2,1,0:T(8,128)(2,1)S(1)}, u32[]{:S(2)}, u32[]{:S(2)}) collective-permute-start(bf16[96,16,128]{2,1,0:T(8,128)(2,1)S(1)} %get-tuple-element.30), channel_id=1, source_target_pairs={{0,1},{1,2},{2,3},{3,4},{4,5},{5,6},{6,7},{7,8},{8,9},{9,10},{10,1... | collective-permute-start | bytes 1179656 | tf_op jit(solution)/shard_map/ppermute | solution.py:502
  7.2 12.1 %collective-permute-start = (bf16[4,16,128]{2,1,0:T(8,128)(2,1)S(1)}, bf16[4,16,128]{2,1,0:T(8,128)(2,1)S(1)}, u32[]{:S(2)}, u32[]{:S(2)}) collective-permute-start(bf16[4,16,128]{2,1,0:T(8,128)(2,1)S(1)} %get-tuple-element.23), channel_id=1, source_target_pairs={{1,0},{2,1},{3,2},{4,3},{5,4},{6,5},{7,6},{8,7},{9,8},{10,9},{11,1... | collective-permute-start | bytes 49160 | tf_op jit(solution)/shard_map/ppermute | solution.py:503
  23.9 2.0 %collective-permute-start.3 = (bf16[4,4,32,256]{3,2,1,0:T(8,128)(2,1)S(1)}, bf16[4,4,32,256]{3,2,1,0:T(8,128)(2,1)S(1)}, u32[]{:S(2)}, u32[]{:S(2)}) collective-permute-start(bf16[4,4,32,256]{3,2,1,0:T(8,128)(2,1)S(1)} %get-tuple-element.34), channel_id=1, source_target_pairs={{0,1},{1,0},{2,3},{3,2},{4,5},{5,4},{6,7},{7,6},{8,9},{9,8},{10,11... | collective-permute-start | bytes 786440 | tf_op jit(solution)/shard_map/ppermute | solution.py:469
  26.0 5.5 %collective-permute-start.4 = (bf16[4,32,256]{2,1,0:T(8,128)(2,1)S(1)}, bf16[4,32,256]{2,1,0:T(8,128)(2,1)S(1)}, u32[]{:S(2)}, u32[]{:S(2)}) collective-permute-start(bf16[4,32,256]{2,1,0:T(8,128)(2,1)S(1)} %get-tuple-element.39), channel_id=1, source_target_pairs={{0,24},{1,25},{2,26},{3,27},{4,28},{5,29},{6,30},{7,31},{8,16},{9,... | collective-permute-start | bytes 196616 | tf_op jit(solution)/shard_map/ppermute | solution.py:469
  28.0 4.8 %collective-permute-start.6 = (bf16[4,32,256]{2,1,0:T(8,128)(2,1)S(1)}, bf16[4,32,256]{2,1,0:T(8,128)(2,1)S(1)}, u32[]{:S(2)}, u32[]{:S(2)}) collective-permute-start(bf16[4,32,256]{2,1,0:T(8,128)(2,1)S(1)} %get-tuple-element.40), channel_id=1, source_target_pairs={{0,16},{1,17},{2,18},{3,19},{4,20},{5,21},{6,22},{7,23},{8,24},{9,... | collective-permute-start | bytes 196616 | tf_op jit(solution)/shard_map/ppermute | solution.py:469
  28.6 4.8 %collective-permute-start.5 = (bf16[4,32,256]{2,1,0:T(8,128)(2,1)S(1)}, bf16[4,32,256]{2,1,0:T(8,128)(2,1)S(1)}, u32[]{:S(2)}, u32[]{:S(2)}) collective-permute-start(bf16[4,32,256]{2,1,0:T(8,128)(2,1)S(1)} %get-tuple-element.41), channel_id=1, source_target_pairs={{0,8},{1,9},{2,10},{3,11},{4,12},{5,13},{6,14},{7,15},{8,0},{9,1},... | collective-permute-start | bytes 196616 | tf_op jit(solution)/shard_map/ppermute | solution.py:469
  33.4 3.8 %collective-permute-start.7 = (bf16[32,256]{1,0:T(8,128)(2,1)S(1)}, bf16[32,256]{1,0:T(8,128)(2,1)S(1)}, u32[]{:S(2)}, u32[]{:S(2)}) collective-permute-start(bf16[32,256]{1,0:T(8,128)(2,1)S(1)} %get-tuple-element.42), channel_id=1, source_target_pairs={{0,2},{1,3},{2,0},{3,1},{4,6},{5,7},{6,4},{7,5},{8,10},{9,11},{10,... | collective-permute-start | bytes 49160 | tf_op jit(solution)/shard_map/ppermute | solution.py:469
  33.5 5.7 %collective-permute-start.9 = (bf16[32,256]{1,0:T(8,128)(2,1)S(1)}, bf16[32,256]{1,0:T(8,128)(2,1)S(1)}, u32[]{:S(2)}, u32[]{:S(2)}) collective-permute-start(bf16[32,256]{1,0:T(8,128)(2,1)S(1)} %get-tuple-element.43), channel_id=1, source_target_pairs={{0,6},{1,7},{2,4},{3,5},{4,2},{5,3},{6,0},{7,1},{8,14},{9,15},{10,... | collective-permute-start | bytes 49160 | tf_op jit(solution)/shard_map/ppermute | solution.py:469
  34.3 4.8 %collective-permute-start.8 = (bf16[32,256]{1,0:T(8,128)(2,1)S(1)}, bf16[32,256]{1,0:T(8,128)(2,1)S(1)}, u32[]{:S(2)}, u32[]{:S(2)}) collective-permute-start(bf16[32,256]{1,0:T(8,128)(2,1)S(1)} %get-tuple-element.44), channel_id=1, source_target_pairs={{0,4},{1,5},{2,6},{3,7},{4,0},{5,1},{6,2},{7,3},{8,12},{9,13},{10,... | collective-permute-start | bytes 49160 | tf_op jit(solution)/shard_map/ppermute | solution.py:469
